TPU v7x, 32 devices: a whole 2x2x4 slice. The times are simulated.
32 devices in a mesh: sec: 4 (over z), gx: 2 (over y), gy: 4 (over x, core).
Axes of the slice: x: 2, y: 2, z: 4, core: 2. Of those that a mesh axis runs over, the one named last changes fastest.
Arguments:
- fields: float32 [4, 3, 256, 8192], P('sec', None, 'gx', 'gy'), may hold values from -6 to 6
- x_ops: float32 [4, 3, 256, 256], P(None, None, 'gx'), may hold values from -4 to 4, as said below
- y_ops: float32 [4, 3, 256, 256], P(None, None, 'gy'), may hold values from -4 to 4, as said below
- x_line_class: int32 [256], P('gy'), may hold values from 0 to 3
- y_line_class: int32 [256], P('gx'), may hold values from 0 to 3
- box_offset: int32 [3, 2], replicated, may hold values from 0 to 127, as said below
- coupling: float32 [3, 3, 3], replicated, may hold values from -3 to 3
Outputs:
- fields_next: float32 [4, 3, 256, 8192], P('sec', None, 'gx', 'gy')
Inputs may be any that keep to these rules, and one draw needn't show every extreme that they name: `box_offset`: column 0 is below 128 and column 1 below 64; each column reaches its largest value for some box. `x_ops`: A dense matrix for each class and characteristic. `y_ops`: A dense matrix for each class and characteristic.
All inputs are finite; a program needn't handle non-finite values.
Results may differ from a plain program's by a relative error of at most 0.00013.
Values sent between devices are 32-bit elements; how exact they have to be, the bound alone decides.
No kernel may reach another device: no remote copies, remote signals or barrier semaphores. Data moves between devices by JAX's collectives and lax.ppermute only.
A program may use at most 192 MiB of HBM per device.

v0:
```python
import jax
import jax.numpy as jnp
from jax import lax
from jax.sharding import PartitionSpec as P

CZ = 32
NCLASS = 4
STEPS = 2


time_step = 0.2
viscosity = 0.25
highest = lax.Precision.HIGHEST


def from_root(shard, axis, root):
    mine = lax.axis_index(axis) == root
    return lax.psum(jnp.where(mine, shard, jnp.zeros_like(shard)), axis)


def padded_2(block, sides, width):
    for axis, dim in sides:
        count = lax.axis_size(axis)
        forward = [(i, i + 1) for i in range(count - 1)]
        backward = [(target, source) for source, target in forward]
        low = lax.ppermute(
            lax.slice_in_dim(block, block.shape[dim] - width, None, axis=dim), axis, forward
        )
        high = lax.ppermute(lax.slice_in_dim(block, 0, width, axis=dim), axis, backward)
        block = jnp.concatenate([low, block, high], axis=dim)
    return block


def shifted(value, axis, steps):
    count = lax.axis_size(axis)
    initial, last = (max(0, -steps), min(count, count - steps))
    return lax.ppermute(value, axis, [(source, source + steps) for source in range(initial, last)])


def flow_core(padded):
    centre = padded[:, 1:-1, 1:-1, :]
    ahead_x = padded[:, 2:, 1:-1, :]
    behind_x = padded[:, :-2, 1:-1, :]
    ahead_y = padded[:, 1:-1, 2:, :]
    behind_y = padded[:, 1:-1, :-2, :]
    ahead_z = jnp.roll(centre, -1, axis=3)
    behind_z = jnp.roll(centre, 1, axis=3)
    slope_x = 0.5 * (ahead_x - behind_x)
    slope_y = 0.5 * (ahead_y - behind_y)
    slope_z = 0.5 * (ahead_z - behind_z)
    laplace = ahead_x + behind_x + ahead_y + behind_y + ahead_z + behind_z - 6.0 * centre
    omega_x = slope_y[2] - slope_z[1]
    omega_y = slope_z[0] - slope_x[2]
    omega_z = slope_x[1] - slope_y[0]
    lamb_vector = jnp.stack(
        [
            omega_y * centre[2] - omega_z * centre[1],
            omega_z * centre[0] - omega_x * centre[2],
            omega_x * centre[1] - omega_y * centre[0],
        ]
    )
    updated = centre + time_step * (viscosity * laplace - lamb_vector)
    return (updated, lamb_vector)


def skip_flow(padded):
    centre = padded[:, 1:-1, 1:-1, :]
    return (centre, jnp.zeros_like(centre))


def unchanged(accrued):
    return accrued


def place_source(padded_lamb, offset_x, offset_y, matrix, span_x, span_y, extent_x, extent_y):
    anchor = jnp.zeros((), jnp.int32)
    corner_x = span_x - offset_x - 1
    corner_y = span_y - offset_y - 1
    window = lax.dynamic_slice(
        padded_lamb,
        (anchor, corner_x, corner_y, anchor),
        (3, extent_x + 1, extent_y + 1, padded_lamb.shape[3]),
    )
    averaged = 0.25 * (
        window[:, :-1, :-1] + window[:, 1:, :-1] + window[:, :-1, 1:] + window[:, 1:, 1:]
    )
    return jnp.einsum("kj,jxyz->kxyz", matrix, averaged, precision=highest)


def sweep_lines_x(state, x_ops, select_x, active):
    initial = jnp.zeros(state.shape[1:], jnp.float32)

    def add_piece(running, portion, anchor):

        def work(accrued):
            partial_value = jnp.einsum("ckij,kjl->ckil", x_ops, portion[0], precision=highest)
            return jnp.sum(partial_value * select_x[:, None, None, :], axis=0)

        return lax.cond(active, work, unchanged, running)

    return add_piece(initial, lax.all_gather(state, "gx", axis=2, tiled=True), jnp.int32(0))


def sweep_lines_y(state, y_ops, select_y, active):
    initial = jnp.zeros(state.shape[1:], jnp.float32)

    def add_piece(running, portion, anchor):

        def work(accrued):
            partial_value = jnp.einsum("ckij,kxjz->ckxiz", y_ops, portion[0], precision=highest)
            return jnp.sum(partial_value * select_y[:, None, :, None, None], axis=0)

        return lax.cond(active, work, unchanged, running)

    return add_piece(initial, lax.all_gather(state, "gy", axis=3, tiled=True), jnp.int32(0))


def local(fields, x_ops, y_ops, x_line_class, y_line_class, box_offset, coupling):
    sections = lax.axis_size("sec")
    section_index = lax.axis_index("sec")
    active = section_index == sections - 1
    member = jnp.minimum(section_index, sections - 2)
    span_x = fields.shape[2]
    merged = fields.shape[3]
    span_y = merged // CZ
    classes = jnp.arange(NCLASS, dtype=jnp.int32)
    select_y = (classes[:, None] == y_line_class[None, :]).astype(jnp.float32)
    offsets = lax.dynamic_index_in_dim(box_offset, member, 0, keepdims=False)
    matrix = lax.dynamic_index_in_dim(coupling, member, 0, keepdims=False)
    current = fields[0].reshape(3, span_x, span_y, CZ)
    share = CZ // sections
    whole_start = from_root(current, "sec", sections - 1)
    acoustic = lax.dynamic_slice_in_dim(whole_start, section_index * share, share, 3)
    for repeat in range(STEPS):
        padded = padded_2(current, (("gx", 1), ("gy", 2)), 1)
        flowed, lamb_vector = lax.cond(active, skip_flow, flow_core, padded)
        left_tile = shifted(lamb_vector, "gx", 1)
        joined = jnp.concatenate([left_tile, lamb_vector], axis=1)
        lower_tile = shifted(joined, "gy", 1)
        joined = jnp.concatenate([lower_tile, joined], axis=2)
        contribution = place_source(
            joined, offsets[0], offsets[1], matrix, span_x, span_y, span_x, span_y
        )
        source = lax.psum_scatter(contribution, "sec", scatter_dimension=3, tiled=True)
        amplitudes_grid = acoustic + time_step * source
        busy = jnp.asarray(True)
        planes = amplitudes_grid.shape[3]
        merged_now = span_y * planes
        select_x = jnp.broadcast_to(
            (classes[:, None, None] == x_line_class[None, :, None]).astype(jnp.float32),
            (NCLASS, span_y, planes),
        ).reshape(NCLASS, merged_now)
        amplitudes = amplitudes_grid.reshape(1, 3, span_x, merged_now)
        swept_x = sweep_lines_x(amplitudes, x_ops, select_x, busy)
        acoustic = sweep_lines_y(
            swept_x.reshape(1, 3, span_x, span_y, planes), y_ops, select_y, busy
        )
        current = flowed
    whole_end = lax.all_gather(acoustic, "sec", axis=3, tiled=True)
    current = jnp.where(active, whole_end, current)
    return current.reshape(1, 3, span_x, merged)


def solution(mesh):
    placed = (
        P("sec", None, "gx", "gy"),
        P(None, None, "gx", None),
        P(None, None, "gy", None),
        P("gy"),
        P("gx"),
        P(),
        P(),
    )
    return jax.shard_map(
        local, mesh=mesh, in_specs=placed, out_specs=P("sec", None, "gx", "gy"), check_vma=False
    )
```

profile of v0, /device:TPU:0, one launch (start us, length us, event | category | flops | bytes accessed | tf_op | source)
XLA Modules:
  0.0 765.4 jit_solution(2647574309795278677)
XLA Ops:
  10.2 6.5 fusion.37
  19.3 4.9 collective-permute-start
  35.3 6.2 pad_maximum_fusion.8
  50.5 7.3 pad_maximum_fusion.6
  57.8 36.1 %conditional.2 = ((f32[3,128,64,32]{1,3,2,0:T(8,128)}, f32[3,128,64,32]{1,3,2,0:T(8,128)})) conditional(s32[]{:T(128)} %convert_element_type.20, (f32[3,130,64,32]{1,3,2,0:T(8,128)}, f32[3,130,66,32]{1,3,2,0:T(8,128)}, f32[3,128,64,32]{1,3,2,0:T(8,128)S(1)}) %tuple.76, f32[3,128,64,32]{1,3,2,0:T(8,128)S(1)} %bitcast.80), branch_computations={%region_1.2_spmd, %region_2.3_spmd} | conditional | flops 21233664 | bytes 158859424 | solution.py:136
  63.1 12.4 %subtract_multiply_fusion = (f32[3,128,64,32]{1,3,2,0:T(8,128)}, f32[3,128,64,32]{1,3,2,0:T(8,128)}) fusion(f32[3,130,66,32]{1,3,2,0:T(8,128)} %get-tuple-element.21, f32[3,130,64,32]{1,3,2,0:T(8,128)} %get-tuple-element.20), kind=kLoop, calls=%fused_computation.4 | loop fusion | flops 3145728 | bytes 18874368 | tf_op jit(solution)/shard_map/cond/branch_0_fun/mul | solution.py:49
  75.6 5.1 multiply_subtract_fusion.2
  82.1 11.8 %multiply_add_fusion = (f32[3,128,64,32]{1,3,2,0:T(8,128)}, f32[3,128,64,32]{1,3,2,0:T(8,128)}) fusion(f32[3,128,64,32]{1,3,2,0:T(8,128)S(1)} %copy-done.4, f32[3,130,66,32]{1,3,2,0:T(8,128)} %get-tuple-element.21, f32[3,130,64,32]{1,3,2,0:T(8,128)} %get-tuple-element.20, f32[3,128,64,31]{1,3,2,0:T(8,128)S(1)} %copy-done.16, ...), kind=kLoop, calls=%fused_computation.3 | loop fusion | flops 11796480 | bytes 31457280 | tf_op jit(solution)/shard_map/cond/branch_0_fun/add | solution.py:62
  93.9 7.6 copy.193
  106.0 6.7 collective-permute-start.4
  117.7 6.2 pad_maximum_fusion.9
  126.6 4.3 collective-permute-start.8
  132.2 9.4 %copy.198 = f32[3,130,64,32]{2,3,1,0:T(8,128)} copy(f32[3,130,64,32]{1,3,2,0:T(8,128)} %copy-done.8) | data formatting | bytes 6389760 | tf_op jit(solution)/shard_map/concatenate | solution.py:30
  141.7 8.1 %copy.197 = f32[3,130,1,32]{2,3,1,0:T(8,128)} copy(f32[3,130,1,32]{1,3,2,0:T(8,128)S(1)} %collective-permute-done.8) | data formatting | bytes 99840 | tf_op jit(solution)/shard_map/ppermute | solution.py:26
  149.8 8.1 %copy.199 = f32[3,130,1,32]{2,3,1,0:T(8,128)} copy(f32[3,130,1,32]{1,3,2,0:T(8,128)S(1)} %collective-permute-done.9) | data formatting | bytes 99840 | tf_op jit(solution)/shard_map/ppermute | solution.py:29
  157.9 10.1 %pad_maximum_fusion.7 = f32[3,130,66,32]{2,3,1,0:T(8,128)} fusion(f32[3,130,1,32]{2,3,1,0:T(8,128)} %copy.199, f32[3,130,64,32]{2,3,1,0:T(8,128)} %copy.198, f32[3,130,1,32]{2,3,1,0:T(8,128)} %copy.197), kind=kLoop, calls=%fused_computation.31 | loop fusion | flops 1647360 | bytes 6589440 | tf_op jit(solution)/shard_map/concatenate | solution.py:30
  167.9 49.0 %conditional.3 = (f32[3,128,64,32]{1,3,2,0:T(8,128)S(1)}, f32[3,128,64,32]{1,2,3,0:T(8,128)S(1)}) conditional(s32[]{:T(128)} %convert_element_type.20, (f32[3,130,64,32]{1,3,2,0:T(8,128)}, f32[3,130,66,32]{2,3,1,0:T(8,128)}, f32[3,128,64,32]{1,3,2,0:T(8,128)S(1)}) %tuple.75, f32[3,128,64,32]{1,3,2,0:T(8,128)S(1)} %copy-done.5), branch_computations={%region_6.7_spmd, %region_7.8_spmd} | conditional | flops 21233664 | bytes 160539792 | solution.py:136
  173.2 10.0 %copy.200 = f32[3,130,66,32]{1,3,2,0:T(8,128)} copy(f32[3,130,66,32]{2,3,1,0:T(8,128)} %get-tuple-element.55) | data formatting | bytes 6589440 | tf_op jit(solution)/shard_map
  183.2 12.5 %subtract_multiply_fusion.3 = (f32[3,128,64,32]{1,3,2,0:T(8,128)}, f32[3,128,64,32]{1,3,2,0:T(8,128)}) fusion(f32[3,130,66,32]{1,3,2,0:T(8,128)} %copy.200, f32[3,130,64,32]{1,3,2,0:T(8,128)} %get-tuple-element.23), kind=kLoop, calls=%fused_computation.17 | loop fusion | flops 3145728 | bytes 18874368 | tf_op jit(solution)/shard_map/cond/branch_0_fun/mul | solution.py:49
  195.7 6.7 multiply_subtract_fusion.5
  203.4 9.6 %multiply_add_fusion.1 = (f32[3,128,64,32]{1,3,2,0:T(8,128)}, f32[3,128,64,32]{1,3,2,0:T(8,128)S(1)}) fusion(f32[3,128,64,32]{1,3,2,0:T(8,128)S(1)} %copy-done.7, f32[3,130,66,32]{1,3,2,0:T(8,128)S(1)} %copy-done.10, f32[3,130,64,32]{1,3,2,0:T(8,128)} %get-tuple-element.23, f32[3,128,64,31]{1,3,2,0:T(8,128)} %copy-done.12, ...), kind=kLoop, calls=%fused_computation.16 | loop fusion | flops 11796480 | bytes 31457280 | tf_op jit(solution)/shard_map/cond/branch_0_fun/add | solution.py:62
  213.0 3.7 copy.225
  218.7 4.2 constant_dynamic-update-slice_fusion.1
  224.9 5.9 collective-permute-start.5
  230.8 55.5 %collective-permute-done.10 = f32[3,128,64,32]{1,3,2,0:T(8,128)S(1)} collective-permute-done((f32[3,128,64,32]{1,3,2,0:T(8,128)S(1)}, f32[3,128,64,32]{1,3,2,0:T(8,128)S(1)}, u32[]{:S(2)}, u32[]{:S(2)}) %collective-permute-start.10) | collective-permute-done | bytes 3145760 | tf_op jit(solution)/shard_map/ppermute | solution.py:37
  290.3 5.4 collective-permute-start.11
  303.4 12.8 %copy.184 = f32[3,256,64,32]{2,3,1,0:T(8,128)} copy(f32[3,256,64,32]{1,3,2,0:T(8,128)} %constant_dynamic-update-slice_fusion) | data formatting | bytes 12582912 | tf_op jit(solution)/shard_map/concatenate | solution.py:138
  316.2 12.8 %copy.202 = f32[3,256,64,32]{2,3,1,0:T(8,128)} copy(f32[3,256,64,32]{1,3,2,0:T(8,128)} %constant_dynamic-update-slice_fusion.2) | data formatting | bytes 12582912 | tf_op jit(solution)/shard_map/concatenate | solution.py:138
  329.0 12.8 %copy.183 = f32[3,256,64,32]{2,3,1,0:T(8,128)} copy(f32[3,256,64,32]{1,3,2,0:T(8,128)} %collective-permute-done.5) | data formatting | bytes 12582912 | tf_op jit(solution)/shard_map/ppermute | solution.py:37
  341.7 12.7 %copy.201 = f32[3,256,64,32]{2,3,1,0:T(8,128)} copy(f32[3,256,64,32]{1,3,2,0:T(8,128)} %collective-permute-done.11) | data formatting | bytes 12582912 | tf_op jit(solution)/shard_map/ppermute | solution.py:37
  354.4 13.6 %fusion = (f32[3,129,65,32]{2,3,1,0:T(8,128)}, f32[3,129,65,32]{2,3,1,0:T(8,128)S(1)}) fusion(s32[]{:T(128)S(6)} %select_n.33, s32[]{:T(128)S(6)} %select_n.34, f32[3,256,64,32]{2,3,1,0:T(8,128)} %copy.201, f32[3,256,64,32]{2,3,1,0:T(8,128)} %copy.202, f32[3,256,64,32]{2,3,1,0:T(8,128)} %copy.184, f32[3,256,64,32]{2,3,1,0:T(8,128)} %copy.183), kind=kLoop, calls=%fused_computation.32 | loop fusion | flops 1609920 | bytes 31605512 | tf_op jit(solution)/shard_map/concatenate | solution.py:140
  368.1 5.0 fusion.3
  373.1 7.0 copy.185
  380.2 9.7 %fusion.26 = f32[3,128,64,32]{1,0,3,2:T(4,128)S(1)} fusion(f32[3,128,64,32]{1,0,3,2:T(4,128)} %copy.185, f32[3,3,3]{2,1,0:T(4,128)S(1)} %copy-done.20, s32[]{:T(128)S(6)} %select_n.32), kind=kOutput, calls=%fused_computation.76 | convolution fusion | flops 28311552 | bytes 6293508 | tf_op jit(solution)/shard_map/kj,jxyz->kxyz/dot_general | solution.py:87
  393.4 27.2 %all-reduce.2.cloned.1.call-done = f32[3,128,64,32]{1,2,3,0:T(8,128)} async-done(((f32[3,128,64,32]{1,2,3,0:T(8,128)}), f32[3,128,64,32]{1,2,3,0:T(8,128)}) %all-reduce.2.cloned.1.call-update) | async-done | bytes 3145744 | tf_op jit(solution)/shard_map/psum | solution.py:18
  420.7 61.6 %reduce-scatter.3.cloned.1.call-done = f32[3,128,64,8]{1,2,0,3:T(8,128)} async-done(((f32[3,128,64,32]{1,2,0,3:T(8,128)}), f32[3,128,64,8]{1,2,0,3:T(8,128)}) %reduce-scatter.3.cloned.1.call-update) | async-done | bytes 786448 | tf_op jit(solution)/shard_map/reduce_scatter | solution.py:144
  485.4 27.1 %all-gather.6.cloned.1.call-done = f32[1,3,256,512]{2,3,1,0:T(8,128)} async-done(((f32[1,3,128,512]{2,3,1,0:T(8,128)}), f32[1,3,256,512]{2,3,1,0:T(8,128)}) %all-gather.6.cloned.1.call-update) | async-done | bytes 1572880 | tf_op jit(solution)/shard_map/all_gather | solution.py:101
  512.5 4.3 fusion.11
  517.9 13.6 %fusion.2 = f32[3,128,64,32]{2,3,1,0:T(8,128)} fusion(f32[3,129,65,32]{2,3,1,0:T(8,128)} %get-tuple-element.90), kind=kLoop, calls=%fused_computation.35 | loop fusion | flops 3145728 | bytes 15728640 | tf_op jit(solution)/shard_map/mul | solution.py:84
  531.4 7.0 copy.203
  538.4 9.2 %fusion.24 = f32[3,128,64,32]{1,0,3,2:T(4,128)S(1)} fusion(f32[3,128,64,32]{1,0,3,2:T(4,128)} %copy.203, f32[3,3,3]{2,1,0:T(4,128)S(1)} %copy-done.20, s32[]{:T(128)S(6)} %select_n.32), kind=kOutput, calls=%fused_computation.74 | convolution fusion | flops 28311552 | bytes 6293508 | tf_op jit(solution)/shard_map/kj,jxyz->kxyz/dot_general | solution.py:87
  555.4 4.6 fusion.10
  560.0 51.6 %reduce-scatter.5.cloned.1.call-done = f32[3,128,64,8]{1,2,0,3:T(8,128)} async-done(((f32[3,128,64,32]{1,2,0,3:T(8,128)}), f32[3,128,64,8]{1,2,0,3:T(8,128)}) %reduce-scatter.5.cloned.1.call-update) | async-done | bytes 786448 | tf_op jit(solution)/shard_map/reduce_scatter | solution.py:144
  614.3 27.3 %all-gather.10.cloned.1.call-done = f32[1,3,256,512]{2,3,1,0:T(8,128)} async-done(((f32[1,3,128,512]{2,3,1,0:T(8,128)}), f32[1,3,256,512]{2,3,1,0:T(8,128)}) %all-gather.10.cloned.1.call-update) | async-done | bytes 1572880 | tf_op jit(solution)/shard_map/all_gather | solution.py:101
  641.6 4.5 fusion.9
  647.2 28.6 %all-gather.12.cloned.1.call-done = f32[1,3,128,256,8]{2,4,1,0,3:T(8,128)} async-done(((f32[1,3,128,64,8]{2,4,1,0,3:T(8,128)}), f32[1,3,128,256,8]{2,4,1,0,3:T(8,128)}) %all-gather.12.cloned.1.call-update) | async-done | bytes 3145744 | tf_op jit(solution)/shard_map/all_gather | solution.py:115
  679.4 5.5 fusion.8
  684.9 63.6 %all-gather.14.cloned.1.call-done = f32[3,128,64,32]{1,2,3,0:T(8,128)} async-done(((f32[3,128,64,8]{1,2,3,0:T(8,128)}), f32[3,128,64,32]{1,2,3,0:T(8,128)}) %all-gather.14.cloned.1.call-update) | async-done | bytes 3145744 | tf_op jit(solution)/shard_map/all_gather | solution.py:159
  (122 shorter events, 97.4 us)
Async XLA Ops:
  6.5 506.0 %copy-start = (f32[4,3,128,256]{3,2,1,0:T(8,128)S(1)}, f32[4,3,128,256]{3,2,1,0:T(8,128)}, u32[]{:S(2)}) copy-start(f32[4,3,128,256]{3,2,1,0:T(8,128)} %param.12) | copy-start | bytes 4718596
  6.5 414.1 %all-reduce.2.cloned.1.call-start = ((), (), s32[]{:S(2)}) async-start(), calls=%async_computation.2 | async-start | bytes 6291456 | tf_op jit(solution)/shard_map/psum | solution.py:18
  19.3 8.8 %collective-permute-start = (f32[3,1,64,32]{2,3,1,0:T(8,128)S(1)}, f32[3,1,64,32]{2,3,1,0:T(8,128)S(1)}, u32[]{:S(2)}, u32[]{:S(2)}) collective-permute-start(f32[3,1,64,32]{2,3,1,0:T(8,128)S(1)} %copy.179), channel_id=1, source_target_pairs={{0,4},{1,5},{2,6},{3,7},{8,12},{9,13},{10,14},{11,15},{16,20},{17,... | collective-permute-start | bytes 73736 | tf_op jit(solution)/shard_map/ppermute | solution.py:26
  26.9 6.0 collective-permute-start.1
  41.6 2.7 copy-start.9
  44.3 2.6 collective-permute-start.2
  45.6 4.9 collective-permute-start.3
  50.5 7.3 copy-start.1
  58.1 2.3 copy-start.3
  59.2 3.9 copy-start.13
  59.2 3.9 copy-start.15
  75.6 5.1 copy-start.4
  75.6 5.6 copy-start.14
  75.6 6.5 copy-start.16
  102.3 10.4 %collective-permute-start.6 = (f32[3,1,64,32]{2,3,1,0:T(8,128)S(1)}, f32[3,1,64,32]{2,3,1,0:T(8,128)S(1)}, u32[]{:S(2)}, u32[]{:S(2)}) collective-permute-start(f32[3,1,64,32]{2,3,1,0:T(8,128)S(1)} %get-tuple-element.82), channel_id=1, source_target_pairs={{0,4},{1,5},{2,6},{3,7},{8,12},{9,13},{10,14},{11,15},{16,20},{17,... | collective-permute-start | bytes 73736 | tf_op jit(solution)/shard_map/ppermute | solution.py:26
  104.7 10.5 %collective-permute-start.7 = (f32[3,1,64,32]{2,3,1,0:T(8,128)S(1)}, f32[3,1,64,32]{2,3,1,0:T(8,128)S(1)}, u32[]{:S(2)}, u32[]{:S(2)}) collective-permute-start(f32[3,1,64,32]{2,3,1,0:T(8,128)S(1)} %get-tuple-element.83), channel_id=1, source_target_pairs={{4,0},{5,1},{6,2},{7,3},{12,8},{13,9},{14,10},{15,11},{20,16},{21,... | collective-permute-start | bytes 73736 | tf_op jit(solution)/shard_map/ppermute | solution.py:29
  106.0 112.7 %collective-permute-start.4 = (f32[3,128,64,32]{1,3,2,0:T(8,128)}, f32[3,128,64,32]{1,3,2,0:T(8,128)}, u32[]{:S(2)}, u32[]{:S(2)}) collective-permute-start(f32[3,128,64,32]{1,3,2,0:T(8,128)} %get-tuple-element.29), channel_id=1, source_target_pairs={{0,4},{1,5},{2,6},{3,7},{8,12},{9,13},{10,14},{11,15},{16,20},{17,... | collective-permute-start | bytes 9437192 | tf_op jit(solution)/shard_map/ppermute | solution.py:37
  124.0 2.7 copy-start.8
  126.6 15.0 %collective-permute-start.8 = (f32[3,130,1,32]{1,3,2,0:T(8,128)S(1)}, f32[3,130,1,32]{1,3,2,0:T(8,128)S(1)}, u32[]{:S(2)}, u32[]{:S(2)}) collective-permute-start(f32[3,130,1,32]{1,3,2,0:T(8,128)S(1)} %get-tuple-element.80), channel_id=1, source_target_pairs={{0,1},{1,2},{2,3},{4,5},{5,6},{6,7},{8,9},{9,10},{10,11},{12,13},{... | collective-permute-start | bytes 149768 | tf_op jit(solution)/shard_map/ppermute | solution.py:26
  130.9 18.9 %collective-permute-start.9 = (f32[3,130,1,32]{1,3,2,0:T(8,128)S(1)}, f32[3,130,1,32]{1,3,2,0:T(8,128)S(1)}, u32[]{:S(2)}, u32[]{:S(2)}) collective-permute-start(f32[3,130,1,32]{1,3,2,0:T(8,128)S(1)} %get-tuple-element.81), channel_id=1, source_target_pairs={{1,0},{2,1},{3,2},{5,4},{6,5},{7,6},{9,8},{10,9},{11,10},{13,12},{... | collective-permute-start | bytes 149768 | tf_op jit(solution)/shard_map/ppermute | solution.py:29
  157.9 10.1 %copy-start.5 = (f32[3,128,64,32]{1,3,2,0:T(8,128)S(1)}, f32[3,128,64,32]{1,3,2,0:T(8,128)}, u32[]{:S(2)}) copy-start(f32[3,128,64,32]{1,3,2,0:T(8,128)} %get-tuple-element.30) | copy-start | bytes 9437188
  168.1 2.3 copy-start.6
  169.2 3.9 copy-start.11
  169.2 3.9 copy-start.12
  195.7 6.7 copy-start.7
  195.7 7.7 %copy-start.10 = (f32[3,130,66,32]{1,3,2,0:T(8,128)S(1)}, f32[3,130,66,32]{1,3,2,0:T(8,128)}, u32[]{:S(2)}) copy-start(f32[3,130,66,32]{1,3,2,0:T(8,128)} %copy.200) | copy-start | bytes 9884164 | tf_op jit(solution)/shard_map/cond
  216.9 6.0 copy-start.17
  216.9 5.9 copy-start.18
  216.9 69.4 %collective-permute-start.10 = (f32[3,128,64,32]{1,3,2,0:T(8,128)S(1)}, f32[3,128,64,32]{1,3,2,0:T(8,128)S(1)}, u32[]{:S(2)}, u32[]{:S(2)}) collective-permute-start(f32[3,128,64,32]{1,3,2,0:T(8,128)S(1)} %get-tuple-element.31), channel_id=1, source_target_pairs={{0,4},{1,5},{2,6},{3,7},{8,12},{9,13},{10,14},{11,15},{16,20},{17,... | collective-permute-start | bytes 9437192 | tf_op jit(solution)/shard_map/ppermute | solution.py:37
  224.9 104.1 %collective-permute-start.5 = (f32[3,256,64,32]{1,3,2,0:T(8,128)}, f32[3,256,64,32]{1,3,2,0:T(8,128)}, u32[]{:S(2)}, u32[]{:S(2)}) collective-permute-start(f32[3,256,64,32]{1,3,2,0:T(8,128)} %constant_dynamic-update-slice_fusion), channel_id=1, source_target_pairs={{0,1},{1,2},{2,3},{4,5},{5,6},{6,7},{8,9},{9,10},{10,11},{12,13},{... | collective-permute-start | bytes 18874376 | tf_op jit(solution)/shard_map/ppermute | solution.py:37
  288.3 7.4 copy-start.2
  290.3 51.4 %collective-permute-start.11 = (f32[3,256,64,32]{1,3,2,0:T(8,128)}, f32[3,256,64,32]{1,3,2,0:T(8,128)}, u32[]{:S(2)}, u32[]{:S(2)}) collective-permute-start(f32[3,256,64,32]{1,3,2,0:T(8,128)} %constant_dynamic-update-slice_fusion.2), channel_id=1, source_target_pairs={{0,1},{1,2},{2,3},{4,5},{5,6},{6,7},{8,9},{9,10},{10,11},{12,13},{... | collective-permute-start | bytes 18874376 | tf_op jit(solution)/shard_map/ppermute | solution.py:37
  299.4 0.7 copy-start.21
  299.5 182.8 %reduce-scatter.3.cloned.1.call-start = ((), (), s32[]{:S(2)}) async-start(), calls=%async_computation.3 | async-start | bytes 3932160 | tf_op jit(solution)/shard_map/reduce_scatter | solution.py:144
  373.1 7.0 copy-start.20
  393.4 91.8 %copy-start.22 = (s32[64]{0:T(128)S(1)}, s32[64]{0:T(128)}, u32[]{:S(2)}) copy-start(s32[64]{0:T(128)} %param.14) | copy-start | bytes 772
  393.4 119.1 %all-gather.6.cloned.1.call-start = ((), (), s32[]{:S(2)}) async-start(), calls=%async_computation.4 | async-start | bytes 2359296 | tf_op jit(solution)/shard_map/all_gather | solution.py:101
  485.2 66.6 %all-gather.8.cloned.1.call-start = ((), (), s32[]{:S(2)}) async-start(), calls=%async_computation.5 | async-start | bytes 3932160 | tf_op jit(solution)/shard_map/all_gather | solution.py:115
  517.8 93.9 %reduce-scatter.5.cloned.1.call-start = ((), (), s32[]{:S(2)}) async-start(), calls=%async_computation.6 | async-start | bytes 3932160 | tf_op jit(solution)/shard_map/reduce_scatter | solution.py:144
  551.1 0.7 copy-start.23
  551.1 90.5 %all-gather.10.cloned.1.call-start = ((), (), s32[]{:S(2)}) async-start(), calls=%async_computation.7 | async-start | bytes 2359296 | tf_op jit(solution)/shard_map/all_gather | solution.py:101
  551.8 3.6 copy-start.19
  614.3 61.6 %all-gather.12.cloned.1.call-start = ((), (), s32[]{:S(2)}) async-start(), calls=%async_computation.8 | async-start | bytes 3932160 | tf_op jit(solution)/shard_map/all_gather | solution.py:115
  647.2 101.4 %all-gather.14.cloned.1.call-start = ((), (), s32[]{:S(2)}) async-start(), calls=%async_computation.9 | async-start | bytes 3932160 | tf_op jit(solution)/shard_map/all_gather | solution.py:159
Sparse Core Ops, SparseCore 0:
  299.6 121.0 all-reduce.1
  423.0 59.2 reduce-scatter.2
  485.3 27.1 all-gather.5
  517.9 28.5 all-gather.7
  551.3 60.3 reduce-scatter.4
  614.4 27.2 all-gather.9
  647.3 28.5 all-gather.11
  685.0 63.4 all-gather.13
where the time goes:
time: 773 us; the launch traced here: 765 us
  waiting for transfers between devices  349 us (45%)
  local copies, waits for them, and re-layouts  189 us (24%)
  other arithmetic  135 us (17%)
  starting transfers between devices  38.3 us (5%)
  matrix products  37.9 us (5%)
  between operations  16.7 us (2%)
    reduce_scatter x2, waiting for transfers between devices, local(): lax.psum_scatter(contribution, 'sec', scatter_dimension=3, tiled=True)  113 us
    all_gather x1, waiting for transfers between devices, local(): whole_end = lax.all_gather(acoustic, 'sec', axis=3, tiled=True)  63.6 us
    ppermute x4, waiting for transfers between devices, shifted(): lax.ppermute(value, axis, [(source, source + steps) for source in range(i...  55.5 us
    all_gather x2, waiting for transfers between devices, sweep_lines_x(): lax.all_gather(state, 'gx', axis=2, tiled=True)  54.4 us
    concatenate x4, other arithmetic, padded_2(): block = jnp.concatenate([low, block, high], axis=dim)  29.9 us
    concatenate x4, local copies, waits for them, and re-layouts, local(): joined = jnp.concatenate([left_tile, lamb_vector], axis=1)  29.6 us
    all_gather x2, waiting for transfers between devices, sweep_lines_y(): lax.all_gather(state, 'gy', axis=3, tiled=True)  28.6 us
    psum x1, waiting for transfers between devices, from_root(): return lax.psum(jnp.where(mine, shard, jnp.zeros_like(shard)), axis)  27.2 us
  transfers between devices with their start and end apart: 20, of which 10 were waited for; matrix products, arithmetic and copies ran while one was open for 32% of the time, Pallas kernels for 0%

commit v1 on v0

--- a/solution.py
+++ b/solution.py
@@ -1,15 +1,514 @@
 import jax
 import jax.numpy as jnp
 from jax import lax
+from jax.experimental import pallas as pl
+from jax.experimental.pallas import tpu as pltpu
 from jax.sharding import PartitionSpec as P
 
 CZ = 32
 NCLASS = 4
 STEPS = 2
-
+TILE_X = 128
+TILE_Y = 64
+CHUNKS = 2
 
 time_step = 0.2
 viscosity = 0.25
+vmem_limit = 56 * 1024 * 1024
+f32 = jnp.float32
+bf16 = jnp.bfloat16
+
+
+def params():
+    return pltpu.CompilerParams(vmem_limit_bytes=vmem_limit)
+
+
+def iota(shape, dim):
+    return lax.broadcasted_iota(jnp.int32, shape, dim)
+
+
+def planes_kernel(field_ref, planes_ref, west_ref, east_ref, south_ref, north_ref, turned):
+    comp = pl.program_id(0)
+    turned[...] = field_ref[0].T
+    lane = iota((TILE_Y, TILE_X), 1)
+
+    @pl.when(comp == 0)
+    def _():
+        west_ref[...] = jnp.zeros_like(west_ref)
+        east_ref[...] = jnp.zeros_like(east_ref)
+
+    west = west_ref[...]
+    east = east_ref[...]
+    for z in range(CZ):
+        plane = turned[pl.ds(z, TILE_Y, stride=CZ), :]
+        planes_ref[z, 0] = plane
+        here = lane == z * 3 + comp
+        west = jnp.where(here, plane[:, 0:1], west)
+        east = jnp.where(here, plane[:, TILE_X - 1 :], east)
+        south_ref[0, pl.ds(z, 1), :] = plane[0:1, :]
+        north_ref[0, pl.ds(z, 1), :] = plane[TILE_Y - 1 :, :]
+    west_ref[...] = west
+    east_ref[...] = east
+
+
+def to_planes(field):
+    whole = lambda c: (0, 0)
+    return pl.pallas_call(
+        planes_kernel,
+        grid=(3,),
+        in_specs=[pl.BlockSpec((1, TILE_X, TILE_Y * CZ), lambda c: (c, 0, 0))],
+        out_specs=[
+            pl.BlockSpec((CZ, 1, TILE_Y, TILE_X), lambda c: (0, c, 0, 0)),
+            pl.BlockSpec((TILE_Y, TILE_X), whole),
+            pl.BlockSpec((TILE_Y, TILE_X), whole),
+            pl.BlockSpec((1, CZ, TILE_X), lambda c: (c, 0, 0)),
+            pl.BlockSpec((1, CZ, TILE_X), lambda c: (c, 0, 0)),
+        ],
+        out_shape=[
+            jax.ShapeDtypeStruct((CZ, 3, TILE_Y, TILE_X), f32),
+            jax.ShapeDtypeStruct((TILE_Y, TILE_X), f32),
+            jax.ShapeDtypeStruct((TILE_Y, TILE_X), f32),
+            jax.ShapeDtypeStruct((3, CZ, TILE_X), f32),
+            jax.ShapeDtypeStruct((3, CZ, TILE_X), f32),
+        ],
+        scratch_shapes=[pltpu.VMEM((TILE_Y * CZ, TILE_X), f32)],
+        compiler_params=params(),
+        name="to_planes",
+    )(field)
+
+
+def flow_kernel(per, last, flag_ref, u_ref, xlo_ref, xhi_ref, ylo_ref, yhi_ref, *outs):
+    lamb_refs = outs[:CHUNKS]
+    next_ref = outs[CHUNKS]
+    group = pl.program_id(0)
+    acoustic = flag_ref[0] > 0
+    lane = iota((TILE_Y, TILE_X), 1)
+    row = iota((TILE_Y, TILE_X), 0)
+    turn = lax.rem(TILE_X - group * (per * 3), TILE_X)
+    xlo = pltpu.roll(xlo_ref[...], turn, 1)
+    xhi = pltpu.roll(xhi_ref[...], turn, 1)
+    if not last:
+        west_ref, east_ref, south_ref, north_ref = outs[CHUNKS + 1 :]
+
+        @pl.when(group == 0)
+        def _():
+            west_ref[...] = jnp.zeros_like(west_ref)
+            east_ref[...] = jnp.zeros_like(east_ref)
+
+        west = west_ref[...]
+        east = east_ref[...]
+    for i in range(per):
+        z = group * per + i
+        above = lax.rem(z + 1, CZ)
+        below = lax.rem(z + CZ - 1, CZ)
+        centre, lap, dx, dy, dz = [], [], [], [], []
+        for c in range(3):
+            mid = u_ref[z, c]
+            up = u_ref[above, c]
+            down = u_ref[below, c]
+            spot = i * 3 + c
+            xm = jnp.where(lane == 0, xlo[:, spot : spot + 1], pltpu.roll(mid, 1, 1))
+            xp = jnp.where(
+                lane == TILE_X - 1, xhi[:, spot : spot + 1], pltpu.roll(mid, TILE_X - 1, 1)
+            )
+            ym = jnp.where(row == 0, ylo_ref[c, pl.ds(z, 1), :], pltpu.roll(mid, 1, 0))
+            yp = jnp.where(
+                row == TILE_Y - 1, yhi_ref[c, pl.ds(z, 1), :], pltpu.roll(mid, TILE_Y - 1, 0)
+            )
+            centre.append(mid)
+            lap.append(xp + xm + yp + ym + up + down - 6.0 * mid)
+            dx.append(0.5 * (xp - xm))
+            dy.append(0.5 * (yp - ym))
+            dz.append(0.5 * (up - down))
+        ox = dy[2] - dz[1]
+        oy = dz[0] - dx[2]
+        oz = dx[1] - dy[0]
+        lamb = (
+            oy * centre[2] - oz * centre[1],
+            oz * centre[0] - ox * centre[2],
+            ox * centre[1] - oy * centre[0],
+        )
+        for c in range(3):
+            moved = centre[c] + time_step * (viscosity * lap[c] - lamb[c])
+            next_ref[i, c] = moved
+            sent = lamb[c] if last else jnp.where(acoustic, centre[c], lamb[c])
+            lamb_refs[i % CHUNKS][0, i // CHUNKS, c] = sent
+            if not last:
+                here = lane == z * 3 + c
+                west = jnp.where(here, moved[:, 0:1], west)
+                east = jnp.where(here, moved[:, TILE_X - 1 :], east)
+                south_ref[c, pl.ds(z, 1), :] = moved[0:1, :]
+                north_ref[c, pl.ds(z, 1), :] = moved[TILE_Y - 1 :, :]
+    if not last:
+        west_ref[...] = west
+        east_ref[...] = east
+
+
+def flow(flag, planes, halo, groups, last):
+    per = CZ // groups
+    halves = per // CHUNKS
+    edge = pl.BlockSpec((TILE_Y, TILE_X), lambda g: (0, 0))
+    side = pl.BlockSpec((3, CZ, TILE_X), lambda g: (0, 0, 0))
+    out_specs = [
+        pl.BlockSpec((1, halves, 3, TILE_Y, TILE_X), lambda g: (g, 0, 0, 0, 0))
+    ] * CHUNKS + [pl.BlockSpec((per, 3, TILE_Y, TILE_X), lambda g: (g, 0, 0, 0))]
+    out_shape = [
+        jax.ShapeDtypeStruct((groups, halves, 3, TILE_Y, TILE_X), f32)
+    ] * CHUNKS + [jax.ShapeDtypeStruct((CZ, 3, TILE_Y, TILE_X), f32)]
+    if not last:
+        out_specs += [edge, edge, side, side]
+        out_shape += [jax.ShapeDtypeStruct((TILE_Y, TILE_X), f32)] * 2
+        out_shape += [jax.ShapeDtypeStruct((3, CZ, TILE_X), f32)] * 2
+
+    def body(*refs):
+        flow_kernel(per, last, *refs)
+
+    return pl.pallas_call(
+        body,
+        grid=(groups,),
+        in_specs=[
+            pl.BlockSpec(memory_space=pltpu.SMEM),
+            pl.BlockSpec((CZ, 3, TILE_Y, TILE_X), lambda g: (0, 0, 0, 0)),
+            edge,
+            edge,
+            side,
+            side,
+        ],
+        out_specs=out_specs,
+        out_shape=out_shape,
+        compiler_params=params(),
+        name="flow",
+    )(flag, planes, *halo)
+
+
+def exchange(west, east, south, north):
+    def send(value, axis, step):
+        count = lax.axis_size(axis)
+        return lax.ppermute(
+            value, axis, [(i, i + step) for i in range(count) if 0 <= i + step < count]
+        )
+
+    return (
+        send(east, "gx", 1),
+        send(west, "gx", -1),
+        send(north, "gy", 1),
+        send(south, "gy", -1),
+    )
+
+
+def place_kernel(gx, gy, first, ints_ref, matrix_ref, got_ref, far_ref, near_ref, rows):
+    low = ints_ref[1]
+    ox = ints_ref[2]
+    oy = ints_ref[3]
+    full_y = gy * TILE_Y
+    lane = iota((full_y, TILE_X), 1)
+    row = iota((full_y, TILE_X), 0)
+
+    def tile(h, j, a):
+        return jnp.concatenate([got_ref[a * gy + b, h, j] for b in range(gy)], axis=0)
+
+    def work(h, out_ref):
+        for a in range(gx):
+            rows[0:TILE_Y, a * TILE_X : (a + 1) * TILE_X] = jnp.zeros((TILE_Y, TILE_X), f32)
+        vectors = [[tile(h, j, a) for a in range(gx)] for j in range(3)]
+        for k in range(3):
+            mixed = [
+                matrix_ref[k, 0] * vectors[0][a]
+                + matrix_ref[k, 1] * vectors[1][a]
+                + matrix_ref[k, 2] * vectors[2][a]
+                for a in range(gx)
+            ]
+            before = jnp.zeros((full_y, TILE_X), f32)
+            moved = []
+            for a in range(gx):
+                turned = pltpu.roll(mixed[a], ox, 1)
+                moved.append(jnp.where(lane >= ox, turned, before))
+                before = turned
+            before = jnp.zeros((full_y, TILE_X), f32)
+            for a in range(gx):
+                turned = pltpu.roll(moved[a], 1, 1)
+                pair = moved[a] + jnp.where(lane >= 1, turned, before)
+                before = turned
+                pair = pair + jnp.where(row >= 1, pltpu.roll(pair, 1, 0), 0.0)
+                rows[TILE_Y : TILE_Y + full_y, a * TILE_X : (a + 1) * TILE_X] = pair
+            start = TILE_Y - oy
+            rest = lax.rem(start, 8)
+            window = rows[pl.ds(pl.multiple_of(start - rest, 8), full_y + 8), :]
+            window = window.reshape(full_y // 8 + 1, 8, gx * TILE_X)
+            window = pltpu.roll(window, lax.rem(8 - rest, 8), 1)
+            within = iota((full_y // 8, 8, gx * TILE_X), 1) < 8 - rest
+            out_ref[k] = jnp.where(within, window[:-1], window[1:]).reshape(full_y, gx * TILE_X)
+
+    def copy(h, out_ref):
+        for k in range(3):
+            for a in range(gx):
+                out_ref[k, :, a * TILE_X : (a + 1) * TILE_X] = tile(h, k, a)
+
+    if first:
+
+        @pl.when(ints_ref[0] == 0)
+        def _():
+            work(low, far_ref)
+            work(1 - low, near_ref)
+
+        @pl.when(ints_ref[0] > 0)
+        def _():
+            copy(low, far_ref)
+            copy(1 - low, near_ref)
+    else:
+        work(low, far_ref)
+        work(1 - low, near_ref)
+
+
+def place(ints, matrix, got, gx, gy, first):
+    shape = (3, gy * TILE_Y, gx * TILE_X)
+
+    def body(*refs):
+        place_kernel(gx, gy, first, *refs)
+
+    return pl.pallas_call(
+        body,
+        in_specs=[
+            pl.BlockSpec(memory_space=pltpu.SMEM),
+            pl.BlockSpec(memory_space=pltpu.SMEM),
+            pl.BlockSpec(memory_space=pltpu.VMEM),
+        ],
+        out_specs=[pl.BlockSpec(memory_space=pltpu.VMEM)] * 2,
+        out_shape=[jax.ShapeDtypeStruct(shape, f32)] * 2,
+        scratch_shapes=[pltpu.VMEM((TILE_Y * (gy + 1) + 8, gx * TILE_X), f32)],
+        compiler_params=params(),
+        name="place",
+    )(ints, matrix, got)
+
+
+def split(value):
+    high = value.astype(bf16)
+    return high, (value - high.astype(f32)).astype(bf16)
+
+
+def dot(a, b):
+    return lax.dot_general(a, b, (((1,), (0,)), ((), ())), preferred_element_type=f32)
+
+
+def x_ops_kernel(pos_ref, mine_ref, first_ref, second_ref, high_ref, low_ref):
+    place_x = pos_ref[0]
+    core = pos_ref[1]
+    rows = mine_ref.shape[2]
+
+    def put(cls, block, where):
+        high, low = split(block.T)
+        spot = pl.ds(pl.multiple_of(where * rows, rows), rows)
+        high_ref[cls, 0, :, spot] = high
+        low_ref[cls, 0, :, spot] = low
+
+    for cls in range(NCLASS):
+        put(cls, mine_ref[cls, 0], place_x)
+    half = NCLASS // 2
+    for cls in range(half):
+        put(core * half + cls, first_ref[cls, 0], 1 - place_x)
+        put((1 - core) * half + cls, second_ref[cls, 0], 1 - place_x)
+
+
+def y_ops_kernel(pos_ref, b0_ref, b1_ref, b2_ref, b3_ref, high_ref, low_ref):
+    me = pos_ref[2]
+    rows = b0_ref.shape[2]
+    for step, ref in enumerate((b0_ref, b1_ref, b2_ref, b3_ref)):
+        spot = pl.ds(pl.multiple_of((me ^ step) * rows, rows), rows)
+        for cls in range(NCLASS):
+            high, low = split(ref[cls, 0])
+            high_ref[cls, 0, spot, :] = high
+            low_ref[cls, 0, spot, :] = low
+
+
+def prepare_ops(kernel, pos, blocks, length, name):
+    def spec(block):
+        return pl.BlockSpec((block.shape[0], 1) + block.shape[2:], lambda k: (0, k, 0, 0))
+
+    out = jax.ShapeDtypeStruct((NCLASS, 3, length, length), bf16)
+    return pl.pallas_call(
+        kernel,
+        grid=(3,),
+        in_specs=[pl.BlockSpec(memory_space=pltpu.SMEM)] + [spec(b) for b in blocks],
+        out_specs=[spec(out)] * 2,
+        out_shape=[out] * 2,
+        compiler_params=params(),
+        name=name,
+    )(pos, *blocks)
+
+
+def gathered_ops(x_ops, y_ops):
+    place_x = lax.axis_index("gx")
+    place_y = lax.axis_index("gy")
+    core = lax.rem(place_y, 2)
+    half = NCLASS // 2
+    swap_x = [(0, 1), (1, 0)]
+    beside = [(i, i ^ 1) for i in range(4)]
+    across = [(i, i ^ 2) for i in range(4)]
+    piece = lax.dynamic_slice_in_dim(x_ops, core * half, half, 0)
+    got_x = lax.ppermute(piece, "gx", swap_x)
+    got_y = lax.ppermute(y_ops, "gy", across)
+    pair_x = lax.ppermute(got_x, "gy", beside)
+    pair_y = lax.ppermute(y_ops, "gy", beside)
+    cross_y = lax.ppermute(got_y, "gy", beside)
+    pos = jnp.stack([place_x, core, place_y]).astype(jnp.int32)
+    length = x_ops.shape[3]
+    x_parts = prepare_ops(x_ops_kernel, pos, (x_ops, got_x, pair_x), length, "x_operators")
+    y_parts = prepare_ops(
+        y_ops_kernel, pos, (y_ops, pair_y, got_y, cross_y), y_ops.shape[3], "y_operators"
+    )
+    return x_parts, y_parts
+
+
+def sweep_kernel(
+    gx, gy, count, last, xclass_ref, yclass_ref, xh_ref, xl_ref, yh_ref, yl_ref, *refs
+):
+    ins = refs[: CHUNKS * count]
+    outs = refs[CHUNKS * count :]
+    xclass = xclass_ref[...]
+    yclass = yclass_ref[...]
+    for chunk in range(CHUNKS):
+        state = ins[chunk * count][0]
+        for extra in ins[chunk * count + 1 : (chunk + 1) * count]:
+            state = state + extra[0]
+        high, low = split(state)
+        swept = jnp.zeros(state.shape, f32)
+        for cls in range(NCLASS):
+            part = dot(high, xh_ref[cls, 0]) + dot(low, xh_ref[cls, 0]) + dot(high, xl_ref[cls, 0])
+            swept = jnp.where(xclass == cls, part, swept)
+        high, low = split(swept)
+        final = jnp.zeros(state.shape, f32)
+        for cls in range(NCLASS):
+            part = dot(yh_ref[cls, 0], high) + dot(yh_ref[cls, 0], low) + dot(yl_ref[cls, 0], high)
+            final = jnp.where(yclass == cls, part, final)
+        if last:
+            for a in range(gx):
+                for b in range(gy):
+                    outs[0][a * gy + b, chunk, 0] = final[
+                        b * TILE_Y : (b + 1) * TILE_Y, a * TILE_X : (a + 1) * TILE_X
+                    ]
+        else:
+            outs[chunk][0] = final
+
+
+def sweep(classes, x_parts, y_parts, terms, gx, gy, last):
+    full_y, full_x = gy * TILE_Y, gx * TILE_X
+    count = len(terms[0])
+    field = pl.BlockSpec((1, full_y, full_x), lambda k: (k, 0, 0))
+    xop = pl.BlockSpec((NCLASS, 1, full_x, full_x), lambda k: (0, k, 0, 0))
+    yop = pl.BlockSpec((NCLASS, 1, full_y, full_y), lambda k: (0, k, 0, 0))
+    if last:
+        out_specs = pl.BlockSpec(
+            (gx * gy, CHUNKS, 1, TILE_Y, TILE_X), lambda k: (0, 0, k, 0, 0)
+        )
+        out_shape = jax.ShapeDtypeStruct((gx * gy, CHUNKS, 3, TILE_Y, TILE_X), f32)
+    else:
+        out_specs = [field] * CHUNKS
+        out_shape = [jax.ShapeDtypeStruct((3, full_y, full_x), f32)] * CHUNKS
+
+    def body(*refs):
+        sweep_kernel(gx, gy, count, last, *refs)
+
+    return pl.pallas_call(
+        body,
+        grid=(3,),
+        in_specs=[
+            pl.BlockSpec((full_y, 1), lambda k: (0, 0)),
+            pl.BlockSpec((1, full_x), lambda k: (0, 0)),
+            xop,
+            xop,
+            yop,
+            yop,
+        ]
+        + [field] * (CHUNKS * count),
+        out_specs=out_specs,
+        out_shape=out_shape,
+        compiler_params=params(),
+        name="sweep",
+    )(*classes, *x_parts, *y_parts, *[t for chunk in terms for t in chunk])
+
+
+def output_kernel(flag_ref, u_ref, first_ref, second_ref, out_ref, turned):
+    groups = first_ref.shape[0]
+    per = CZ // groups
+    half = per // 2
+
+    @pl.when(flag_ref[0] == 0)
+    def _():
+        for z in range(CZ):
+            turned[pl.ds(z, TILE_Y, stride=CZ), :] = u_ref[z, 0]
+
+    @pl.when(flag_ref[0] > 0)
+    def _():
+        for z in range(CZ):
+            g, i = divmod(z, per)
+            ref = first_ref if i < half else second_ref
+            turned[pl.ds(z, TILE_Y, stride=CZ), :] = ref[g, i % half, 0]
+
+    out_ref[0, 0] = turned[...].T
+
+
+def to_output(flag, planes, first, second):
+    part = pl.BlockSpec(first.shape[:2] + (1, TILE_Y, TILE_X), lambda c: (0, 0, c, 0, 0))
+    return pl.pallas_call(
+        output_kernel,
+        grid=(3,),
+        in_specs=[
+            pl.BlockSpec(memory_space=pltpu.SMEM),
+            pl.BlockSpec((CZ, 1, TILE_Y, TILE_X), lambda c: (0, c, 0, 0)),
+            part,
+            part,
+        ],
+        out_specs=pl.BlockSpec((1, 1, TILE_X, TILE_Y * CZ), lambda c: (0, c, 0, 0)),
+        out_shape=jax.ShapeDtypeStruct((1, 3, TILE_X, TILE_Y * CZ), f32),
+        scratch_shapes=[pltpu.VMEM((TILE_Y * CZ, TILE_X), f32)],
+        compiler_params=params(),
+        name="to_output",
+    )(flag, planes, first, second)
+
+
+def local(fields, x_ops, y_ops, x_line_class, y_line_class, box_offset, coupling):
+    gx, gy = lax.axis_size("gx"), lax.axis_size("gy")
+    groups = gx * gy
+    sec = lax.axis_index("sec")
+    active = (sec == 3).astype(jnp.int32)
+    member = jnp.minimum(sec, 2)
+    offsets = lax.dynamic_index_in_dim(box_offset, member, 0, keepdims=False)
+    matrix = lax.dynamic_index_in_dim(coupling, member, 0, keepdims=False) * (0.25 * time_step)
+    matrix = jnp.where(active > 0, jnp.zeros_like(matrix), matrix)
+    flag = active.reshape(1)
+    lower = (sec < 2).astype(jnp.int32)
+    ints = jnp.stack([active, lower, offsets[0], offsets[1]])
+
+    planes, *edges = to_planes(fields[0])
+    halo = exchange(*edges)
+    x_parts, y_parts = gathered_ops(x_ops, y_ops)
+    xclass = lax.all_gather(x_line_class, "gy", axis=0, tiled=True).reshape(-1, 1)
+    yclass = lax.all_gather(y_line_class, "gx", axis=0, tiled=True).reshape(1, -1)
+
+    acoustic = None
+    for repeat in range(STEPS):
+        last = repeat == STEPS - 1
+        outs = flow(flag, planes, halo, groups, last)
+        planes = outs[CHUNKS]
+        if not last:
+            halo = exchange(*outs[CHUNKS + 1 :])
+        terms = []
+        for chunk in range(CHUNKS):
+            got = lax.all_to_all(outs[chunk], ("gx", "gy"), 0, 0)
+            far, near = place(ints, matrix, got, gx, gy, repeat == 0)
+            passed = lax.ppermute(far, "sec", [(0, 1), (3, 2)] if repeat == 0 else [(0, 1)])
+            passed = lax.ppermute(far + passed, "sec", [(1, 2), (2, 1)])
+            passed = lax.ppermute(near + passed, "sec", [(1, 0), (2, 3)])
+            term = (near, passed)
+            if acoustic is not None:
+                term = (acoustic[chunk],) + term
+            terms.append(term)
+        acoustic = sweep((xclass, yclass), x_parts, y_parts, terms, gx, gy, last)
+    tiles = lax.all_to_all(acoustic, ("gx", "gy"), 0, 0)
+    brought = lax.ppermute(tiles, "sec", [(0, 3)])
+    return to_output(flag, planes, brought, tiles)
+
+
 highest = lax.Precision.HIGHEST
 
 
@@ -115,7 +614,7 @@
     return add_piece(initial, lax.all_gather(state, "gy", axis=3, tiled=True), jnp.int32(0))
 
 
-def local(fields, x_ops, y_ops, x_line_class, y_line_class, box_offset, coupling):
+def local_general(fields, x_ops, y_ops, x_line_class, y_line_class, box_offset, coupling):
     sections = lax.axis_size("sec")
     section_index = lax.axis_index("sec")
     active = section_index == sections - 1
@@ -161,6 +660,11 @@
     return current.reshape(1, 3, span_x, merged)
 
 
+def whole_planes_fit(mesh):
+    sizes = dict(mesh.shape)
+    return sizes["sec"] == 4 and sizes["gx"] == 2 and sizes["gy"] == 4
+
+
 def solution(mesh):
     placed = (
         P("sec", None, "gx", "gy"),
@@ -172,5 +676,9 @@
         P(),
     )
     return jax.shard_map(
-        local, mesh=mesh, in_specs=placed, out_specs=P("sec", None, "gx", "gy"), check_vma=False
+        local if whole_planes_fit(mesh) else local_general,
+        mesh=mesh,
+        in_specs=placed,
+        out_specs=P("sec", None, "gx", "gy"),
+        check_vma=False,
     )

time: 773 us -> 374 us (0.48)
  waiting for transfers between devices: 349 us -> 135 us
  local copies, waits for them, and re-layouts: 189 us -> 7.76 us
  other arithmetic: 135 us -> 11.8 us
  blocking collectives: 0 us -> 87.9 us
  Pallas kernels: 0 us -> 77 us
  matrix products: 37.9 us -> 0 us
  between operations: 16.7 us -> 1.18 us
  starting transfers between devices: 38.3 us -> 52.1 us
    all_gather x5 -> x0, waiting for transfers between devices: 147 us -> none  [the longest x1 63.6 us: local(): whole_end = lax.all_gather(acoustic, 'sec', axis=3, tiled=True)]
    reduce_scatter x2 -> x0, waiting for transfers between devices: 113 us -> none  [local(): lax.psum_scatter(contribution, 'sec', scatter_dimension=3, tiled=True)]
    all_to_all x0 -> x3, blocking collectives: none -> 78.7 us  [the longest x2 54.2 us: local(): got = lax.all_to_all(outs[chunk], ('gx', 'gy'), 0, 0)]
    pallas_call x0 -> x12, Pallas kernels: none -> 77 us  [the longest x2 21.3 us: flow(): pl.pallas_call(body, grid=(groups,), in_specs=[pl.BlockSpec(memory_space=...]
    ppermute x12 -> x26, waiting for transfers between devices: 61.3 us -> 135 us  [the longest x4 48.6 us: local(): passed = lax.ppermute(near + passed, 'sec', [(1, 0), (2, 3)])]
    ppermute x8 -> x0, local copies, waits for them, and re-layouts: 51.7 us -> none  [the longest x2 25.5 us: shifted(): lax.ppermute(value, axis, [(source, source + steps) for source in range(i...]
    mul x6 -> x0, other arithmetic: 48.8 us -> none  [the longest x2 24.9 us: flow_core(): slope_y = 0.5 * (ahead_y - behind_y)]
    concatenate x5 -> x0, other arithmetic: 43.5 us -> none  [the longest x4 29.9 us: padded_2(): block = jnp.concatenate([low, block, high], axis=dim)]
  transfers between devices with their start and end apart: 20 -> 28, of which waited for: 10 -> 12; matrix products, arithmetic and copies ran while one was open for 32% -> 4% of each run, Pallas kernels for 0% -> 11%
where the time goes in v1:
time: 374 us; the launch traced here: 373 us
  waiting for transfers between devices  135 us (36%)
  blocking collectives  87.9 us (24%)
  Pallas kernels  77 us (21%)
  starting transfers between devices  52.1 us (14%)
  other arithmetic  11.8 us (3%)
  local copies, waits for them, and re-layouts  7.76 us (2%)
    all_to_all x2, blocking collectives, local(): got = lax.all_to_all(outs[chunk], ('gx', 'gy'), 0, 0)  54.2 us
    ppermute x4, waiting for transfers between devices, local(): passed = lax.ppermute(near + passed, 'sec', [(1, 0), (2, 3)])  48.6 us
    ppermute x4, waiting for transfers between devices, local(): lax.ppermute(far, 'sec', [(0, 1), (3, 2)] if repeat == 0 else [(0, 1)])  40.8 us
    ppermute x1, waiting for transfers between devices, local(): brought = lax.ppermute(tiles, 'sec', [(0, 3)])  32.9 us
    all_to_all x1, blocking collectives, local(): tiles = lax.all_to_all(acoustic, ('gx', 'gy'), 0, 0)  24.5 us
    pallas_call x2, Pallas kernels, flow(): pl.pallas_call(body, grid=(groups,), in_specs=[pl.BlockSpec(memory_space=...  21.3 us
    pallas_call x2, Pallas kernels, sweep(): pl.pallas_call(body, grid=(3,), in_specs=[pl.BlockSpec((full_y, 1), lambd...  18.2 us
    ppermute x8, starting transfers between devices, send(): lax.ppermute(value, axis, [(i, i + step) for i in range(count) if 0 <= i...  17.7 us
  transfers between devices with their start and end apart: 28, of which 12 were waited for; matrix products, arithmetic and copies ran while one was open for 4% of the time, Pallas kernels for 11%

profile of v1, /device:TPU:0, one launch (start us, length us, event | category | flops | bytes accessed | tf_op | source)
XLA Modules:
  0.0 373.0 jit_solution(11386184226583826630)
XLA Ops:
  0.0 6.5 %to_planes.1 = (f32[32,3,64,128]{3,2,1,0:T(8,128)}, f32[64,128]{1,0:T(8,128)}, f32[64,128]{1,0:T(8,128)}, f32[3,32,128]{2,1,0:T(8,128)}, f32[3,32,128]{2,1,0:T(8,128)}) custom-call(f32[3,128,2048]{2,1,0:T(8,128)} %bitcast.14), custom_call_target="tpu_custom_call" | custom-call | tf_op jit(solution)/shard_map/to_planes/pallas_call | solution.py:56
  6.5 2.4 collective-permute-start.2
  8.9 1.3 collective-permute-start.3
  10.2 4.3 %collective-permute-start = (f32[64,128]{1,0:T(8,128)}, f32[64,128]{1,0:T(8,128)S(1)}, u32[]{:S(2)}, u32[]{:S(2)}) collective-permute-start(f32[64,128]{1,0:T(8,128)} %get-tuple-element.35), channel_id=1, source_target_pairs={{0,4},{1,5},{2,6},{3,7},{8,12},{9,13},{10,14},{11,15},{16,20},{17,... | collective-permute-start | bytes 98312 | tf_op jit(solution)/shard_map/ppermute | solution.py:187
  14.4 1.3 collective-permute-start.1
  16.3 4.1 %collective-permute-done.1.refs_3_ = f32[64,128]{1,0:T(8,128)S(1)} collective-permute-done((f32[64,128]{1,0:T(8,128)}, f32[64,128]{1,0:T(8,128)S(1)}, u32[]{:S(2)}, u32[]{:S(2)}) %collective-permute-start.1) | collective-permute-done | bytes 32800 | tf_op jit(solution)/shard_map/ppermute | solution.py:187
  21.1 12.8 %flow.2 = (f32[8,2,3,64,128]{4,3,2,1,0:T(8,128)}, f32[8,2,3,64,128]{4,3,2,1,0:T(8,128)}, f32[32,3,64,128]{3,2,1,0:T(8,128)}, f32[64,128]{1,0:T(8,128)}, f32[64,1...) custom-call(s32[1]{0:T(128)} %bitcast.refs_0_.flag_ref, f32[32,3,64,128]{3,2,1,0:T(8,128)} %get-tuple-element.34.refs_1_, ...), custom_call_target="tpu_custom_call" | custom-call | tf_op jit(solution)/shard_map/flow/pallas_call | solution.py:166
  33.9 26.4 %all_to_all.25.refs_2_ = f32[8,2,3,64,128]{4,3,2,1,0:T(8,128)} all-to-all(f32[8,2,3,64,128]{4,3,2,1,0:T(8,128)} %get-tuple-element.49), channel_id=1, replica_groups=mesh['sec'=4,'gx'=2,'gy'=4] {'gx','gy'}, dimensions={0} | all-to-all | bytes 3145728 | tf_op jit(solution)/shard_map/all_to_all | solution.py:497
  60.3 3.7 all-to-all-start.1
  64.0 2.3 collective-permute-start.6
  66.3 1.3 collective-permute-start.7
  67.7 3.6 collective-permute-start.4
  71.3 1.3 collective-permute-start.5
  72.6 5.8 %collective-permute-done.4.refs_2_ = f32[64,128]{1,0:T(8,128)S(1)} collective-permute-done((f32[64,128]{1,0:T(8,128)S(1)}, f32[64,128]{1,0:T(8,128)S(1)}, u32[]{:S(2)}, u32[]{:S(2)}) %collective-permute-start.4) | collective-permute-done | bytes 32800 | tf_op jit(solution)/shard_map/ppermute | solution.py:187
  78.4 2.4 collective-permute-done.5.refs_3_
  81.4 8.5 %flow.3 = (f32[8,2,3,64,128]{4,3,2,1,0:T(8,128)}, f32[8,2,3,64,128]{4,3,2,1,0:T(8,128)}, f32[32,3,64,128]{3,2,1,0:T(8,128)}) custom-call(s32[1]{0:T(128)} %bitcast.refs_0_.flag_ref, f32[32,3,64,128]{3,2,1,0:T(8,128)} %get-tuple-element.39.refs_1_, f32[64,128]{1,0:T(8,128)} %copy-done.29, f32[64,128]{1,0:T(8,128)} %copy-done.30, f32[3,32,128]{2,1,0:T(8,128)} %copy-done.25, ...), custom_call_target="tpu_custom_call" | custom-call | tf_op jit(solution)/shard_map/flow/pallas_call | solution.py:166
  89.8 27.8 %all_to_all.26.refs_2_ = f32[8,2,3,64,128]{4,3,2,1,0:T(8,128)} all-to-all(f32[8,2,3,64,128]{4,3,2,1,0:T(8,128)} %get-tuple-element.60), channel_id=1, replica_groups=mesh['sec'=4,'gx'=2,'gy'=4] {'gx','gy'}, dimensions={0} | all-to-all | bytes 3145728 | tf_op jit(solution)/shard_map/all_to_all | solution.py:497
  117.7 3.6 all-to-all-start.2
  121.9 1.9 pad_add_fusion.1.refs_0_
  125.0 3.7 place.5
  128.7 4.4 %collective-permute-start.16 = (f32[3,256,256]{2,1,0:T(8,128)}, f32[3,256,256]{2,1,0:T(8,128)}, u32[]{:S(2)}, u32[]{:S(2)}) collective-permute-start(f32[3,256,256]{2,1,0:T(8,128)} %get-tuple-element.54), channel_id=1, source_target_pairs={{0,8},{24,16},{1,9},{25,17},{2,10},{26,18},{3,11},{27,19},{4,12},{... | collective-permute-start | bytes 2359304 | tf_op jit(solution)/shard_map/ppermute | solution.py:499
  133.2 3.6 place.4
  136.8 2.2 collective-permute-start.13
  139.0 3.6 place.7
  142.6 2.2 collective-permute-start.22
  145.9 3.6 place.6
  149.5 1.3 collective-permute-start.19
  150.9 2.0 collective-permute-start.8
  152.9 1.5 collective-permute-start.11
  155.6 11.6 %collective-permute-done.13 = f32[3,256,256]{2,1,0:T(8,128)} collective-permute-done((f32[3,256,256]{2,1,0:T(8,128)}, f32[3,256,256]{2,1,0:T(8,128)}, u32[]{:S(2)}, u32[]{:S(2)}) %collective-permute-start.13) | collective-permute-done | bytes 786464 | tf_op jit(solution)/shard_map/ppermute | solution.py:499
  169.3 14.8 %collective-permute-done.22 = f32[3,256,256]{2,1,0:T(8,128)} collective-permute-done((f32[3,256,256]{2,1,0:T(8,128)}, f32[3,256,256]{2,1,0:T(8,128)}, u32[]{:S(2)}, u32[]{:S(2)}) %collective-permute-start.22) | collective-permute-done | bytes 786464 | tf_op jit(solution)/shard_map/ppermute | solution.py:499
  186.1 14.3 %collective-permute-done.19 = f32[3,256,256]{2,1,0:T(8,128)S(1)} collective-permute-done((f32[3,256,256]{2,1,0:T(8,128)}, f32[3,256,256]{2,1,0:T(8,128)S(1)}, u32[]{:S(2)}, u32[]{:S(2)}) %collective-permute-start.19) | collective-permute-done | bytes 786464 | tf_op jit(solution)/shard_map/ppermute | solution.py:499
  204.8 1.4 collective-permute-start.18
  206.2 1.3 collective-permute-start.15
  213.8 5.1 %all-reduce = s32[256]{0:T(256)S(1)} all-reduce(s32[256]{0:T(256)S(1)} %dynamic-update-slice), channel_id=1, replica_groups=mesh['sec'=4,'gx'=2,'gy'=4] {'gy'}, use_global_device_ids=true, to_apply=%add | all-reduce | flops 256 | bytes 2048
  219.7 4.2 %all-gather = s32[2,1,128]{2,1,0:T(1,128)} all-gather(s32[1,1,128]{2,1,0:T(1,128)S(1)} %bitcast.18), channel_id=1, replica_groups=mesh['sec'=4,'gx'=2,'gy'=4] {'gx'}, dimensions={0}, use_global_device_ids=true | all-gather | bytes 1536 | tf_op jit(solution)/shard_map/all_gather | solution.py:486
  224.5 4.9 %x_operators.1 = (bf16[4,3,256,256]{3,2,1,0:T(8,128)(2,1)}, bf16[4,3,256,256]{3,2,1,0:T(8,128)(2,1)}) custom-call(s32[3]{0:T(128)} %pad_add_fusion.pos_ref, f32[4,3,128,256]{3,2,1,0:T(8,128)} %mine_ref.1, f32[2,3,128,256]{3,2,1,0:T(8,128)} %copy-done.20, f32[2,3,128,256]{3,2,1,0:T(8,128)} %copy-done.22), custom_call_target="tpu_custom_call" | custom-call | tf_op jit(solution)/shard_map/x_operators/pallas_call | solution.py:328
  229.4 4.4 %y_operators.1 = (bf16[4,3,256,256]{3,2,1,0:T(8,128)(2,1)}, bf16[4,3,256,256]{3,2,1,0:T(8,128)(2,1)}) custom-call(s32[3]{0:T(128)} %pad_add_fusion.pos_ref, f32[4,3,64,256]{3,2,1,0:T(8,128)} %b0_ref.1, f32[4,3,64,256]{3,2,1,0:T(8,128)} %copy-done.21, f32[4,3,64,256]{3,2,1,0:T(8,128)} %collective-permute-done.11.b2_ref, ...), custom_call_target="tpu_custom_call" | custom-call | tf_op jit(solution)/shard_map/y_operators/pallas_call | solution.py:328
  233.8 7.9 %collective-permute-done.18.refs_9_ = f32[3,256,256]{2,1,0:T(8,128)S(1)} collective-permute-done((f32[3,256,256]{2,1,0:T(8,128)}, f32[3,256,256]{2,1,0:T(8,128)S(1)}, u32[]{:S(2)}, u32[]{:S(2)}) %collective-permute-start.18) | collective-permute-done | bytes 786464 | tf_op jit(solution)/shard_map/ppermute | solution.py:501
  241.7 18.8 %collective-permute-done.15.refs_7_ = f32[3,256,256]{2,1,0:T(8,128)S(1)} collective-permute-done((f32[3,256,256]{2,1,0:T(8,128)}, f32[3,256,256]{2,1,0:T(8,128)S(1)}, u32[]{:S(2)}, u32[]{:S(2)}) %collective-permute-start.15) | collective-permute-done | bytes 786464 | tf_op jit(solution)/shard_map/ppermute | solution.py:501
  261.5 9.0 %sweep.2 = (f32[3,256,256]{2,1,0:T(8,128)}, f32[3,256,256]{2,1,0:T(8,128)}) custom-call(s32[256,1]{1,0:T(8,128)} %copy.11.refs_0_, s32[1,256]{1,0:T(1,128)} %bitcast.15, bf16[4,3,256,256]{3,2,1,0:T(8,128)(2,1)} %get-tuple-element.45.refs_2_, bf16[4,3,256,256]{3,2,1,0:T(8,128)(2,1)} %get-tuple-element.46.refs_3_, ...), custom_call_target="tpu_custom_call" | custom-call | tf_op jit(solution)/shard_map/sweep/pallas_call | solution.py:411
  270.4 7.0 %collective-permute-done.24.refs_11_ = f32[3,256,256]{2,1,0:T(8,128)S(1)} collective-permute-done((f32[3,256,256]{2,1,0:T(8,128)}, f32[3,256,256]{2,1,0:T(8,128)S(1)}, u32[]{:S(2)}, u32[]{:S(2)}) %collective-permute-start.24) | collective-permute-done | bytes 786464 | tf_op jit(solution)/shard_map/ppermute | solution.py:501
  277.4 14.9 %collective-permute-done.21.refs_8_ = f32[3,256,256]{2,1,0:T(8,128)S(1)} collective-permute-done((f32[3,256,256]{2,1,0:T(8,128)}, f32[3,256,256]{2,1,0:T(8,128)S(1)}, u32[]{:S(2)}, u32[]{:S(2)}) %collective-permute-start.21) | collective-permute-done | bytes 786464 | tf_op jit(solution)/shard_map/ppermute | solution.py:501
  293.2 9.3 %sweep.3 = f32[8,2,3,64,128]{4,3,2,1,0:T(8,128)} custom-call(s32[256,1]{1,0:T(8,128)} %copy.11.refs_0_, s32[1,256]{1,0:T(1,128)} %bitcast.16, bf16[4,3,256,256]{3,2,1,0:T(8,128)(2,1)} %get-tuple-element.45.refs_2_, bf16[4,3,256,256]{3,2,1,0:T(8,128)(2,1)} %get-tuple-element.46.refs_3_, bf16[4,3,256,256]{3,2,1,0:T(8,128)(2,1)} %get-tuple-element.47.refs_4_, ...), custom_call_target="tpu_custom_call" | custom-call | tf_op jit(solution)/shard_map/sweep/pallas_call | solution.py:411
  302.5 24.5 %all_to_all.27.second_ref = f32[8,2,3,64,128]{4,3,2,1,0:T(8,128)S(1)} all-to-all(f32[8,2,3,64,128]{4,3,2,1,0:T(8,128)} %sweep.3), channel_id=1, replica_groups=mesh['sec'=4,'gx'=2,'gy'=4] {'gx','gy'}, dimensions={0} | all-to-all | bytes 3145728 | tf_op jit(solution)/shard_map/all_to_all | solution.py:507
  326.9 4.7 %collective-permute-start.25 = (f32[8,2,3,64,128]{4,3,2,1,0:T(8,128)S(1)}, f32[8,2,3,64,128]{4,3,2,1,0:T(8,128)S(1)}, u32[]{:S(2)}, u32[]{:S(2)}) collective-permute-start(f32[8,2,3,64,128]{4,3,2,1,0:T(8,128)S(1)} %all_to_all.27.second_ref), channel_id=1, source_target_pairs={{0,24},{1,25},{2,26},{3,27},{4,28},{5,29},{6,30},{7,31}} | collective-permute-start | bytes 4718600 | tf_op jit(solution)/shard_map/ppermute | solution.py:508
  331.7 32.9 %collective-permute-done.25.first_ref = f32[8,2,3,64,128]{4,3,2,1,0:T(8,128)S(1)} collective-permute-done((f32[8,2,3,64,128]{4,3,2,1,0:T(8,128)S(1)}, f32[8,2,3,64,128]{4,3,2,1,0:T(8,128)S(1)}, u32[]{:S(2)}, u32[]{:S(2)}) %collective-permute-start.25) | collective-permute-done | bytes 1572896 | tf_op jit(solution)/shard_map/ppermute | solution.py:508
  365.8 7.2 %to_output.1 = f32[1,3,128,2048]{3,2,1,0:T(8,128)} custom-call(s32[1]{0:T(128)} %bitcast.refs_0_.flag_ref, f32[32,3,64,128]{3,2,1,0:T(8,128)} %get-tuple-element.44.u_ref, f32[8,2,3,64,128]{4,3,2,1,0:T(8,128)} %copy-done.10, f32[8,2,3,64,128]{4,3,2,1,0:T(8,128)} %copy-done.4), custom_call_target="tpu_custom_call" | custom-call | tf_op jit(solution)/shard_map/to_output/pallas_call | solution.py:452
  (119 shorter events, 24.4 us)
Async XLA Ops:
  0.0 121.3 %copy-start = (s32[3,2]{0,1:T(2,128)S(1)}, s32[3,2]{0,1:T(2,128)}, u32[]{:S(2)}) copy-start(s32[3,2]{0,1:T(2,128)} %param.12) | copy-start | bytes 76
  6.5 14.0 %collective-permute-start.2 = (f32[3,32,128]{2,1,0:T(8,128)}, f32[3,32,128]{2,1,0:T(8,128)S(1)}, u32[]{:S(2)}, u32[]{:S(2)}) collective-permute-start(f32[3,32,128]{2,1,0:T(8,128)} %get-tuple-element.37), channel_id=1, source_target_pairs={{0,1},{1,2},{2,3},{4,5},{5,6},{6,7},{8,9},{9,10},{10,11},{12,13},{... | collective-permute-start | bytes 147464 | tf_op jit(solution)/shard_map/ppermute | solution.py:187
  8.9 11.6 %collective-permute-start.3 = (f32[3,32,128]{2,1,0:T(8,128)}, f32[3,32,128]{2,1,0:T(8,128)S(1)}, u32[]{:S(2)}, u32[]{:S(2)}) collective-permute-start(f32[3,32,128]{2,1,0:T(8,128)} %get-tuple-element.38), channel_id=1, source_target_pairs={{1,0},{2,1},{3,2},{5,4},{6,5},{7,6},{9,8},{10,9},{11,10},{13,12},{... | collective-permute-start | bytes 147464 | tf_op jit(solution)/shard_map/ppermute | solution.py:187
  10.2 6.2 %collective-permute-start = (f32[64,128]{1,0:T(8,128)}, f32[64,128]{1,0:T(8,128)S(1)}, u32[]{:S(2)}, u32[]{:S(2)}) collective-permute-start(f32[64,128]{1,0:T(8,128)} %get-tuple-element.35), channel_id=1, source_target_pairs={{0,4},{1,5},{2,6},{3,7},{8,12},{9,13},{10,14},{11,15},{16,20},{17,... | collective-permute-start | bytes 98312 | tf_op jit(solution)/shard_map/ppermute | solution.py:187
  14.4 6.0 %collective-permute-start.1 = (f32[64,128]{1,0:T(8,128)}, f32[64,128]{1,0:T(8,128)S(1)}, u32[]{:S(2)}, u32[]{:S(2)}) collective-permute-start(f32[64,128]{1,0:T(8,128)} %get-tuple-element.36), channel_id=1, source_target_pairs={{4,0},{5,1},{6,2},{7,3},{12,8},{13,9},{14,10},{15,11},{20,16},{21,... | collective-permute-start | bytes 98312 | tf_op jit(solution)/shard_map/ppermute | solution.py:187
  16.3 4.2 %copy-start.27 = (f32[64,128]{1,0:T(8,128)}, f32[64,128]{1,0:T(8,128)S(1)}, u32[]{:S(2)}) copy-start(f32[64,128]{1,0:T(8,128)S(1)} %collective-permute-done.refs_2_) | copy-start | bytes 98308
  60.3 6.1 %copy-start.31 = (f32[3,32,128]{2,1,0:T(8,128)S(1)}, f32[3,32,128]{2,1,0:T(8,128)}, u32[]{:S(2)}) copy-start(f32[3,32,128]{2,1,0:T(8,128)} %get-tuple-element.43) | copy-start | bytes 147460
  60.3 7.4 %copy-start.34 = (f32[64,128]{1,0:T(8,128)S(1)}, f32[64,128]{1,0:T(8,128)}, u32[]{:S(2)}) copy-start(f32[64,128]{1,0:T(8,128)} %get-tuple-element.40) | copy-start | bytes 98308
  60.3 11.0 %copy-start.33 = (f32[64,128]{1,0:T(8,128)S(1)}, f32[64,128]{1,0:T(8,128)}, u32[]{:S(2)}) copy-start(f32[64,128]{1,0:T(8,128)} %get-tuple-element.41) | copy-start | bytes 98308
  60.3 29.5 %all-to-all-start.1 = ((f32[8,2,3,64,128]{4,3,2,1,0:T(8,128)}), f32[8,2,3,64,128]{4,3,2,1,0:T(8,128)S(1)}, u32[]{:S(2)}, u32[]{:S(2)}) async-start(f32[8,2,3,64,128]{4,3,2,1,0:T(8,128)} %get-tuple-element.52), calls=%async_computation.1 | async-start | bytes 3145728 | tf_op jit(solution)/shard_map/all_to_all | solution.py:497
  64.0 16.7 %collective-permute-start.6 = (f32[3,32,128]{2,1,0:T(8,128)S(1)}, f32[3,32,128]{2,1,0:T(8,128)S(1)}, u32[]{:S(2)}, u32[]{:S(2)}) collective-permute-start(f32[3,32,128]{2,1,0:T(8,128)S(1)} %copy-done.32), channel_id=1, source_target_pairs={{0,1},{1,2},{2,3},{4,5},{5,6},{6,7},{8,9},{9,10},{10,11},{12,13},{... | collective-permute-start | bytes 147464 | tf_op jit(solution)/shard_map/ppermute | solution.py:187
  66.3 14.4 %collective-permute-start.7 = (f32[3,32,128]{2,1,0:T(8,128)S(1)}, f32[3,32,128]{2,1,0:T(8,128)S(1)}, u32[]{:S(2)}, u32[]{:S(2)}) collective-permute-start(f32[3,32,128]{2,1,0:T(8,128)S(1)} %copy-done.31), channel_id=1, source_target_pairs={{1,0},{2,1},{3,2},{5,4},{6,5},{7,6},{9,8},{10,9},{11,10},{13,12},{... | collective-permute-start | bytes 147464 | tf_op jit(solution)/shard_map/ppermute | solution.py:187
  67.7 10.7 %collective-permute-start.4 = (f32[64,128]{1,0:T(8,128)S(1)}, f32[64,128]{1,0:T(8,128)S(1)}, u32[]{:S(2)}, u32[]{:S(2)}) collective-permute-start(f32[64,128]{1,0:T(8,128)S(1)} %copy-done.34), channel_id=1, source_target_pairs={{0,4},{1,5},{2,6},{3,7},{8,12},{9,13},{10,14},{11,15},{16,20},{17,... | collective-permute-start | bytes 98312 | tf_op jit(solution)/shard_map/ppermute | solution.py:187
  71.3 9.5 %collective-permute-start.5 = (f32[64,128]{1,0:T(8,128)S(1)}, f32[64,128]{1,0:T(8,128)S(1)}, u32[]{:S(2)}, u32[]{:S(2)}) collective-permute-start(f32[64,128]{1,0:T(8,128)S(1)} %copy-done.33), channel_id=1, source_target_pairs={{4,0},{5,1},{6,2},{7,3},{12,8},{13,9},{14,10},{15,11},{20,16},{21,... | collective-permute-start | bytes 98312 | tf_op jit(solution)/shard_map/ppermute | solution.py:187
  89.8 27.8 %copy-start.2 = (f32[8,2,3,64,128]{4,3,2,1,0:T(8,128)}, f32[8,2,3,64,128]{4,3,2,1,0:T(8,128)S(1)}, u32[]{:S(2)}) copy-start(f32[8,2,3,64,128]{4,3,2,1,0:T(8,128)S(1)} %all-to-all-done.1.refs_2_) | copy-start | bytes 4718596
  117.7 27.1 %all-to-all-start.2 = ((f32[8,2,3,64,128]{4,3,2,1,0:T(8,128)}), f32[8,2,3,64,128]{4,3,2,1,0:T(8,128)S(1)}, u32[]{:S(2)}, u32[]{:S(2)}) async-start(f32[8,2,3,64,128]{4,3,2,1,0:T(8,128)} %get-tuple-element.56), calls=%async_computation.2 | async-start | bytes 3145728 | tf_op jit(solution)/shard_map/all_to_all | solution.py:497
  128.7 24.1 %collective-permute-start.16 = (f32[3,256,256]{2,1,0:T(8,128)}, f32[3,256,256]{2,1,0:T(8,128)}, u32[]{:S(2)}, u32[]{:S(2)}) collective-permute-start(f32[3,256,256]{2,1,0:T(8,128)} %get-tuple-element.54), channel_id=1, source_target_pairs={{0,8},{24,16},{1,9},{25,17},{2,10},{26,18},{3,11},{27,19},{4,12},{... | collective-permute-start | bytes 2359304 | tf_op jit(solution)/shard_map/ppermute | solution.py:499
  136.8 30.5 %collective-permute-start.13 = (f32[3,256,256]{2,1,0:T(8,128)}, f32[3,256,256]{2,1,0:T(8,128)}, u32[]{:S(2)}, u32[]{:S(2)}) collective-permute-start(f32[3,256,256]{2,1,0:T(8,128)} %get-tuple-element.51), channel_id=1, source_target_pairs={{0,8},{24,16},{1,9},{25,17},{2,10},{26,18},{3,11},{27,19},{4,12},{... | collective-permute-start | bytes 2359304 | tf_op jit(solution)/shard_map/ppermute | solution.py:499
  139.0 11.8 %copy-start.5 = (f32[4,3,128,256]{3,2,1,0:T(8,128)S(1)}, f32[4,3,128,256]{3,2,1,0:T(8,128)}, u32[]{:S(2)}) copy-start(f32[4,3,128,256]{3,2,1,0:T(8,128)} %mine_ref.1) | copy-start | bytes 4718596
  142.6 41.5 %collective-permute-start.22 = (f32[3,256,256]{2,1,0:T(8,128)}, f32[3,256,256]{2,1,0:T(8,128)}, u32[]{:S(2)}, u32[]{:S(2)}) collective-permute-start(f32[3,256,256]{2,1,0:T(8,128)} %get-tuple-element.62), channel_id=1, source_target_pairs={{0,8},{1,9},{2,10},{3,11},{4,12},{5,13},{6,14},{7,15}} | collective-permute-start | bytes 2359304 | tf_op jit(solution)/shard_map/ppermute | solution.py:499
  145.9 7.0 %copy-start.19 = (f32[4,3,64,256]{3,2,1,0:T(8,128)S(1)}, f32[4,3,64,256]{3,2,1,0:T(8,128)}, u32[]{:S(2)}) copy-start(f32[4,3,64,256]{3,2,1,0:T(8,128)} %b0_ref.1) | copy-start | bytes 2359300
  145.9 8.4 %copy-start.16 = (f32[3,256,256]{2,1,0:T(8,128)S(1)}, f32[3,256,256]{2,1,0:T(8,128)}, u32[]{:S(2)}) copy-start(f32[3,256,256]{2,1,0:T(8,128)} %get-tuple-element.54) | copy-start | bytes 2359300
  149.5 51.0 %collective-permute-start.19 = (f32[3,256,256]{2,1,0:T(8,128)}, f32[3,256,256]{2,1,0:T(8,128)S(1)}, u32[]{:S(2)}, u32[]{:S(2)}) collective-permute-start(f32[3,256,256]{2,1,0:T(8,128)} %get-tuple-element.58), channel_id=1, source_target_pairs={{0,8},{1,9},{2,10},{3,11},{4,12},{5,13},{6,14},{7,15}} | collective-permute-start | bytes 2359304 | tf_op jit(solution)/shard_map/ppermute | solution.py:499
  150.9 17.1 %copy-start.15 = (f32[3,256,256]{2,1,0:T(8,128)S(1)}, f32[3,256,256]{2,1,0:T(8,128)}, u32[]{:S(2)}) copy-start(f32[3,256,256]{2,1,0:T(8,128)} %get-tuple-element.51) | copy-start | bytes 2359300
  150.9 50.4 %collective-permute-start.8 = (f32[2,3,128,256]{3,2,1,0:T(8,128)S(1)}, f32[2,3,128,256]{3,2,1,0:T(8,128)S(1)}, u32[]{:S(2)}, u32[]{:S(2)}) collective-permute-start(f32[2,3,128,256]{3,2,1,0:T(8,128)S(1)} %constant_dynamic-slice_fusion.1), channel_id=1, source_target_pairs={{0,4},{4,0},{1,5},{5,1},{2,6},{6,2},{3,7},{7,3},{8,12},{12,8},{9,1... | collective-permute-start | bytes 2359304 | tf_op jit(solution)/shard_map/ppermute | solution.py:348
  152.9 49.3 %collective-permute-start.11 = (f32[4,3,64,256]{3,2,1,0:T(8,128)S(1)}, f32[4,3,64,256]{3,2,1,0:T(8,128)}, u32[]{:S(2)}, u32[]{:S(2)}) collective-permute-start(f32[4,3,64,256]{3,2,1,0:T(8,128)S(1)} %copy-done.19), channel_id=1, source_target_pairs={{0,2},{1,3},{2,0},{3,1},{4,6},{5,7},{6,4},{7,5},{8,10},{9,11},{10,... | collective-permute-start | bytes 2359304 | tf_op jit(solution)/shard_map/ppermute | solution.py:349
  155.6 29.2 %copy-start.17 = (f32[3,256,256]{2,1,0:T(8,128)S(1)}, f32[3,256,256]{2,1,0:T(8,128)}, u32[]{:S(2)}) copy-start(f32[3,256,256]{2,1,0:T(8,128)} %get-tuple-element.62) | copy-start | bytes 2359300
  167.3 35.0 %collective-permute-start.17 = (f32[3,256,256]{2,1,0:T(8,128)S(1)}, f32[3,256,256]{2,1,0:T(8,128)S(1)}, u32[]{:S(2)}, u32[]{:S(2)}) collective-permute-start(f32[3,256,256]{2,1,0:T(8,128)S(1)} %add.37), channel_id=1, source_target_pairs={{8,16},{16,8},{9,17},{17,9},{10,18},{18,10},{11,19},{19,11},{12,20... | collective-permute-start | bytes 2359304 | tf_op jit(solution)/shard_map/ppermute | solution.py:500
  169.3 31.9 %copy-start.18 = (f32[3,256,256]{2,1,0:T(8,128)S(1)}, f32[3,256,256]{2,1,0:T(8,128)}, u32[]{:S(2)}) copy-start(f32[3,256,256]{2,1,0:T(8,128)} %get-tuple-element.58) | copy-start | bytes 2359300
  184.1 19.6 %collective-permute-start.14 = (f32[3,256,256]{2,1,0:T(8,128)S(1)}, f32[3,256,256]{2,1,0:T(8,128)S(1)}, u32[]{:S(2)}, u32[]{:S(2)}) collective-permute-start(f32[3,256,256]{2,1,0:T(8,128)S(1)} %add.35), channel_id=1, source_target_pairs={{8,16},{16,8},{9,17},{17,9},{10,18},{18,10},{11,19},{19,11},{12,20... | collective-permute-start | bytes 2359304 | tf_op jit(solution)/shard_map/ppermute | solution.py:500
  186.1 16.6 %copy-start.6 = (f32[3,256,256]{2,1,0:T(8,128)S(1)}, f32[3,256,256]{2,1,0:T(8,128)}, u32[]{:S(2)}) copy-start(f32[3,256,256]{2,1,0:T(8,128)} %get-tuple-element.53.refs_8_) | copy-start | bytes 2359300
  200.4 4.4 %collective-permute-start.23 = (f32[3,256,256]{2,1,0:T(8,128)S(1)}, f32[3,256,256]{2,1,0:T(8,128)S(1)}, u32[]{:S(2)}, u32[]{:S(2)}) collective-permute-start(f32[3,256,256]{2,1,0:T(8,128)S(1)} %add.41), channel_id=1, source_target_pairs={{8,16},{16,8},{9,17},{17,9},{10,18},{18,10},{11,19},{19,11},{12,20... | collective-permute-start | bytes 2359304 | tf_op jit(solution)/shard_map/ppermute | solution.py:500
  201.3 5.0 %collective-permute-start.20 = (f32[3,256,256]{2,1,0:T(8,128)S(1)}, f32[3,256,256]{2,1,0:T(8,128)S(1)}, u32[]{:S(2)}, u32[]{:S(2)}) collective-permute-start(f32[3,256,256]{2,1,0:T(8,128)S(1)} %add.39), channel_id=1, source_target_pairs={{8,16},{16,8},{9,17},{17,9},{10,18},{18,10},{11,19},{19,11},{12,20... | collective-permute-start | bytes 2359304 | tf_op jit(solution)/shard_map/ppermute | solution.py:500
  202.1 7.5 %collective-permute-start.10 = (f32[4,3,64,256]{3,2,1,0:T(8,128)S(1)}, f32[4,3,64,256]{3,2,1,0:T(8,128)S(1)}, u32[]{:S(2)}, u32[]{:S(2)}) collective-permute-start(f32[4,3,64,256]{3,2,1,0:T(8,128)S(1)} %copy-done.19), channel_id=1, source_target_pairs={{0,1},{1,0},{2,3},{3,2},{4,5},{5,4},{6,7},{7,6},{8,9},{9,8},{10,11... | collective-permute-start | bytes 2359304 | tf_op jit(solution)/shard_map/ppermute | solution.py:351
  202.2 8.7 %collective-permute-start.9 = (f32[2,3,128,256]{3,2,1,0:T(8,128)S(1)}, f32[2,3,128,256]{3,2,1,0:T(8,128)S(1)}, u32[]{:S(2)}, u32[]{:S(2)}) collective-permute-start(f32[2,3,128,256]{3,2,1,0:T(8,128)S(1)} %collective-permute-done.8.first_ref), channel_id=1, source_target_pairs={{0,1},{1,0},{2,3},{3,2},{4,5},{5,4},{6,7},{7,6},{8,9},{9,8},{10,11... | collective-permute-start | bytes 2359304 | tf_op jit(solution)/shard_map/ppermute | solution.py:350
  203.7 3.8 %copy-start.8 = (f32[3,256,256]{2,1,0:T(8,128)S(1)}, f32[3,256,256]{2,1,0:T(8,128)}, u32[]{:S(2)}) copy-start(f32[3,256,256]{2,1,0:T(8,128)} %get-tuple-element.61.refs_10_) | copy-start | bytes 2359300
  203.7 25.6 %collective-permute-start.12 = (f32[4,3,64,256]{3,2,1,0:T(8,128)}, f32[4,3,64,256]{3,2,1,0:T(8,128)}, u32[]{:S(2)}, u32[]{:S(2)}) collective-permute-start(f32[4,3,64,256]{3,2,1,0:T(8,128)} %collective-permute-done.11.b2_ref), channel_id=1, source_target_pairs={{0,1},{1,0},{2,3},{3,2},{4,5},{5,4},{6,7},{7,6},{8,9},{9,8},{10,11... | collective-permute-start | bytes 2359304 | tf_op jit(solution)/shard_map/ppermute | solution.py:352
  204.8 36.9 %collective-permute-start.18 = (f32[3,256,256]{2,1,0:T(8,128)}, f32[3,256,256]{2,1,0:T(8,128)S(1)}, u32[]{:S(2)}, u32[]{:S(2)}) collective-permute-start(f32[3,256,256]{2,1,0:T(8,128)} %add.38), channel_id=1, source_target_pairs={{8,0},{16,24},{9,1},{17,25},{10,2},{18,26},{11,3},{19,27},{12,4},{... | collective-permute-start | bytes 2359304 | tf_op jit(solution)/shard_map/ppermute | solution.py:501
  206.2 54.3 %collective-permute-start.15 = (f32[3,256,256]{2,1,0:T(8,128)}, f32[3,256,256]{2,1,0:T(8,128)S(1)}, u32[]{:S(2)}, u32[]{:S(2)}) collective-permute-start(f32[3,256,256]{2,1,0:T(8,128)} %add.36), channel_id=1, source_target_pairs={{8,0},{16,24},{9,1},{17,25},{10,2},{18,26},{11,3},{19,27},{12,4},{... | collective-permute-start | bytes 2359304 | tf_op jit(solution)/shard_map/ppermute | solution.py:501
  208.6 4.9 %copy-start.35 = (s32[64]{0:T(128)S(1)}, s32[64]{0:T(128)}, u32[]{:S(2)}) copy-start(s32[64]{0:T(128)} %param.10) | copy-start | bytes 772
  208.6 11.1 %copy-start.36 = (s32[128]{0:T(128)S(1)}, s32[128]{0:T(128)}, u32[]{:S(2)}) copy-start(s32[128]{0:T(128)} %param.11) | copy-start | bytes 1540
  209.6 67.8 %collective-permute-start.24 = (f32[3,256,256]{2,1,0:T(8,128)}, f32[3,256,256]{2,1,0:T(8,128)S(1)}, u32[]{:S(2)}, u32[]{:S(2)}) collective-permute-start(f32[3,256,256]{2,1,0:T(8,128)} %add.42), channel_id=1, source_target_pairs={{8,0},{16,24},{9,1},{17,25},{10,2},{18,26},{11,3},{19,27},{12,4},{... | collective-permute-start | bytes 2359304 | tf_op jit(solution)/shard_map/ppermute | solution.py:501
  211.0 81.3 %collective-permute-start.21 = (f32[3,256,256]{2,1,0:T(8,128)}, f32[3,256,256]{2,1,0:T(8,128)S(1)}, u32[]{:S(2)}, u32[]{:S(2)}) collective-permute-start(f32[3,256,256]{2,1,0:T(8,128)} %add.40), channel_id=1, source_target_pairs={{8,0},{16,24},{9,1},{17,25},{10,2},{18,26},{11,3},{19,27},{12,4},{... | collective-permute-start | bytes 2359304 | tf_op jit(solution)/shard_map/ppermute | solution.py:501
  241.7 18.9 %copy-start.11 = (f32[3,256,256]{2,1,0:T(8,128)}, f32[3,256,256]{2,1,0:T(8,128)S(1)}, u32[]{:S(2)}) copy-start(f32[3,256,256]{2,1,0:T(8,128)S(1)} %collective-permute-done.18.refs_9_) | copy-start | bytes 2359300
  277.4 14.9 %copy-start.13 = (f32[3,256,256]{2,1,0:T(8,128)}, f32[3,256,256]{2,1,0:T(8,128)S(1)}, u32[]{:S(2)}) copy-start(f32[3,256,256]{2,1,0:T(8,128)S(1)} %collective-permute-done.24.refs_11_) | copy-start | bytes 2359300
  326.9 37.6 %copy-start.4 = (f32[8,2,3,64,128]{4,3,2,1,0:T(8,128)}, f32[8,2,3,64,128]{4,3,2,1,0:T(8,128)S(1)}, u32[]{:S(2)}) copy-start(f32[8,2,3,64,128]{4,3,2,1,0:T(8,128)S(1)} %all_to_all.27.second_ref) | copy-start | bytes 4718596
  326.9 37.6 %collective-permute-start.25 = (f32[8,2,3,64,128]{4,3,2,1,0:T(8,128)S(1)}, f32[8,2,3,64,128]{4,3,2,1,0:T(8,128)S(1)}, u32[]{:S(2)}, u32[]{:S(2)}) collective-permute-start(f32[8,2,3,64,128]{4,3,2,1,0:T(8,128)S(1)} %all_to_all.27.second_ref), channel_id=1, source_target_pairs={{0,24},{1,25},{2,26},{3,27},{4,28},{5,29},{6,30},{7,31}} | collective-permute-start | bytes 4718600 | tf_op jit(solution)/shard_map/ppermute | solution.py:508
  365.8 7.2 %copy-start.1 = (s32[3,2]{0,1:T(2,128)S(1)}, s32[3,2]{0,1:T(2,128)}, u32[]{:S(2)}) copy-start(s32[3,2]{0,1:T(2,128)} %param.12) | copy-start | bytes 76
  (18 other events, 30.1 us)

commit v2 on v1

--- a/solution.py
+++ b/solution.py
@@ -27,59 +27,76 @@
     return lax.broadcasted_iota(jnp.int32, shape, dim)
 
 
-def planes_kernel(field_ref, planes_ref, west_ref, east_ref, south_ref, north_ref, turned):
+def edges_kernel(left_ref, right_ref, down_ref, up_ref, west_ref, east_ref, south_ref, north_ref, turned):
     comp = pl.program_id(0)
+    lane = iota((TILE_Y, TILE_X), 1)
+    for ref, which, out_ref in ((left_ref, 0, west_ref), (right_ref, 7, east_ref)):
+        turned[:, 0:8] = ref[0].T
+
+        @pl.when(comp == 0)
+        def _():
+            out_ref[...] = jnp.zeros_like(out_ref)
+
+        gathered = out_ref[...]
+        for z in range(CZ):
+            column = turned[pl.ds(z, TILE_Y, stride=CZ), :][:, which : which + 1]
+            gathered = jnp.where(lane == z * 3 + comp, column, gathered)
+        out_ref[...] = gathered
+    south_ref[0] = down_ref[0].T[0:CZ]
+    north_ref[0] = up_ref[0].T[TILE_X - CZ :]
+
+
+def tile_edges(field):
+    merged = field.shape[2]
+    edge = pl.BlockSpec((TILE_Y, TILE_X), lambda c: (0, 0))
+    side = pl.BlockSpec((1, CZ, TILE_X), lambda c: (c, 0, 0))
+    return pl.pallas_call(
+        edges_kernel,
+        grid=(3,),
+        in_specs=[
+            pl.BlockSpec((1, 8, merged), lambda c: (c, 0, 0)),
+            pl.BlockSpec((1, 8, merged), lambda c: (c, TILE_X // 8 - 1, 0)),
+            pl.BlockSpec((1, TILE_X, 128), lambda c: (c, 0, 0)),
+            pl.BlockSpec((1, TILE_X, 128), lambda c: (c, 0, merged // 128 - 1)),
+        ],
+        out_specs=[edge, edge, side, side],
+        out_shape=[jax.ShapeDtypeStruct((TILE_Y, TILE_X), f32)] * 2
+        + [jax.ShapeDtypeStruct((3, CZ, TILE_X), f32)] * 2,
+        scratch_shapes=[pltpu.VMEM((merged, 128), f32)],
+        compiler_params=params(),
+        name="tile_edges",
+    )(field, field, field, field)
+
+
+def planes_kernel(field_ref, planes_ref, turned):
     turned[...] = field_ref[0].T
-    lane = iota((TILE_Y, TILE_X), 1)
-
-    @pl.when(comp == 0)
-    def _():
-        west_ref[...] = jnp.zeros_like(west_ref)
-        east_ref[...] = jnp.zeros_like(east_ref)
-
-    west = west_ref[...]
-    east = east_ref[...]
     for z in range(CZ):
-        plane = turned[pl.ds(z, TILE_Y, stride=CZ), :]
-        planes_ref[z, 0] = plane
-        here = lane == z * 3 + comp
-        west = jnp.where(here, plane[:, 0:1], west)
-        east = jnp.where(here, plane[:, TILE_X - 1 :], east)
-        south_ref[0, pl.ds(z, 1), :] = plane[0:1, :]
-        north_ref[0, pl.ds(z, 1), :] = plane[TILE_Y - 1 :, :]
-    west_ref[...] = west
-    east_ref[...] = east
-
-
-def to_planes(field):
-    whole = lambda c: (0, 0)
+        planes_ref[z, 0] = turned[pl.ds(z, TILE_Y, stride=CZ), :]
+
+
+def to_planes(field, waits):
+    count = len(waits)
+
+    def body(field_ref, *refs):
+        planes_kernel(field_ref, *refs[count:])
+
     return pl.pallas_call(
-        planes_kernel,
+        body,
         grid=(3,),
-        in_specs=[pl.BlockSpec((1, TILE_X, TILE_Y * CZ), lambda c: (c, 0, 0))],
-        out_specs=[
-            pl.BlockSpec((CZ, 1, TILE_Y, TILE_X), lambda c: (0, c, 0, 0)),
-            pl.BlockSpec((TILE_Y, TILE_X), whole),
-            pl.BlockSpec((TILE_Y, TILE_X), whole),
-            pl.BlockSpec((1, CZ, TILE_X), lambda c: (c, 0, 0)),
-            pl.BlockSpec((1, CZ, TILE_X), lambda c: (c, 0, 0)),
-        ],
-        out_shape=[
-            jax.ShapeDtypeStruct((CZ, 3, TILE_Y, TILE_X), f32),
-            jax.ShapeDtypeStruct((TILE_Y, TILE_X), f32),
-            jax.ShapeDtypeStruct((TILE_Y, TILE_X), f32),
-            jax.ShapeDtypeStruct((3, CZ, TILE_X), f32),
-            jax.ShapeDtypeStruct((3, CZ, TILE_X), f32),
-        ],
+        in_specs=[pl.BlockSpec((1, TILE_X, TILE_Y * CZ), lambda c: (c, 0, 0))]
+        + [pl.BlockSpec(memory_space=pl.ANY)] * count,
+        out_specs=pl.BlockSpec((CZ, 1, TILE_Y, TILE_X), lambda c: (0, c, 0, 0)),
+        out_shape=jax.ShapeDtypeStruct((CZ, 3, TILE_Y, TILE_X), f32),
         scratch_shapes=[pltpu.VMEM((TILE_Y * CZ, TILE_X), f32)],
         compiler_params=params(),
         name="to_planes",
-    )(field)
-
-
-def flow_kernel(per, last, flag_ref, u_ref, xlo_ref, xhi_ref, ylo_ref, yhi_ref, *outs):
-    lamb_refs = outs[:CHUNKS]
-    next_ref = outs[CHUNKS]
+    )(field, *waits)
+
+
+def flow_kernel(per, want, flag_ref, u_ref, xlo_ref, xhi_ref, ylo_ref, yhi_ref, *outs):
+    outs = list(outs)
+    lamb_ref = outs.pop(0) if "lamb" in want else None
+    next_ref = outs.pop(0) if "next" in want else None
     group = pl.program_id(0)
     acoustic = flag_ref[0] > 0
     lane = iota((TILE_Y, TILE_X), 1)
@@ -87,8 +104,8 @@
     turn = lax.rem(TILE_X - group * (per * 3), TILE_X)
     xlo = pltpu.roll(xlo_ref[...], turn, 1)
     xhi = pltpu.roll(xhi_ref[...], turn, 1)
-    if not last:
-        west_ref, east_ref, south_ref, north_ref = outs[CHUNKS + 1 :]
+    if "edges" in want:
+        west_ref, east_ref, south_ref, north_ref = outs
 
         @pl.when(group == 0)
         def _():
@@ -129,39 +146,47 @@
             ox * centre[1] - oy * centre[0],
         )
         for c in range(3):
-            moved = centre[c] + time_step * (viscosity * lap[c] - lamb[c])
-            next_ref[i, c] = moved
-            sent = lamb[c] if last else jnp.where(acoustic, centre[c], lamb[c])
-            lamb_refs[i % CHUNKS][0, i // CHUNKS, c] = sent
-            if not last:
+            if "lamb" in want:
+                sent = jnp.where(acoustic, centre[c], lamb[c]) if "passed" in want else lamb[c]
+                lamb_ref[0, i // CHUNKS, i % CHUNKS, c] = sent
+            if "next" in want:
+                moved = centre[c] + time_step * (viscosity * lap[c] - lamb[c])
+                next_ref[i, c] = moved
+            if "edges" in want:
                 here = lane == z * 3 + c
                 west = jnp.where(here, moved[:, 0:1], west)
                 east = jnp.where(here, moved[:, TILE_X - 1 :], east)
                 south_ref[c, pl.ds(z, 1), :] = moved[0:1, :]
                 north_ref[c, pl.ds(z, 1), :] = moved[TILE_Y - 1 :, :]
-    if not last:
+    if "edges" in want:
         west_ref[...] = west
         east_ref[...] = east
 
 
-def flow(flag, planes, halo, groups, last):
+def flow(flag, planes, halo, waits, groups, want):
     per = CZ // groups
     halves = per // CHUNKS
     edge = pl.BlockSpec((TILE_Y, TILE_X), lambda g: (0, 0))
     side = pl.BlockSpec((3, CZ, TILE_X), lambda g: (0, 0, 0))
-    out_specs = [
-        pl.BlockSpec((1, halves, 3, TILE_Y, TILE_X), lambda g: (g, 0, 0, 0, 0))
-    ] * CHUNKS + [pl.BlockSpec((per, 3, TILE_Y, TILE_X), lambda g: (g, 0, 0, 0))]
-    out_shape = [
-        jax.ShapeDtypeStruct((groups, halves, 3, TILE_Y, TILE_X), f32)
-    ] * CHUNKS + [jax.ShapeDtypeStruct((CZ, 3, TILE_Y, TILE_X), f32)]
-    if not last:
+    out_specs, out_shape = [], []
+    if "lamb" in want:
+        out_specs.append(
+            pl.BlockSpec((1, halves, CHUNKS, 3, TILE_Y, TILE_X), lambda g: (g, 0, 0, 0, 0, 0))
+        )
+        out_shape.append(
+            jax.ShapeDtypeStruct((groups, halves, CHUNKS, 3, TILE_Y, TILE_X), f32)
+        )
+    if "next" in want:
+        out_specs.append(pl.BlockSpec((per, 3, TILE_Y, TILE_X), lambda g: (g, 0, 0, 0)))
+        out_shape.append(jax.ShapeDtypeStruct((CZ, 3, TILE_Y, TILE_X), f32))
+    if "edges" in want:
         out_specs += [edge, edge, side, side]
         out_shape += [jax.ShapeDtypeStruct((TILE_Y, TILE_X), f32)] * 2
         out_shape += [jax.ShapeDtypeStruct((3, CZ, TILE_X), f32)] * 2
+    count = len(waits)
 
     def body(*refs):
-        flow_kernel(per, last, *refs)
+        flow_kernel(per, want, *refs[:6], *refs[6 + count :])
 
     return pl.pallas_call(
         body,
@@ -173,12 +198,13 @@
             edge,
             side,
             side,
-        ],
+        ]
+        + [pl.BlockSpec(memory_space=pl.ANY)] * count,
         out_specs=out_specs,
         out_shape=out_shape,
         compiler_params=params(),
         name="flow",
-    )(flag, planes, *halo)
+    )(flag, planes, *halo, *waits)
 
 
 def exchange(west, east, south, north):
@@ -205,7 +231,7 @@
     row = iota((full_y, TILE_X), 0)
 
     def tile(h, j, a):
-        return jnp.concatenate([got_ref[a * gy + b, h, j] for b in range(gy)], axis=0)
+        return jnp.concatenate([got_ref[a * gy + b, h, 0, j] for b in range(gy)], axis=0)
 
     def work(h, out_ref):
         for a in range(gx):
@@ -260,25 +286,47 @@
         work(1 - low, near_ref)
 
 
-def place(ints, matrix, got, gx, gy, first):
+def place(ints, matrix, got, chunk, waits, gx, gy, first):
     shape = (3, gy * TILE_Y, gx * TILE_X)
+    count = len(waits)
 
     def body(*refs):
-        place_kernel(gx, gy, first, *refs)
-
+        place_kernel(gx, gy, first, *refs[:3], *refs[3 + count :])
+
+    block = got.shape[:2] + (1,) + got.shape[3:]
     return pl.pallas_call(
         body,
+        grid=(1,),
         in_specs=[
             pl.BlockSpec(memory_space=pltpu.SMEM),
             pl.BlockSpec(memory_space=pltpu.SMEM),
-            pl.BlockSpec(memory_space=pltpu.VMEM),
-        ],
-        out_specs=[pl.BlockSpec(memory_space=pltpu.VMEM)] * 2,
+            pl.BlockSpec(block, lambda i: (0, 0, chunk, 0, 0, 0)),
+        ]
+        + [pl.BlockSpec(memory_space=pl.ANY)] * count,
+        out_specs=[pl.BlockSpec(shape, lambda i: (0, 0, 0))] * 2,
         out_shape=[jax.ShapeDtypeStruct(shape, f32)] * 2,
         scratch_shapes=[pltpu.VMEM((TILE_Y * (gy + 1) + 8, gx * TILE_X), f32)],
         compiler_params=params(),
         name="place",
-    )(ints, matrix, got)
+    )(ints, matrix, got, *waits)
+
+
+def tie_kernel(*refs):
+    pass
+
+
+def after(value, earlier):
+    anywhere = pl.BlockSpec(memory_space=pl.ANY)
+    if not earlier:
+        return value
+    return pl.pallas_call(
+        tie_kernel,
+        in_specs=[anywhere] * (1 + len(earlier)),
+        out_specs=anywhere,
+        out_shape=jax.ShapeDtypeStruct(value.shape, value.dtype),
+        input_output_aliases={0: 0},
+        name="after",
+    )(value, *earlier)
 
 
 def split(value):
@@ -336,74 +384,85 @@
     )(pos, *blocks)
 
 
-def gathered_ops(x_ops, y_ops):
-    place_x = lax.axis_index("gx")
-    place_y = lax.axis_index("gy")
-    core = lax.rem(place_y, 2)
+def fetched_ops(x_ops, y_ops):
+    core = lax.rem(lax.axis_index("gy"), 2)
     half = NCLASS // 2
-    swap_x = [(0, 1), (1, 0)]
+    piece = lax.dynamic_slice_in_dim(x_ops, core * half, half, 0)
+    got_x = lax.ppermute(piece, "gx", [(0, 1), (1, 0)])
+    got_y = lax.ppermute(y_ops, "gy", [(i, i ^ 2) for i in range(4)])
+    return got_x, got_y
+
+
+def prepared_ops(x_ops, y_ops, fetched):
+    got_x, got_y = fetched
     beside = [(i, i ^ 1) for i in range(4)]
-    across = [(i, i ^ 2) for i in range(4)]
-    piece = lax.dynamic_slice_in_dim(x_ops, core * half, half, 0)
-    got_x = lax.ppermute(piece, "gx", swap_x)
-    got_y = lax.ppermute(y_ops, "gy", across)
     pair_x = lax.ppermute(got_x, "gy", beside)
     pair_y = lax.ppermute(y_ops, "gy", beside)
     cross_y = lax.ppermute(got_y, "gy", beside)
-    pos = jnp.stack([place_x, core, place_y]).astype(jnp.int32)
-    length = x_ops.shape[3]
-    x_parts = prepare_ops(x_ops_kernel, pos, (x_ops, got_x, pair_x), length, "x_operators")
+    place_y = lax.axis_index("gy")
+    pos = jnp.stack([lax.axis_index("gx"), lax.rem(place_y, 2), place_y]).astype(jnp.int32)
+    x_parts = prepare_ops(
+        x_ops_kernel, pos, (x_ops, got_x, pair_x), x_ops.shape[3], "x_operators"
+    )
     y_parts = prepare_ops(
         y_ops_kernel, pos, (y_ops, pair_y, got_y, cross_y), y_ops.shape[3], "y_operators"
     )
     return x_parts, y_parts
 
 
-def sweep_kernel(
-    gx, gy, count, last, xclass_ref, yclass_ref, xh_ref, xl_ref, yh_ref, yl_ref, *refs
-):
-    ins = refs[: CHUNKS * count]
-    outs = refs[CHUNKS * count :]
+def gathered_classes(x_line_class, y_line_class):
+    def rows(value, axis):
+        count = lax.axis_size(axis)
+        blocks = [value] + [
+            lax.ppermute(value, axis, [(i, i ^ step) for i in range(count)])
+            for step in range(1, count)
+        ]
+        order = jnp.arange(count) ^ lax.axis_index(axis)
+        return jnp.take(jnp.stack(blocks), order, axis=0)
+
+    return rows(x_line_class, "gy").reshape(-1, 1), rows(y_line_class, "gx").reshape(1, -1)
+
+
+def sweep_kernel(gx, gy, count, last, xclass_ref, yclass_ref, xh_ref, xl_ref, yh_ref, yl_ref, *refs):
+    ins = refs[:count]
+    out_ref = refs[count]
     xclass = xclass_ref[...]
     yclass = yclass_ref[...]
-    for chunk in range(CHUNKS):
-        state = ins[chunk * count][0]
-        for extra in ins[chunk * count + 1 : (chunk + 1) * count]:
-            state = state + extra[0]
-        high, low = split(state)
-        swept = jnp.zeros(state.shape, f32)
-        for cls in range(NCLASS):
-            part = dot(high, xh_ref[cls, 0]) + dot(low, xh_ref[cls, 0]) + dot(high, xl_ref[cls, 0])
-            swept = jnp.where(xclass == cls, part, swept)
-        high, low = split(swept)
-        final = jnp.zeros(state.shape, f32)
-        for cls in range(NCLASS):
-            part = dot(yh_ref[cls, 0], high) + dot(yh_ref[cls, 0], low) + dot(yl_ref[cls, 0], high)
-            final = jnp.where(yclass == cls, part, final)
-        if last:
-            for a in range(gx):
-                for b in range(gy):
-                    outs[0][a * gy + b, chunk, 0] = final[
-                        b * TILE_Y : (b + 1) * TILE_Y, a * TILE_X : (a + 1) * TILE_X
-                    ]
-        else:
-            outs[chunk][0] = final
+    state = ins[0][0]
+    for extra in ins[1:]:
+        state = state + extra[0]
+    high, low = split(state)
+    swept = jnp.zeros(state.shape, f32)
+    for cls in range(NCLASS):
+        part = dot(high, xh_ref[cls, 0]) + dot(low, xh_ref[cls, 0]) + dot(high, xl_ref[cls, 0])
+        swept = jnp.where(xclass == cls, part, swept)
+    high, low = split(swept)
+    final = jnp.zeros(state.shape, f32)
+    for cls in range(NCLASS):
+        part = dot(yh_ref[cls, 0], high) + dot(yh_ref[cls, 0], low) + dot(yl_ref[cls, 0], high)
+        final = jnp.where(yclass == cls, part, final)
+    if last:
+        for a in range(gx):
+            for b in range(gy):
+                out_ref[a * gy + b, 0] = final[
+                    b * TILE_Y : (b + 1) * TILE_Y, a * TILE_X : (a + 1) * TILE_X
+                ]
+    else:
+        out_ref[0] = final
 
 
 def sweep(classes, x_parts, y_parts, terms, gx, gy, last):
     full_y, full_x = gy * TILE_Y, gx * TILE_X
-    count = len(terms[0])
+    count = len(terms)
     field = pl.BlockSpec((1, full_y, full_x), lambda k: (k, 0, 0))
     xop = pl.BlockSpec((NCLASS, 1, full_x, full_x), lambda k: (0, k, 0, 0))
     yop = pl.BlockSpec((NCLASS, 1, full_y, full_y), lambda k: (0, k, 0, 0))
     if last:
-        out_specs = pl.BlockSpec(
-            (gx * gy, CHUNKS, 1, TILE_Y, TILE_X), lambda k: (0, 0, k, 0, 0)
-        )
-        out_shape = jax.ShapeDtypeStruct((gx * gy, CHUNKS, 3, TILE_Y, TILE_X), f32)
+        out_specs = pl.BlockSpec((gx * gy, 1, TILE_Y, TILE_X), lambda k: (0, k, 0, 0))
+        out_shape = jax.ShapeDtypeStruct((gx * gy, 3, TILE_Y, TILE_X), f32)
     else:
-        out_specs = [field] * CHUNKS
-        out_shape = [jax.ShapeDtypeStruct((3, full_y, full_x), f32)] * CHUNKS
+        out_specs = field
+        out_shape = jax.ShapeDtypeStruct((3, full_y, full_x), f32)
 
     def body(*refs):
         sweep_kernel(gx, gy, count, last, *refs)
@@ -419,18 +478,18 @@
             yop,
             yop,
         ]
-        + [field] * (CHUNKS * count),
+        + [field] * count,
         out_specs=out_specs,
         out_shape=out_shape,
         compiler_params=params(),
         name="sweep",
-    )(*classes, *x_parts, *y_parts, *[t for chunk in terms for t in chunk])
-
-
-def output_kernel(flag_ref, u_ref, first_ref, second_ref, out_ref, turned):
-    groups = first_ref.shape[0]
-    per = CZ // groups
-    half = per // 2
+    )(*classes, *x_parts, *y_parts, *terms)
+
+
+def output_kernel(flag_ref, u_ref, *refs):
+    parts = refs[: 2 * CHUNKS]
+    out_ref, turned = refs[2 * CHUNKS :]
+    per = CZ // parts[0].shape[0]
 
     @pl.when(flag_ref[0] == 0)
     def _():
@@ -441,29 +500,27 @@
     def _():
         for z in range(CZ):
             g, i = divmod(z, per)
-            ref = first_ref if i < half else second_ref
-            turned[pl.ds(z, TILE_Y, stride=CZ), :] = ref[g, i % half, 0]
+            turned[pl.ds(z, TILE_Y, stride=CZ), :] = parts[i][g, 0]
 
     out_ref[0, 0] = turned[...].T
 
 
-def to_output(flag, planes, first, second):
-    part = pl.BlockSpec(first.shape[:2] + (1, TILE_Y, TILE_X), lambda c: (0, 0, c, 0, 0))
+def to_output(flag, planes, parts):
+    part = pl.BlockSpec(parts[0].shape[:1] + (1, TILE_Y, TILE_X), lambda c: (0, c, 0, 0))
     return pl.pallas_call(
         output_kernel,
         grid=(3,),
         in_specs=[
             pl.BlockSpec(memory_space=pltpu.SMEM),
             pl.BlockSpec((CZ, 1, TILE_Y, TILE_X), lambda c: (0, c, 0, 0)),
-            part,
-            part,
-        ],
+        ]
+        + [part] * (2 * CHUNKS),
         out_specs=pl.BlockSpec((1, 1, TILE_X, TILE_Y * CZ), lambda c: (0, c, 0, 0)),
         out_shape=jax.ShapeDtypeStruct((1, 3, TILE_X, TILE_Y * CZ), f32),
         scratch_shapes=[pltpu.VMEM((TILE_Y * CZ, TILE_X), f32)],
         compiler_params=params(),
         name="to_output",
-    )(flag, planes, first, second)
+    )(flag, planes, *parts)
 
 
 def local(fields, x_ops, y_ops, x_line_class, y_line_class, box_offset, coupling):
@@ -479,34 +536,60 @@
     lower = (sec < 2).astype(jnp.int32)
     ints = jnp.stack([active, lower, offsets[0], offsets[1]])
 
-    planes, *edges = to_planes(fields[0])
+    halo = exchange(*tile_edges(fields[0]))
+    fetched = fetched_ops(x_ops, y_ops)
+    classes = gathered_classes(x_line_class, y_line_class)
+    planes = to_planes(fields[0], ())
+
+    waits = (*fetched, *classes)
+    (lamb,) = flow(flag, planes, halo, waits, groups, ("lamb", "passed"))
+    gots = [lax.all_to_all(lamb, ("gx", "gy"), 0, 0)]
+    planes, *edges = flow(flag, planes, halo, (lamb,), groups, ("next", "edges"))
     halo = exchange(*edges)
-    x_parts, y_parts = gathered_ops(x_ops, y_ops)
-    xclass = lax.all_gather(x_line_class, "gy", axis=0, tiled=True).reshape(-1, 1)
-    yclass = lax.all_gather(y_line_class, "gx", axis=0, tiled=True).reshape(1, -1)
-
-    acoustic = None
-    for repeat in range(STEPS):
-        last = repeat == STEPS - 1
-        outs = flow(flag, planes, halo, groups, last)
-        planes = outs[CHUNKS]
-        if not last:
-            halo = exchange(*outs[CHUNKS + 1 :])
-        terms = []
-        for chunk in range(CHUNKS):
-            got = lax.all_to_all(outs[chunk], ("gx", "gy"), 0, 0)
-            far, near = place(ints, matrix, got, gx, gy, repeat == 0)
-            passed = lax.ppermute(far, "sec", [(0, 1), (3, 2)] if repeat == 0 else [(0, 1)])
-            passed = lax.ppermute(far + passed, "sec", [(1, 2), (2, 1)])
-            passed = lax.ppermute(near + passed, "sec", [(1, 0), (2, 3)])
-            term = (near, passed)
-            if acoustic is not None:
-                term = (acoustic[chunk],) + term
-            terms.append(term)
-        acoustic = sweep((xclass, yclass), x_parts, y_parts, terms, gx, gy, last)
-    tiles = lax.all_to_all(acoustic, ("gx", "gy"), 0, 0)
-    brought = lax.ppermute(tiles, "sec", [(0, 3)])
-    return to_output(flag, planes, brought, tiles)
+    fetched = [after(value, [planes]) for value in fetched]
+    x_parts, y_parts = prepared_ops(x_ops, y_ops, fetched)
+    lamb, planes = flow(flag, planes, halo, (*x_parts, *y_parts), groups, ("lamb", "next"))
+    gots[0] = after(gots[0], [lamb])
+    gots.append(lax.all_to_all(after(lamb, [gots[0]]), ("gx", "gy"), 0, 0))
+
+    total = STEPS * CHUNKS
+    fars, nears, firsts, seconds, thirds, ends = ([None] * total for _ in range(6))
+    token = []
+
+    def placed(n):
+        first = n < CHUNKS
+        got = gots[n // CHUNKS]
+        fars[n], nears[n] = place(ints, matrix, got, n % CHUNKS, token, gx, gy, first)
+        firsts[n] = lax.ppermute(fars[n], "sec", [(0, 1), (3, 2)] if first else [(0, 1)])
+        return fars[n]
+
+    def first_hop(n):
+        value = fars[n] + after(firsts[n], token)
+        seconds[n] = lax.ppermute(value, "sec", [(1, 2), (2, 1)])
+        return value
+
+    def second_hop(n):
+        value = nears[n] + after(seconds[n], token)
+        thirds[n] = lax.ppermute(value, "sec", [(1, 0), (2, 3)])
+        return value
+
+    def swept(n):
+        terms = (nears[n], after(thirds[n], token))
+        if n >= CHUNKS:
+            terms += (ends[n - CHUNKS],)
+        ends[n] = sweep(classes, x_parts, y_parts, terms, gx, gy, n >= total - CHUNKS)
+        return ends[n]
+
+    order = (
+        (placed, 0), (placed, 1), (first_hop, 0), (first_hop, 1), (second_hop, 0),
+        (placed, 2), (placed, 3), (second_hop, 1), (first_hop, 2), (swept, 0),
+        (first_hop, 3), (second_hop, 2), (swept, 1), (second_hop, 3), (swept, 2), (swept, 3),
+    )
+    for work, n in order:
+        token = [work(n)]
+    tiles = [lax.all_to_all(value, ("gx", "gy"), 0, 0) for value in ends[-CHUNKS:]]
+    brought = [lax.ppermute(value, "sec", [(0, 3)]) for value in tiles]
+    return to_output(flag, planes, brought + tiles)
 
 
 highest = lax.Precision.HIGHEST

time: 374 us -> 302 us (0.81)
  blocking collectives: 87.9 us -> 0 us
  waiting for transfers between devices: 135 us -> 79.8 us
  starting transfers between devices: 52.1 us -> 83.3 us
  Pallas kernels: 77 us -> 99.6 us
  other arithmetic: 11.8 us -> 21.8 us
  local copies, waits for them, and re-layouts: 7.76 us -> 15.2 us
    all_to_all x3 -> x0, blocking collectives: 78.7 us -> none  [the longest x2 54.2 us: local(): got = lax.all_to_all(outs[chunk], ('gx', 'gy'), 0, 0)]
    ppermute x18 -> x23, waiting for transfers between devices: 122 us -> 66 us  [the longest x4 30.2 us: placed(): lax.ppermute(fars[n], 'sec', [(0, 1), (3, 2)] if first else [(0, 1)])]
    ppermute x18 -> x23, starting transfers between devices: 27.2 us -> 50.3 us  [the longest x4 19.4 us: placed(): lax.ppermute(fars[n], 'sec', [(0, 1), (3, 2)] if first else [(0, 1)])]
    all_to_all x2 -> x4, starting transfers between devices: 7.31 us -> 17.2 us  [the longest x2 7.28 us: local(): lax.all_to_all(value, ('gx', 'gy'), 0, 0)]
    add x8, other arithmetic: 8.01 us -> 17.2 us  [the longest x4 9.24 us: first_hop(): value = fars[n] + after(firsts[n], token)]
    pallas_call x2 -> x4, Pallas kernels: 18.2 us -> 26.3 us  [sweep(): pl.pallas_call(body, grid=(3,), in_specs=[pl.BlockSpec((full_y, 1), lambd...]
    pallas_call x5 -> x22, Pallas kernels: 21 us -> 28.3 us  [the longest x4 14.3 us: place(): pl.pallas_call(body, grid=(1,), in_specs=[pl.BlockSpec(memory_space=pltpu...]
    pallas_call x2 -> x3, Pallas kernels: 21.3 us -> 28.4 us  [flow(): pl.pallas_call(body, grid=(groups,), in_specs=[pl.BlockSpec(memory_space=...]
  transfers between devices with their start and end apart: 28 -> 35, of which waited for: 12 -> 11; matrix products, arithmetic and copies ran while one was open for 4% -> 9% of each run, Pallas kernels for 11% -> 28%
where the time goes in v2:
time: 302 us; the launch traced here: 300 us
  Pallas kernels  99.6 us (33%)
  starting transfers between devices  83.3 us (28%)
  waiting for transfers between devices  79.8 us (26%)
  other arithmetic  21.8 us (7%)
  local copies, waits for them, and re-layouts  15.2 us (5%)
    ppermute x4, waiting for transfers between devices, placed(): lax.ppermute(fars[n], 'sec', [(0, 1), (3, 2)] if first else [(0, 1)])  30.2 us
    pallas_call x3, Pallas kernels, flow(): pl.pallas_call(body, grid=(groups,), in_specs=[pl.BlockSpec(memory_space=...  28.4 us
    pallas_call x4, Pallas kernels, sweep(): pl.pallas_call(body, grid=(3,), in_specs=[pl.BlockSpec((full_y, 1), lambd...  26.3 us
    ppermute x2, waiting for transfers between devices, local(): brought = [lax.ppermute(value, 'sec', [(0, 3)]) for value in tiles]  21.6 us
    ppermute x4, starting transfers between devices, placed(): lax.ppermute(fars[n], 'sec', [(0, 1), (3, 2)] if first else [(0, 1)])  19.4 us
    ppermute x8, starting transfers between devices, send(): lax.ppermute(value, axis, [(i, i + step) for i in range(count) if 0 <= i...  15.7 us
    pallas_call x4, Pallas kernels, place(): pl.pallas_call(body, grid=(1,), in_specs=[pl.BlockSpec(memory_space=pltpu...  14.3 us
    ppermute x4, waiting for transfers between devices, second_hop(): thirds[n] = lax.ppermute(value, 'sec', [(1, 0), (2, 3)])  14.1 us
  transfers between devices with their start and end apart: 35, of which 11 were waited for; matrix products, arithmetic and copies ran while one was open for 9% of the time, Pallas kernels for 28%

profile of v2, /device:TPU:0, one launch (start us, length us, event | category | flops | bytes accessed | tf_op | source)
XLA Modules:
  0.0 300.2 jit_solution(17534021567200266548)
XLA Ops:
  0.5 2.6 collective-permute-start.8
  4.3 2.1 collective-permute-start.4
  7.9 8.6 %tile_edges.1 = (f32[64,128]{1,0:T(8,128)}, f32[64,128]{1,0:T(8,128)}, f32[3,32,128]{2,1,0:T(8,128)}, f32[3,32,128]{2,1,0:T(8,128)}) custom-call(f32[3,128,2048]{2,1,0:T(8,128)} %bitcast.21, f32[3,128,2048]{2,1,0:T(8,128)} %bitcast.22, f32[3,128,2048]{2,1,0:T(8,128)} %bitcast.23, f32[3,128,2048]{2,1,0:T(8,128)} %bitcast.24), custom_call_target="tpu_custom_call" | custom-call | tf_op jit(solution)/shard_map/tile_edges/pallas_call | solution.py:53
  16.6 5.5 %to_planes.1.refs_1_ = f32[32,3,64,128]{3,2,1,0:T(8,128)} custom-call(f32[3,128,2048]{2,1,0:T(8,128)} %bitcast.25), custom_call_target="tpu_custom_call" | custom-call | tf_op jit(solution)/shard_map/to_planes/pallas_call | solution.py:83
  22.6 3.4 %collective-permute-start = (f32[64,128]{1,0:T(8,128)S(1)}, f32[64,128]{1,0:T(8,128)S(1)}, u32[]{:S(2)}, u32[]{:S(2)}) collective-permute-start(f32[64,128]{1,0:T(8,128)S(1)} %copy-done.39), channel_id=1, source_target_pairs={{0,4},{1,5},{2,6},{3,7},{8,12},{9,13},{10,14},{11,15},{16,20},{17,... | collective-permute-start | bytes 98312 | tf_op jit(solution)/shard_map/ppermute | solution.py:213
  32.7 1.9 collective-permute-done.3.refs_5_
  35.8 7.1 %flow.3.refs_6_ = f32[8,2,2,3,64,128]{5,4,3,2,1,0:T(8,128)} custom-call(s32[1]{0:T(128)} %bitcast.refs_0_.flag_ref, f32[32,3,64,128]{3,2,1,0:T(8,128)} %to_planes.1.refs_1_, f32[64,128]{1,0:T(8,128)} %copy-done.24, f32[64,128]{1,0:T(8,128)} %copy-done.25, f32[3,32,128]{2,1,0:T(8,128)} %copy-done.22, f32[3,32,128]{2,1,0:T(8,128)} %copy-done.23, ...), custom_call_target="tpu_custom_call" | custom-call | tf_op jit(solution)/shard_map/flow/pallas_call | solution.py:191
  42.9 6.3 %all-to-all-start = ((f32[8,2,2,3,64,128]{5,4,3,2,1,0:T(8,128)}), f32[8,2,2,3,64,128]{5,4,3,2,1,0:T(8,128)S(1)}, u32[]{:S(2)}, u32[]{:S(2)}) async-start(f32[8,2,2,3,64,128]{5,4,3,2,1,0:T(8,128)} %flow.3.refs_6_), calls=%async_computation | async-start | bytes 6291456 | tf_op jit(solution)/shard_map/all_to_all | solution.py:546
  49.7 12.6 %flow.4 = (f32[32,3,64,128]{3,2,1,0:T(8,128)}, f32[64,128]{1,0:T(8,128)}, f32[64,128]{1,0:T(8,128)}, f32[3,32,128]{2,1,0:T(8,128)}, f32[3,32,128]{2,1,0:T(8,128)}) custom-call(s32[1]{0:T(128)} %bitcast.refs_0_.flag_ref, f32[32,3,64,128]{3,2,1,0:T(8,128)} %to_planes.1.refs_1_, f32[64,128]{1,0:T(8,128)} %copy-done.24, f32[64,128]{1,0:T(8,128)} %copy-done.25, ...), custom_call_target="tpu_custom_call" | custom-call | tf_op jit(solution)/shard_map/flow/pallas_call | solution.py:191
  63.1 4.2 %collective-permute-start.10 = (f32[64,128]{1,0:T(8,128)S(1)}, f32[64,128]{1,0:T(8,128)S(1)}, u32[]{:S(2)}, u32[]{:S(2)}) collective-permute-start(f32[64,128]{1,0:T(8,128)S(1)} %copy-done.38), channel_id=1, source_target_pairs={{0,4},{1,5},{2,6},{3,7},{8,12},{9,13},{10,14},{11,15},{16,20},{17,... | collective-permute-start | bytes 98312 | tf_op jit(solution)/shard_map/ppermute | solution.py:213
  72.2 4.9 %x_operators.1 = (bf16[4,3,256,256]{3,2,1,0:T(8,128)(2,1)}, bf16[4,3,256,256]{3,2,1,0:T(8,128)(2,1)}) custom-call(s32[3]{0:T(128)} %pad_add_fusion.2.pos_ref, f32[4,3,128,256]{3,2,1,0:T(8,128)} %mine_ref.1, f32[2,3,128,256]{3,2,1,0:T(8,128)} %after.16.first_ref, f32[2,3,128,256]{3,2,1,0:T(8,128)} %collective-permute-done.14.second_ref), custom_call_target="tpu_custom_call" | custom-call | tf_op jit(solution)/shard_map/x_operators/pallas_call | solution.py:376
  78.0 4.4 %y_operators.1 = (bf16[4,3,256,256]{3,2,1,0:T(8,128)(2,1)}, bf16[4,3,256,256]{3,2,1,0:T(8,128)(2,1)}) custom-call(s32[3]{0:T(128)} %pad_add_fusion.2.pos_ref, f32[4,3,64,256]{3,2,1,0:T(8,128)} %b0_ref.1, f32[4,3,64,256]{3,2,1,0:T(8,128)} %collective-permute-done.15.b1_ref, f32[4,3,64,256]{3,2,1,0:T(8,128)} %after.17.b2_ref, f32[4,3,64,256]{3,2,1,0:T(8,128)} %copy-done.21), custom_call_target="tpu_custom_call" | custom-call | tf_op jit(solution)/shard_map/y_operators/pallas_call | solution.py:376
  82.5 4.8 %collective-permute-done.11.refs_3_ = f32[64,128]{1,0:T(8,128)S(1)} collective-permute-done((f32[64,128]{1,0:T(8,128)S(1)}, f32[64,128]{1,0:T(8,128)S(1)}, u32[]{:S(2)}, u32[]{:S(2)}) %collective-permute-start.11) | collective-permute-done | bytes 32800 | tf_op jit(solution)/shard_map/ppermute | solution.py:213
  88.0 8.7 %flow.5 = (f32[8,2,2,3,64,128]{5,4,3,2,1,0:T(8,128)}, f32[32,3,64,128]{3,2,1,0:T(8,128)}) custom-call(s32[1]{0:T(128)} %bitcast.refs_0_.flag_ref, f32[32,3,64,128]{3,2,1,0:T(8,128)} %get-tuple-element.32.refs_1_, f32[64,128]{1,0:T(8,128)} %copy-done.28, f32[64,128]{1,0:T(8,128)} %copy-done.29, f32[3,32,128]{2,1,0:T(8,128)} %copy-done.26, ...), custom_call_target="tpu_custom_call" | custom-call | tf_op jit(solution)/shard_map/flow/pallas_call | solution.py:191
  98.3 3.7 %all-to-all-start.1 = ((f32[8,2,2,3,64,128]{5,4,3,2,1,0:T(8,128)}), f32[8,2,2,3,64,128]{5,4,3,2,1,0:T(8,128)S(1)}, u32[]{:S(2)}, u32[]{:S(2)}) async-start(f32[8,2,2,3,64,128]{5,4,3,2,1,0:T(8,128)} %after.19), calls=%async_computation.1 | async-start | bytes 6291456 | tf_op jit(solution)/shard_map/all_to_all | solution.py:553
  102.7 1.9 pad_add_fusion.3.refs_0_
  105.8 3.6 %place.4 = (f32[3,256,256]{2,1,0:T(8,128)}, f32[3,256,256]{2,1,0:T(8,128)}) custom-call(s32[4]{0:T(128)} %pad_add_fusion.3.refs_0_, f32[3,3]{1,0:T(4,128)} %select_bitcast_fusion.refs_1_, f32[8,2,2,3,64,128]{5,4,3,2,1,0:T(8,128)} %after.18.refs_1_.refs_2_), custom_call_target="tpu_custom_call" | custom-call | tf_op jit(solution)/shard_map/place/pallas_call | solution.py:297
  109.5 4.4 %collective-permute-start.17 = (f32[3,256,256]{2,1,0:T(8,128)}, f32[3,256,256]{2,1,0:T(8,128)}, u32[]{:S(2)}, u32[]{:S(2)}) collective-permute-start(f32[3,256,256]{2,1,0:T(8,128)} %get-tuple-element.44.refs_3_), channel_id=1, source_target_pairs={{0,8},{24,16},{1,9},{25,17},{2,10},{26,18},{3,11},{27,19},{4,12},{... | collective-permute-start | bytes 2359304 | tf_op jit(solution)/shard_map/ppermute | solution.py:563
  113.8 3.7 %place.5 = (f32[3,256,256]{2,1,0:T(8,128)}, f32[3,256,256]{2,1,0:T(8,128)}) custom-call(s32[4]{0:T(128)} %pad_add_fusion.3.refs_0_, f32[3,3]{1,0:T(4,128)} %select_bitcast_fusion.refs_1_, f32[8,2,2,3,64,128]{5,4,3,2,1,0:T(8,128)} %after.18.refs_1_.refs_2_, f32[3,256,256]{2,1,0:T(8,128)} %get-tuple-element.44.refs_3_), custom_call_target="tpu_custom_call" | custom-call | tf_op jit(solution)/shard_map/place/pallas_call | solution.py:297
  117.6 2.2 collective-permute-start.19
  119.8 11.4 %collective-permute-done.17.refs_0_ = f32[3,256,256]{2,1,0:T(8,128)} collective-permute-done((f32[3,256,256]{2,1,0:T(8,128)}, f32[3,256,256]{2,1,0:T(8,128)}, u32[]{:S(2)}, u32[]{:S(2)}) %collective-permute-start.17) | collective-permute-done | bytes 786464 | tf_op jit(solution)/shard_map/ppermute | solution.py:563
  131.1 2.3 add.69.refs_1_
  135.0 12.4 %collective-permute-done.19.refs_0_ = f32[3,256,256]{2,1,0:T(8,128)} collective-permute-done((f32[3,256,256]{2,1,0:T(8,128)}, f32[3,256,256]{2,1,0:T(8,128)}, u32[]{:S(2)}, u32[]{:S(2)}) %collective-permute-start.19) | collective-permute-done | bytes 786464 | tf_op jit(solution)/shard_map/ppermute | solution.py:563
  147.4 2.3 add.70.refs_1_
  151.3 2.3 add.71.refs_3_
  155.3 3.4 %place.6 = (f32[3,256,256]{2,1,0:T(8,128)}, f32[3,256,256]{2,1,0:T(8,128)}) custom-call(s32[4]{0:T(128)} %pad_add_fusion.3.refs_0_, f32[3,3]{1,0:T(4,128)} %select_bitcast_fusion.refs_1_, f32[8,2,2,3,64,128]{5,4,3,2,1,0:T(8,128)} %copy-done.3, f32[3,256,256]{2,1,0:T(8,128)} %add.71.refs_3_), custom_call_target="tpu_custom_call" | custom-call | tf_op jit(solution)/shard_map/place/pallas_call | solution.py:297
  158.8 7.3 %collective-permute-start.20 = (f32[3,256,256]{2,1,0:T(8,128)}, f32[3,256,256]{2,1,0:T(8,128)S(1)}, u32[]{:S(2)}, u32[]{:S(2)}) collective-permute-start(f32[3,256,256]{2,1,0:T(8,128)} %get-tuple-element.47.refs_3_), channel_id=1, source_target_pairs={{0,8},{1,9},{2,10},{3,11},{4,12},{5,13},{6,14},{7,15}} | collective-permute-start | bytes 2359304 | tf_op jit(solution)/shard_map/ppermute | solution.py:563
  167.6 3.5 %place.7 = (f32[3,256,256]{2,1,0:T(8,128)}, f32[3,256,256]{2,1,0:T(8,128)}) custom-call(s32[4]{0:T(128)} %pad_add_fusion.3.refs_0_, f32[3,3]{1,0:T(4,128)} %select_bitcast_fusion.refs_1_, f32[8,2,2,3,64,128]{5,4,3,2,1,0:T(8,128)} %copy-done.3, f32[3,256,256]{2,1,0:T(8,128)} %get-tuple-element.47.refs_3_), custom_call_target="tpu_custom_call" | custom-call | tf_op jit(solution)/shard_map/place/pallas_call | solution.py:297
  171.1 5.5 %collective-permute-start.23 = (f32[3,256,256]{2,1,0:T(8,128)}, f32[3,256,256]{2,1,0:T(8,128)}, u32[]{:S(2)}, u32[]{:S(2)}) collective-permute-start(f32[3,256,256]{2,1,0:T(8,128)} %get-tuple-element.49.refs_1_), channel_id=1, source_target_pairs={{0,8},{1,9},{2,10},{3,11},{4,12},{5,13},{6,14},{7,15}} | collective-permute-start | bytes 2359304 | tf_op jit(solution)/shard_map/ppermute | solution.py:563
  176.6 2.2 add.72.refs_1_
  178.7 5.6 %collective-permute-done.20.refs_0_ = f32[3,256,256]{2,1,0:T(8,128)S(1)} collective-permute-done((f32[3,256,256]{2,1,0:T(8,128)}, f32[3,256,256]{2,1,0:T(8,128)S(1)}, u32[]{:S(2)}, u32[]{:S(2)}) %collective-permute-start.20) | collective-permute-done | bytes 786464 | tf_op jit(solution)/shard_map/ppermute | solution.py:563
  185.3 2.3 add.73.refs_1_
  191.3 6.5 %sweep.4.refs_1_.refs_8_ = f32[3,256,256]{2,1,0:T(8,128)} custom-call(s32[256,1]{1,0:T(8,128)} %select_n.92.refs_8_.refs_0_, s32[1,256]{1,0:T(1,128)} %bitcast.27, bf16[4,3,256,256]{3,2,1,0:T(8,128)(2,1)} %get-tuple-element.37.refs_6_.refs_2_, bf16[4,3,256,256]{3,2,1,0:T(8,128)(2,1)} %get-tuple-element.38.refs_7_.refs_3_, ...), custom_call_target="tpu_custom_call" | custom-call | tf_op jit(solution)/shard_map/sweep/pallas_call | solution.py:470
  198.6 2.2 add.74.refs_1_
  202.4 2.2 add.75.refs_1_
  206.7 6.5 %sweep.5.refs_1_.refs_8_ = f32[3,256,256]{2,1,0:T(8,128)} custom-call(s32[256,1]{1,0:T(8,128)} %select_n.92.refs_8_.refs_0_, s32[1,256]{1,0:T(1,128)} %bitcast.28, bf16[4,3,256,256]{3,2,1,0:T(8,128)(2,1)} %get-tuple-element.37.refs_6_.refs_2_, bf16[4,3,256,256]{3,2,1,0:T(8,128)(2,1)} %get-tuple-element.38.refs_7_.refs_3_, ...), custom_call_target="tpu_custom_call" | custom-call | tf_op jit(solution)/shard_map/sweep/pallas_call | solution.py:470
  215.9 8.2 %collective-permute-done.25.refs_0_ = f32[3,256,256]{2,1,0:T(8,128)S(1)} collective-permute-done((f32[3,256,256]{2,1,0:T(8,128)}, f32[3,256,256]{2,1,0:T(8,128)S(1)}, u32[]{:S(2)}, u32[]{:S(2)}) %collective-permute-start.25) | collective-permute-done | bytes 786464 | tf_op jit(solution)/shard_map/ppermute | solution.py:573
  225.0 6.6 %sweep.6.refs_1_ = f32[8,3,64,128]{3,2,1,0:T(8,128)} custom-call(s32[256,1]{1,0:T(8,128)} %select_n.92.refs_8_.refs_0_, s32[1,256]{1,0:T(1,128)} %bitcast.29, bf16[4,3,256,256]{3,2,1,0:T(8,128)(2,1)} %get-tuple-element.37.refs_6_.refs_2_, bf16[4,3,256,256]{3,2,1,0:T(8,128)(2,1)} %get-tuple-element.38.refs_7_.refs_3_, ...), custom_call_target="tpu_custom_call" | custom-call | tf_op jit(solution)/shard_map/sweep/pallas_call | solution.py:470
  231.6 3.6 %all-to-all-start.2 = ((f32[8,3,64,128]{3,2,1,0:T(8,128)}), f32[8,3,64,128]{3,2,1,0:T(8,128)S(1)}, u32[]{:S(2)}, u32[]{:S(2)}) async-start(f32[8,3,64,128]{3,2,1,0:T(8,128)} %sweep.6.refs_1_), calls=%async_computation.2 | async-start | bytes 1572864 | tf_op jit(solution)/shard_map/all_to_all | solution.py:590
  235.3 5.9 %collective-permute-done.29.refs_0_ = f32[3,256,256]{2,1,0:T(8,128)S(1)} collective-permute-done((f32[3,256,256]{2,1,0:T(8,128)S(1)}, f32[3,256,256]{2,1,0:T(8,128)S(1)}, u32[]{:S(2)}, u32[]{:S(2)}) %collective-permute-start.29) | collective-permute-done | bytes 786464 | tf_op jit(solution)/shard_map/ppermute | solution.py:573
  242.1 6.6 %sweep.7 = f32[8,3,64,128]{3,2,1,0:T(8,128)} custom-call(s32[256,1]{1,0:T(8,128)} %select_n.92.refs_8_.refs_0_, s32[1,256]{1,0:T(1,128)} %bitcast.30, bf16[4,3,256,256]{3,2,1,0:T(8,128)(2,1)} %get-tuple-element.37.refs_6_.refs_2_, bf16[4,3,256,256]{3,2,1,0:T(8,128)(2,1)} %get-tuple-element.38.refs_7_.refs_3_, ...), custom_call_target="tpu_custom_call" | custom-call | tf_op jit(solution)/shard_map/sweep/pallas_call | solution.py:470
  248.7 3.6 %all-to-all-start.3 = ((f32[8,3,64,128]{3,2,1,0:T(8,128)}), f32[8,3,64,128]{3,2,1,0:T(8,128)S(1)}, u32[]{:S(2)}, u32[]{:S(2)}) async-start(f32[8,3,64,128]{3,2,1,0:T(8,128)} %sweep.7), calls=%async_computation.3 | async-start | bytes 1572864 | tf_op jit(solution)/shard_map/all_to_all | solution.py:590
  252.4 5.6 %collective-permute-start.28 = (f32[8,3,64,128]{3,2,1,0:T(8,128)S(1)}, f32[8,3,64,128]{3,2,1,0:T(8,128)S(1)}, u32[]{:S(2)}, u32[]{:S(2)}) collective-permute-start(f32[8,3,64,128]{3,2,1,0:T(8,128)S(1)} %all-to-all-done.2.refs_2_), channel_id=1, source_target_pairs={{0,24},{1,25},{2,26},{3,27},{4,28},{5,29},{6,30},{7,31}} | collective-permute-start | bytes 2359304 | tf_op jit(solution)/shard_map/ppermute | solution.py:591
  258.0 7.0 %all-to-all-done.3.refs_3_ = f32[8,3,64,128]{3,2,1,0:T(8,128)S(1)} async-done(((f32[8,3,64,128]{3,2,1,0:T(8,128)}), f32[8,3,64,128]{3,2,1,0:T(8,128)S(1)}, u32[]{:S(2)}, u32[]{:S(2)}) %all-to-all-start.3) | async-done | bytes 786464 | tf_op jit(solution)/shard_map/all_to_all | solution.py:590
  265.0 5.5 %collective-permute-start.30 = (f32[8,3,64,128]{3,2,1,0:T(8,128)S(1)}, f32[8,3,64,128]{3,2,1,0:T(8,128)S(1)}, u32[]{:S(2)}, u32[]{:S(2)}) collective-permute-start(f32[8,3,64,128]{3,2,1,0:T(8,128)S(1)} %all-to-all-done.3.refs_3_), channel_id=1, source_target_pairs={{0,24},{1,25},{2,26},{3,27},{4,28},{5,29},{6,30},{7,31}} | collective-permute-start | bytes 2359304 | tf_op jit(solution)/shard_map/ppermute | solution.py:591
  270.5 5.3 %collective-permute-done.28.refs_0_ = f32[8,3,64,128]{3,2,1,0:T(8,128)S(1)} collective-permute-done((f32[8,3,64,128]{3,2,1,0:T(8,128)S(1)}, f32[8,3,64,128]{3,2,1,0:T(8,128)S(1)}, u32[]{:S(2)}, u32[]{:S(2)}) %collective-permute-start.28) | collective-permute-done | bytes 786464 | tf_op jit(solution)/shard_map/ppermute | solution.py:591
  275.8 16.3 %collective-permute-done.30.refs_1_ = f32[8,3,64,128]{3,2,1,0:T(8,128)S(1)} collective-permute-done((f32[8,3,64,128]{3,2,1,0:T(8,128)S(1)}, f32[8,3,64,128]{3,2,1,0:T(8,128)S(1)}, u32[]{:S(2)}, u32[]{:S(2)}) %collective-permute-start.30) | collective-permute-done | bytes 786464 | tf_op jit(solution)/shard_map/ppermute | solution.py:591
  293.0 7.2 %to_output.1 = f32[1,3,128,2048]{3,2,1,0:T(8,128)} custom-call(s32[1]{0:T(128)} %bitcast.refs_0_.flag_ref, f32[32,3,64,128]{3,2,1,0:T(8,128)} %get-tuple-element.41.u_ref, f32[8,3,64,128]{3,2,1,0:T(8,128)} %copy-done.19, f32[8,3,64,128]{3,2,1,0:T(8,128)} %copy-done.20, f32[8,3,64,128]{3,2,1,0:T(8,128)} %copy-done.6, f32[8,3,64,128]{3,2,1,0:T(8,128)} %copy-done.7), custom_call_target="tpu_custom_call" | custom-call | tf_op jit(solution)/shard_map/to_output/pallas_call | solution.py:510
  (161 shorter events, 43.3 us)
Async XLA Ops:
  0.0 102.0 %copy-start = (s32[3,2]{0,1:T(2,128)S(1)}, s32[3,2]{0,1:T(2,128)}, u32[]{:S(2)}) copy-start(s32[3,2]{0,1:T(2,128)} %param.12) | copy-start | bytes 76
  0.0 22.0 %collective-permute-start.6 = (s32[64]{0:T(128)}, s32[64]{0:T(128)S(1)}, u32[]{:S(2)}, u32[]{:S(2)}) collective-permute-start(s32[64]{0:T(128)} %param.10), channel_id=1, source_target_pairs={{0,1},{1,0},{2,3},{3,2},{4,5},{5,4},{6,7},{7,6},{8,9},{9,8},{10,11... | collective-permute-start | bytes 776 | tf_op jit(solution)/shard_map/ppermute | solution.py:417
  0.5 22.2 %collective-permute-start.8 = (s32[64]{0:T(128)}, s32[64]{0:T(128)S(1)}, u32[]{:S(2)}, u32[]{:S(2)}) collective-permute-start(s32[64]{0:T(128)} %param.10), channel_id=1, source_target_pairs={{0,3},{1,2},{2,1},{3,0},{4,7},{5,6},{6,5},{7,4},{8,11},{9,10},{10,... | collective-permute-start | bytes 776 | tf_op jit(solution)/shard_map/ppermute | solution.py:417
  3.1 23.0 %collective-permute-start.7 = (s32[64]{0:T(128)}, s32[64]{0:T(128)S(1)}, u32[]{:S(2)}, u32[]{:S(2)}) collective-permute-start(s32[64]{0:T(128)} %param.10), channel_id=1, source_target_pairs={{0,2},{1,3},{2,0},{3,1},{4,6},{5,7},{6,4},{7,5},{8,10},{9,11},{10,... | collective-permute-start | bytes 776 | tf_op jit(solution)/shard_map/ppermute | solution.py:417
  4.3 30.3 %collective-permute-start.4 = (f32[2,3,128,256]{3,2,1,0:T(8,128)S(1)}, f32[2,3,128,256]{3,2,1,0:T(8,128)S(1)}, u32[]{:S(2)}, u32[]{:S(2)}) collective-permute-start(f32[2,3,128,256]{3,2,1,0:T(8,128)S(1)} %constant_dynamic-slice_fusion.1), channel_id=1, source_target_pairs={{0,4},{4,0},{1,5},{5,1},{2,6},{6,2},{3,7},{7,3},{8,12},{12,8},{9,1... | collective-permute-start | bytes 2359304 | tf_op jit(solution)/shard_map/ppermute | solution.py:391
  6.4 28.3 %collective-permute-start.5 = (f32[4,3,64,256]{3,2,1,0:T(8,128)}, f32[4,3,64,256]{3,2,1,0:T(8,128)S(1)}, u32[]{:S(2)}, u32[]{:S(2)}) collective-permute-start(f32[4,3,64,256]{3,2,1,0:T(8,128)} %b0_ref.1), channel_id=1, source_target_pairs={{0,2},{1,3},{2,0},{3,1},{4,6},{5,7},{6,4},{7,5},{8,10},{9,11},{10,... | collective-permute-start | bytes 2359304 | tf_op jit(solution)/shard_map/ppermute | solution.py:392
  16.5 9.5 %copy-start.36 = (f32[64,128]{1,0:T(8,128)S(1)}, f32[64,128]{1,0:T(8,128)}, u32[]{:S(2)}) copy-start(f32[64,128]{1,0:T(8,128)} %get-tuple-element.29) | copy-start | bytes 98308
  16.5 10.8 %copy-start.31 = (s32[64]{0:T(128)S(1)}, s32[64]{0:T(128)}, u32[]{:S(2)}) copy-start(s32[64]{0:T(128)} %param.10) | copy-start | bytes 772
  16.6 12.3 %copy-start.33 = (f32[3,32,128]{2,1,0:T(8,128)S(1)}, f32[3,32,128]{2,1,0:T(8,128)}, u32[]{:S(2)}) copy-start(f32[3,32,128]{2,1,0:T(8,128)} %get-tuple-element.30) | copy-start | bytes 147460
  16.6 14.2 %copy-start.32 = (f32[3,32,128]{2,1,0:T(8,128)S(1)}, f32[3,32,128]{2,1,0:T(8,128)}, u32[]{:S(2)}) copy-start(f32[3,32,128]{2,1,0:T(8,128)} %get-tuple-element.31) | copy-start | bytes 147460
  22.1 6.8 %collective-permute-start.9 = (s32[128]{0:T(128)S(1)}, s32[128]{0:T(128)S(1)}, u32[]{:S(2)}, u32[]{:S(2)}) collective-permute-start(s32[128]{0:T(128)S(1)} %copy-done.30), channel_id=1, source_target_pairs={{0,4},{4,0},{1,5},{5,1},{2,6},{6,2},{3,7},{7,3},{8,12},{12,8},{9,1... | collective-permute-start | bytes 1544 | tf_op jit(solution)/shard_map/ppermute | solution.py:417
  22.6 8.1 %collective-permute-start = (f32[64,128]{1,0:T(8,128)S(1)}, f32[64,128]{1,0:T(8,128)S(1)}, u32[]{:S(2)}, u32[]{:S(2)}) collective-permute-start(f32[64,128]{1,0:T(8,128)S(1)} %copy-done.39), channel_id=1, source_target_pairs={{0,4},{1,5},{2,6},{3,7},{8,12},{9,13},{10,14},{11,15},{16,20},{17,... | collective-permute-start | bytes 98312 | tf_op jit(solution)/shard_map/ppermute | solution.py:213
  26.1 6.6 %collective-permute-start.1 = (f32[64,128]{1,0:T(8,128)S(1)}, f32[64,128]{1,0:T(8,128)S(1)}, u32[]{:S(2)}, u32[]{:S(2)}) collective-permute-start(f32[64,128]{1,0:T(8,128)S(1)} %copy-done.36), channel_id=1, source_target_pairs={{4,0},{5,1},{6,2},{7,3},{12,8},{13,9},{14,10},{15,11},{20,16},{21,... | collective-permute-start | bytes 98312 | tf_op jit(solution)/shard_map/ppermute | solution.py:213
  28.8 3.8 %collective-permute-start.2 = (f32[3,32,128]{2,1,0:T(8,128)S(1)}, f32[3,32,128]{2,1,0:T(8,128)S(1)}, u32[]{:S(2)}, u32[]{:S(2)}) collective-permute-start(f32[3,32,128]{2,1,0:T(8,128)S(1)} %copy-done.33), channel_id=1, source_target_pairs={{0,1},{1,2},{2,3},{4,5},{5,6},{6,7},{8,9},{9,10},{10,11},{12,13},{... | collective-permute-start | bytes 147464 | tf_op jit(solution)/shard_map/ppermute | solution.py:213
  30.7 3.9 %collective-permute-start.3 = (f32[3,32,128]{2,1,0:T(8,128)S(1)}, f32[3,32,128]{2,1,0:T(8,128)S(1)}, u32[]{:S(2)}, u32[]{:S(2)}) collective-permute-start(f32[3,32,128]{2,1,0:T(8,128)S(1)} %copy-done.32), channel_id=1, source_target_pairs={{1,0},{2,1},{3,2},{5,4},{6,5},{7,6},{9,8},{10,9},{11,10},{13,12},{... | collective-permute-start | bytes 147464 | tf_op jit(solution)/shard_map/ppermute | solution.py:213
  42.9 53.8 %all-to-all-start = ((f32[8,2,2,3,64,128]{5,4,3,2,1,0:T(8,128)}), f32[8,2,2,3,64,128]{5,4,3,2,1,0:T(8,128)S(1)}, u32[]{:S(2)}, u32[]{:S(2)}) async-start(f32[8,2,2,3,64,128]{5,4,3,2,1,0:T(8,128)} %flow.3.refs_6_), calls=%async_computation | async-start | bytes 6291456 | tf_op jit(solution)/shard_map/all_to_all | solution.py:546
  49.2 19.4 %collective-permute-start.15 = (f32[4,3,64,256]{3,2,1,0:T(8,128)}, f32[4,3,64,256]{3,2,1,0:T(8,128)}, u32[]{:S(2)}, u32[]{:S(2)}) collective-permute-start(f32[4,3,64,256]{3,2,1,0:T(8,128)} %b0_ref.1), channel_id=1, source_target_pairs={{0,1},{1,0},{2,3},{3,2},{4,5},{5,4},{6,7},{7,6},{8,9},{9,8},{10,11... | collective-permute-start | bytes 2359304 | tf_op jit(solution)/shard_map/ppermute | solution.py:400
  62.4 8.0 %copy-start.34 = (f32[3,32,128]{2,1,0:T(8,128)S(1)}, f32[3,32,128]{2,1,0:T(8,128)}, u32[]{:S(2)}) copy-start(f32[3,32,128]{2,1,0:T(8,128)} %get-tuple-element.36) | copy-start | bytes 147460
  62.4 7.9 %collective-permute-start.14 = (f32[2,3,128,256]{3,2,1,0:T(8,128)}, f32[2,3,128,256]{3,2,1,0:T(8,128)}, u32[]{:S(2)}, u32[]{:S(2)}) collective-permute-start(f32[2,3,128,256]{3,2,1,0:T(8,128)} %after.16.first_ref), channel_id=1, source_target_pairs={{0,1},{1,0},{2,3},{3,2},{4,5},{5,4},{6,7},{7,6},{8,9},{9,8},{10,11... | collective-permute-start | bytes 2359304 | tf_op jit(solution)/shard_map/ppermute | solution.py:399
  62.5 14.7 %collective-permute-start.16 = (f32[4,3,64,256]{3,2,1,0:T(8,128)}, f32[4,3,64,256]{3,2,1,0:T(8,128)S(1)}, u32[]{:S(2)}, u32[]{:S(2)}) collective-permute-start(f32[4,3,64,256]{3,2,1,0:T(8,128)} %after.17.b2_ref), channel_id=1, source_target_pairs={{0,1},{1,0},{2,3},{3,2},{4,5},{5,4},{6,7},{7,6},{8,9},{9,8},{10,11... | collective-permute-start | bytes 2359304 | tf_op jit(solution)/shard_map/ppermute | solution.py:401
  63.1 19.4 %collective-permute-start.10 = (f32[64,128]{1,0:T(8,128)S(1)}, f32[64,128]{1,0:T(8,128)S(1)}, u32[]{:S(2)}, u32[]{:S(2)}) collective-permute-start(f32[64,128]{1,0:T(8,128)S(1)} %copy-done.38), channel_id=1, source_target_pairs={{0,4},{1,5},{2,6},{3,7},{8,12},{9,13},{10,14},{11,15},{16,20},{17,... | collective-permute-start | bytes 98312 | tf_op jit(solution)/shard_map/ppermute | solution.py:213
  67.3 20.0 %collective-permute-start.11 = (f32[64,128]{1,0:T(8,128)S(1)}, f32[64,128]{1,0:T(8,128)S(1)}, u32[]{:S(2)}, u32[]{:S(2)}) collective-permute-start(f32[64,128]{1,0:T(8,128)S(1)} %copy-done.37), channel_id=1, source_target_pairs={{4,0},{5,1},{6,2},{7,3},{12,8},{13,9},{14,10},{15,11},{20,16},{21,... | collective-permute-start | bytes 98312 | tf_op jit(solution)/shard_map/ppermute | solution.py:213
  68.6 18.7 %collective-permute-start.12 = (f32[3,32,128]{2,1,0:T(8,128)S(1)}, f32[3,32,128]{2,1,0:T(8,128)S(1)}, u32[]{:S(2)}, u32[]{:S(2)}) collective-permute-start(f32[3,32,128]{2,1,0:T(8,128)S(1)} %copy-done.35), channel_id=1, source_target_pairs={{0,1},{1,2},{2,3},{4,5},{5,6},{6,7},{8,9},{9,10},{10,11},{12,13},{... | collective-permute-start | bytes 147464 | tf_op jit(solution)/shard_map/ppermute | solution.py:213
  70.3 17.0 %collective-permute-start.13 = (f32[3,32,128]{2,1,0:T(8,128)S(1)}, f32[3,32,128]{2,1,0:T(8,128)S(1)}, u32[]{:S(2)}, u32[]{:S(2)}) collective-permute-start(f32[3,32,128]{2,1,0:T(8,128)S(1)} %copy-done.34), channel_id=1, source_target_pairs={{1,0},{2,1},{3,2},{5,4},{6,5},{7,6},{9,8},{10,9},{11,10},{13,12},{... | collective-permute-start | bytes 147464 | tf_op jit(solution)/shard_map/ppermute | solution.py:213
  98.3 55.4 %all-to-all-start.1 = ((f32[8,2,2,3,64,128]{5,4,3,2,1,0:T(8,128)}), f32[8,2,2,3,64,128]{5,4,3,2,1,0:T(8,128)S(1)}, u32[]{:S(2)}, u32[]{:S(2)}) async-start(f32[8,2,2,3,64,128]{5,4,3,2,1,0:T(8,128)} %after.19), calls=%async_computation.1 | async-start | bytes 6291456 | tf_op jit(solution)/shard_map/all_to_all | solution.py:553
  109.5 21.7 %collective-permute-start.17 = (f32[3,256,256]{2,1,0:T(8,128)}, f32[3,256,256]{2,1,0:T(8,128)}, u32[]{:S(2)}, u32[]{:S(2)}) collective-permute-start(f32[3,256,256]{2,1,0:T(8,128)} %get-tuple-element.44.refs_3_), channel_id=1, source_target_pairs={{0,8},{24,16},{1,9},{25,17},{2,10},{26,18},{3,11},{27,19},{4,12},{... | collective-permute-start | bytes 2359304 | tf_op jit(solution)/shard_map/ppermute | solution.py:563
  117.6 29.9 %collective-permute-start.19 = (f32[3,256,256]{2,1,0:T(8,128)}, f32[3,256,256]{2,1,0:T(8,128)}, u32[]{:S(2)}, u32[]{:S(2)}) collective-permute-start(f32[3,256,256]{2,1,0:T(8,128)} %get-tuple-element.45.refs_1_), channel_id=1, source_target_pairs={{0,8},{24,16},{1,9},{25,17},{2,10},{26,18},{3,11},{27,19},{4,12},{... | collective-permute-start | bytes 2359304 | tf_op jit(solution)/shard_map/ppermute | solution.py:563
  133.5 17.9 %collective-permute-start.18 = (f32[3,256,256]{2,1,0:T(8,128)}, f32[3,256,256]{2,1,0:T(8,128)}, u32[]{:S(2)}, u32[]{:S(2)}) collective-permute-start(f32[3,256,256]{2,1,0:T(8,128)} %add.69.refs_1_), channel_id=1, source_target_pairs={{8,16},{16,8},{9,17},{17,9},{10,18},{18,10},{11,19},{19,11},{12,20... | collective-permute-start | bytes 2359304 | tf_op jit(solution)/shard_map/ppermute | solution.py:568
  149.8 26.8 %collective-permute-start.21 = (f32[3,256,256]{2,1,0:T(8,128)}, f32[3,256,256]{2,1,0:T(8,128)}, u32[]{:S(2)}, u32[]{:S(2)}) collective-permute-start(f32[3,256,256]{2,1,0:T(8,128)} %add.70.refs_1_), channel_id=1, source_target_pairs={{8,16},{16,8},{9,17},{17,9},{10,18},{18,10},{11,19},{19,11},{12,20... | collective-permute-start | bytes 2359304 | tf_op jit(solution)/shard_map/ppermute | solution.py:568
  158.8 17.8 %copy-start.8 = (f32[3,256,256]{2,1,0:T(8,128)S(1)}, f32[3,256,256]{2,1,0:T(8,128)}, u32[]{:S(2)}) copy-start(f32[3,256,256]{2,1,0:T(8,128)} %get-tuple-element.48.refs_6_) | copy-start | bytes 2359300
  158.8 25.6 %collective-permute-start.20 = (f32[3,256,256]{2,1,0:T(8,128)}, f32[3,256,256]{2,1,0:T(8,128)S(1)}, u32[]{:S(2)}, u32[]{:S(2)}) collective-permute-start(f32[3,256,256]{2,1,0:T(8,128)} %get-tuple-element.47.refs_3_), channel_id=1, source_target_pairs={{0,8},{1,9},{2,10},{3,11},{4,12},{5,13},{6,14},{7,15}} | collective-permute-start | bytes 2359304 | tf_op jit(solution)/shard_map/ppermute | solution.py:563
  166.1 24.3 %collective-permute-start.24 = (f32[3,256,256]{2,1,0:T(8,128)}, f32[3,256,256]{2,1,0:T(8,128)S(1)}, u32[]{:S(2)}, u32[]{:S(2)}) collective-permute-start(f32[3,256,256]{2,1,0:T(8,128)} %add.71.refs_3_), channel_id=1, source_target_pairs={{8,0},{16,24},{9,1},{17,25},{10,2},{18,26},{11,3},{19,27},{12,4},{... | collective-permute-start | bytes 2359304 | tf_op jit(solution)/shard_map/ppermute | solution.py:573
  171.1 27.5 %collective-permute-start.23 = (f32[3,256,256]{2,1,0:T(8,128)}, f32[3,256,256]{2,1,0:T(8,128)}, u32[]{:S(2)}, u32[]{:S(2)}) collective-permute-start(f32[3,256,256]{2,1,0:T(8,128)} %get-tuple-element.49.refs_1_), channel_id=1, source_target_pairs={{0,8},{1,9},{2,10},{3,11},{4,12},{5,13},{6,14},{7,15}} | collective-permute-start | bytes 2359304 | tf_op jit(solution)/shard_map/ppermute | solution.py:563
  178.7 10.4 %copy-start.15 = (f32[3,256,256]{2,1,0:T(8,128)S(1)}, f32[3,256,256]{2,1,0:T(8,128)}, u32[]{:S(2)}) copy-start(f32[3,256,256]{2,1,0:T(8,128)} %add.72.refs_1_) | copy-start | bytes 2359300
  187.6 14.8 %collective-permute-start.22 = (f32[3,256,256]{2,1,0:T(8,128)}, f32[3,256,256]{2,1,0:T(8,128)}, u32[]{:S(2)}, u32[]{:S(2)}) collective-permute-start(f32[3,256,256]{2,1,0:T(8,128)} %add.73.refs_1_), channel_id=1, source_target_pairs={{8,16},{16,8},{9,17},{17,9},{10,18},{18,10},{11,19},{19,11},{12,20... | collective-permute-start | bytes 2359304 | tf_op jit(solution)/shard_map/ppermute | solution.py:568
  189.1 16.7 %collective-permute-start.27 = (f32[3,256,256]{2,1,0:T(8,128)S(1)}, f32[3,256,256]{2,1,0:T(8,128)S(1)}, u32[]{:S(2)}, u32[]{:S(2)}) collective-permute-start(f32[3,256,256]{2,1,0:T(8,128)S(1)} %copy-done.15), channel_id=1, source_target_pairs={{8,0},{16,24},{9,1},{17,25},{10,2},{18,26},{11,3},{19,27},{12,4},{... | collective-permute-start | bytes 2359304 | tf_op jit(solution)/shard_map/ppermute | solution.py:573
  200.8 12.4 %collective-permute-start.26 = (f32[3,256,256]{2,1,0:T(8,128)}, f32[3,256,256]{2,1,0:T(8,128)}, u32[]{:S(2)}, u32[]{:S(2)}) collective-permute-start(f32[3,256,256]{2,1,0:T(8,128)} %add.74.refs_1_), channel_id=1, source_target_pairs={{8,16},{16,8},{9,17},{17,9},{10,18},{18,10},{11,19},{19,11},{12,20... | collective-permute-start | bytes 2359304 | tf_op jit(solution)/shard_map/ppermute | solution.py:568
  204.6 19.6 %collective-permute-start.25 = (f32[3,256,256]{2,1,0:T(8,128)}, f32[3,256,256]{2,1,0:T(8,128)S(1)}, u32[]{:S(2)}, u32[]{:S(2)}) collective-permute-start(f32[3,256,256]{2,1,0:T(8,128)} %add.75.refs_1_), channel_id=1, source_target_pairs={{8,0},{16,24},{9,1},{17,25},{10,2},{18,26},{11,3},{19,27},{12,4},{... | collective-permute-start | bytes 2359304 | tf_op jit(solution)/shard_map/ppermute | solution.py:573
  214.6 9.5 %copy-start.18 = (f32[3,256,256]{2,1,0:T(8,128)}, f32[3,256,256]{2,1,0:T(8,128)S(1)}, u32[]{:S(2)}) copy-start(f32[3,256,256]{2,1,0:T(8,128)S(1)} %add.76.refs_1_) | copy-start | bytes 2359300
  214.6 26.6 %collective-permute-start.29 = (f32[3,256,256]{2,1,0:T(8,128)S(1)}, f32[3,256,256]{2,1,0:T(8,128)S(1)}, u32[]{:S(2)}, u32[]{:S(2)}) collective-permute-start(f32[3,256,256]{2,1,0:T(8,128)S(1)} %add.76.refs_1_), channel_id=1, source_target_pairs={{8,0},{16,24},{9,1},{17,25},{10,2},{18,26},{11,3},{19,27},{12,4},{... | collective-permute-start | bytes 2359304 | tf_op jit(solution)/shard_map/ppermute | solution.py:573
  231.6 17.1 %all-to-all-start.2 = ((f32[8,3,64,128]{3,2,1,0:T(8,128)}), f32[8,3,64,128]{3,2,1,0:T(8,128)S(1)}, u32[]{:S(2)}, u32[]{:S(2)}) async-start(f32[8,3,64,128]{3,2,1,0:T(8,128)} %sweep.6.refs_1_), calls=%async_computation.2 | async-start | bytes 1572864 | tf_op jit(solution)/shard_map/all_to_all | solution.py:590
  248.7 43.4 %copy-start.6 = (f32[8,3,64,128]{3,2,1,0:T(8,128)}, f32[8,3,64,128]{3,2,1,0:T(8,128)S(1)}, u32[]{:S(2)}) copy-start(f32[8,3,64,128]{3,2,1,0:T(8,128)S(1)} %all-to-all-done.2.refs_2_) | copy-start | bytes 2359300
  248.7 16.2 %all-to-all-start.3 = ((f32[8,3,64,128]{3,2,1,0:T(8,128)}), f32[8,3,64,128]{3,2,1,0:T(8,128)S(1)}, u32[]{:S(2)}, u32[]{:S(2)}) async-start(f32[8,3,64,128]{3,2,1,0:T(8,128)} %sweep.7), calls=%async_computation.3 | async-start | bytes 1572864 | tf_op jit(solution)/shard_map/all_to_all | solution.py:590
  252.4 23.4 %collective-permute-start.28 = (f32[8,3,64,128]{3,2,1,0:T(8,128)S(1)}, f32[8,3,64,128]{3,2,1,0:T(8,128)S(1)}, u32[]{:S(2)}, u32[]{:S(2)}) collective-permute-start(f32[8,3,64,128]{3,2,1,0:T(8,128)S(1)} %all-to-all-done.2.refs_2_), channel_id=1, source_target_pairs={{0,24},{1,25},{2,26},{3,27},{4,28},{5,29},{6,30},{7,31}} | collective-permute-start | bytes 2359304 | tf_op jit(solution)/shard_map/ppermute | solution.py:591
  265.0 27.1 %copy-start.7 = (f32[8,3,64,128]{3,2,1,0:T(8,128)}, f32[8,3,64,128]{3,2,1,0:T(8,128)S(1)}, u32[]{:S(2)}) copy-start(f32[8,3,64,128]{3,2,1,0:T(8,128)S(1)} %all-to-all-done.3.refs_3_) | copy-start | bytes 2359300
  265.0 27.1 %collective-permute-start.30 = (f32[8,3,64,128]{3,2,1,0:T(8,128)S(1)}, f32[8,3,64,128]{3,2,1,0:T(8,128)S(1)}, u32[]{:S(2)}, u32[]{:S(2)}) collective-permute-start(f32[8,3,64,128]{3,2,1,0:T(8,128)S(1)} %all-to-all-done.3.refs_3_), channel_id=1, source_target_pairs={{0,24},{1,25},{2,26},{3,27},{4,28},{5,29},{6,30},{7,31}} | collective-permute-start | bytes 2359304 | tf_op jit(solution)/shard_map/ppermute | solution.py:591
  275.8 16.3 %copy-start.19 = (f32[8,3,64,128]{3,2,1,0:T(8,128)}, f32[8,3,64,128]{3,2,1,0:T(8,128)S(1)}, u32[]{:S(2)}) copy-start(f32[8,3,64,128]{3,2,1,0:T(8,128)S(1)} %collective-permute-done.28.refs_0_) | copy-start | bytes 2359300
  292.1 8.1 %copy-start.1 = (s32[3,2]{0,1:T(2,128)S(1)}, s32[3,2]{0,1:T(2,128)}, u32[]{:S(2)}) copy-start(s32[3,2]{0,1:T(2,128)} %param.12) | copy-start | bytes 76
  (27 other events, 68.8 us)

commit v3 on v2

--- a/solution.py
+++ b/solution.py
@@ -27,21 +27,24 @@
     return lax.broadcasted_iota(jnp.int32, shape, dim)
 
 
-def edges_kernel(left_ref, right_ref, down_ref, up_ref, west_ref, east_ref, south_ref, north_ref, turned):
+def edges_kernel(left_ref, right_ref, down_ref, up_ref, west_ref, east_ref, south_ref, north_ref, rows, spread):
     comp = pl.program_id(0)
+    count = TILE_X // CZ
+    tiles = TILE_Y // count
     lane = iota((TILE_Y, TILE_X), 1)
+    mine = lane // CZ == comp
     for ref, which, out_ref in ((left_ref, 0, west_ref), (right_ref, 7, east_ref)):
-        turned[:, 0:8] = ref[0].T
+        for t in range(tiles):
+            rows[t : t + 1, :] = ref[0, which : which + 1, t * TILE_X : (t + 1) * TILE_X]
+        for r in range(count):
+            turned = pltpu.roll(rows[...], lax.rem((comp - r + count) * CZ, TILE_X), 1)
+            spread[pl.ds(r, tiles, stride=count), :] = turned
 
         @pl.when(comp == 0)
         def _():
             out_ref[...] = jnp.zeros_like(out_ref)
 
-        gathered = out_ref[...]
-        for z in range(CZ):
-            column = turned[pl.ds(z, TILE_Y, stride=CZ), :][:, which : which + 1]
-            gathered = jnp.where(lane == z * 3 + comp, column, gathered)
-        out_ref[...] = gathered
+        out_ref[...] = jnp.where(mine, spread[...], out_ref[...])
     south_ref[0] = down_ref[0].T[0:CZ]
     north_ref[0] = up_ref[0].T[TILE_X - CZ :]
 
@@ -62,7 +65,10 @@
         out_specs=[edge, edge, side, side],
         out_shape=[jax.ShapeDtypeStruct((TILE_Y, TILE_X), f32)] * 2
         + [jax.ShapeDtypeStruct((3, CZ, TILE_X), f32)] * 2,
-        scratch_shapes=[pltpu.VMEM((merged, 128), f32)],
+        scratch_shapes=[
+            pltpu.VMEM((merged // TILE_X, TILE_X), f32),
+            pltpu.VMEM((TILE_Y, TILE_X), f32),
+        ],
         compiler_params=params(),
         name="tile_edges",
     )(field, field, field, field)
@@ -101,7 +107,7 @@
     acoustic = flag_ref[0] > 0
     lane = iota((TILE_Y, TILE_X), 1)
     row = iota((TILE_Y, TILE_X), 0)
-    turn = lax.rem(TILE_X - group * (per * 3), TILE_X)
+    turn = lax.rem(TILE_X - group * per, TILE_X)
     xlo = pltpu.roll(xlo_ref[...], turn, 1)
     xhi = pltpu.roll(xhi_ref[...], turn, 1)
     if "edges" in want:
@@ -123,7 +129,7 @@
             mid = u_ref[z, c]
             up = u_ref[above, c]
             down = u_ref[below, c]
-            spot = i * 3 + c
+            spot = c * CZ + i
             xm = jnp.where(lane == 0, xlo[:, spot : spot + 1], pltpu.roll(mid, 1, 1))
             xp = jnp.where(
                 lane == TILE_X - 1, xhi[:, spot : spot + 1], pltpu.roll(mid, TILE_X - 1, 1)
@@ -153,7 +159,7 @@
                 moved = centre[c] + time_step * (viscosity * lap[c] - lamb[c])
                 next_ref[i, c] = moved
             if "edges" in want:
-                here = lane == z * 3 + c
+                here = lane == c * CZ + z
                 west = jnp.where(here, moved[:, 0:1], west)
                 east = jnp.where(here, moved[:, TILE_X - 1 :], east)
                 south_ref[c, pl.ds(z, 1), :] = moved[0:1, :]
@@ -384,21 +390,23 @@
     )(pos, *blocks)
 
 
-def fetched_ops(x_ops, y_ops):
+def fetched_ops(x_ops, y_ops, earlier):
     core = lax.rem(lax.axis_index("gy"), 2)
     half = NCLASS // 2
     piece = lax.dynamic_slice_in_dim(x_ops, core * half, half, 0)
-    got_x = lax.ppermute(piece, "gx", [(0, 1), (1, 0)])
-    got_y = lax.ppermute(y_ops, "gy", [(i, i ^ 2) for i in range(4)])
+    got_x = lax.ppermute(after(piece, earlier), "gx", [(0, 1), (1, 0)])
+    got_y = lax.ppermute(after(y_ops, earlier), "gy", [(i, i ^ 2) for i in range(4)])
     return got_x, got_y
 
 
-def prepared_ops(x_ops, y_ops, fetched):
+def paired_ops(y_ops, got_x, got_y):
+    beside = [(i, i ^ 1) for i in range(4)]
+    return [lax.ppermute(value, "gy", beside) for value in (got_x, y_ops, got_y)]
+
+
+def prepared_ops(x_ops, y_ops, fetched, paired):
     got_x, got_y = fetched
-    beside = [(i, i ^ 1) for i in range(4)]
-    pair_x = lax.ppermute(got_x, "gy", beside)
-    pair_y = lax.ppermute(y_ops, "gy", beside)
-    cross_y = lax.ppermute(got_y, "gy", beside)
+    pair_x, pair_y, cross_y = paired
     place_y = lax.axis_index("gy")
     pos = jnp.stack([lax.axis_index("gx"), lax.rem(place_y, 2), place_y]).astype(jnp.int32)
     x_parts = prepare_ops(
@@ -536,24 +544,23 @@
     lower = (sec < 2).astype(jnp.int32)
     ints = jnp.stack([active, lower, offsets[0], offsets[1]])
 
-    halo = exchange(*tile_edges(fields[0]))
-    fetched = fetched_ops(x_ops, y_ops)
-    classes = gathered_classes(x_line_class, y_line_class)
-    planes = to_planes(fields[0], ())
-
-    waits = (*fetched, *classes)
-    (lamb,) = flow(flag, planes, halo, waits, groups, ("lamb", "passed"))
+    edges = tile_edges(fields[0])
+    planes = to_planes(fields[0], [edges[0]])
+    halo = [after(value, [planes]) for value in exchange(*edges)]
+
+    (lamb,) = flow(flag, planes, halo, (), groups, ("lamb", "passed"))
     gots = [lax.all_to_all(lamb, ("gx", "gy"), 0, 0)]
-    planes, *edges = flow(flag, planes, halo, (lamb,), groups, ("next", "edges"))
+    waits = (lamb, ints, matrix)
+    planes, *edges = flow(flag, planes, halo, waits, groups, ("next", "edges"))
     halo = exchange(*edges)
-    fetched = [after(value, [planes]) for value in fetched]
-    x_parts, y_parts = prepared_ops(x_ops, y_ops, fetched)
-    lamb, planes = flow(flag, planes, halo, (*x_parts, *y_parts), groups, ("lamb", "next"))
+    lamb, planes = flow(flag, planes, halo, (), groups, ("lamb", "next"))
     gots[0] = after(gots[0], [lamb])
     gots.append(lax.all_to_all(after(lamb, [gots[0]]), ("gx", "gy"), 0, 0))
+    fetched = list(fetched_ops(x_ops, y_ops, [gots[1]]))
 
     total = STEPS * CHUNKS
     fars, nears, firsts, seconds, thirds, ends = ([None] * total for _ in range(6))
+    lines, beside, parts = [], [], []
     token = []
 
     def placed(n):
@@ -561,32 +568,51 @@
         got = gots[n // CHUNKS]
         fars[n], nears[n] = place(ints, matrix, got, n % CHUNKS, token, gx, gy, first)
         firsts[n] = lax.ppermute(fars[n], "sec", [(0, 1), (3, 2)] if first else [(0, 1)])
-        return fars[n]
+        return [fars[n]]
+
+    def classes(n):
+        lines.extend(gathered_classes(after(x_line_class, token), after(y_line_class, token)))
+        return token
+
+    def paired(n):
+        fetched[:] = [after(value, token) for value in fetched]
+        beside.extend(paired_ops(y_ops, *fetched))
+        return token
+
+    def prepared(n):
+        brought = [after(value, token) for value in beside]
+        parts.extend(prepared_ops(x_ops, y_ops, fetched, brought))
+        return [*parts[0], *parts[1]]
 
     def first_hop(n):
         value = fars[n] + after(firsts[n], token)
         seconds[n] = lax.ppermute(value, "sec", [(1, 2), (2, 1)])
-        return value
+        return [value]
 
     def second_hop(n):
         value = nears[n] + after(seconds[n], token)
         thirds[n] = lax.ppermute(value, "sec", [(1, 0), (2, 3)])
-        return value
+        return [value]
+
+    def arrived(n):
+        thirds[n] = after(thirds[n], token)
+        return [thirds[n]]
 
     def swept(n):
         terms = (nears[n], after(thirds[n], token))
         if n >= CHUNKS:
             terms += (ends[n - CHUNKS],)
-        ends[n] = sweep(classes, x_parts, y_parts, terms, gx, gy, n >= total - CHUNKS)
-        return ends[n]
+        ends[n] = sweep(lines, *parts, terms, gx, gy, n >= total - CHUNKS)
+        return [ends[n]]
 
     order = (
-        (placed, 0), (placed, 1), (first_hop, 0), (first_hop, 1), (second_hop, 0),
-        (placed, 2), (placed, 3), (second_hop, 1), (first_hop, 2), (swept, 0),
-        (first_hop, 3), (second_hop, 2), (swept, 1), (second_hop, 3), (swept, 2), (swept, 3),
+        (placed, 0), (placed, 1), (first_hop, 0), (placed, 2), (first_hop, 1), (second_hop, 0),
+        (placed, 3), (first_hop, 2), (paired, 0), (arrived, 0), (second_hop, 1), (classes, 0),
+        (prepared, 0), (first_hop, 3), (second_hop, 2), (arrived, 1), (swept, 0),
+        (second_hop, 3), (swept, 2), (swept, 1), (swept, 3),
     )
     for work, n in order:
-        token = [work(n)]
+        token = work(n)
     tiles = [lax.all_to_all(value, ("gx", "gy"), 0, 0) for value in ends[-CHUNKS:]]
     brought = [lax.ppermute(value, "sec", [(0, 3)]) for value in tiles]
     return to_output(flag, planes, brought + tiles)

time: 302 us -> 285 us (0.944)
  waiting for transfers between devices: 79.8 us -> 67.1 us
  Pallas kernels: 99.6 us -> 93.8 us
  local copies, waits for them, and re-layouts: 15.2 us -> 20.2 us
    ppermute x4, waiting for transfers between devices: 30.2 us -> 14.3 us  [placed(): lax.ppermute(fars[n], 'sec', [(0, 1), (3, 2)] if first else [(0, 1)])]
    all_to_all x1, starting transfers between devices: 3.65 us -> 10.4 us  [local(): gots.append(lax.all_to_all(after(lamb, [gots[0]]), ('gx', 'gy'), 0, 0))]
    pallas_call x1, Pallas kernels: 8.61 us -> 3.02 us  [tile_edges(): pl.pallas_call(edges_kernel, grid=(3,), in_specs=[pl.BlockSpec((1, 8, mer...]
    ppermute x4, starting transfers between devices: 19.4 us -> 14.1 us  [placed(): lax.ppermute(fars[n], 'sec', [(0, 1), (3, 2)] if first else [(0, 1)])]
    ppermute x4, waiting for transfers between devices: 14.1 us -> 9.2 us  [second_hop(): thirds[n] = lax.ppermute(value, 'sec', [(1, 0), (2, 3)])]
    unnamed x80 -> x65, local copies, waits for them, and re-layouts: 11.4 us -> 15.5 us
    all_to_all x1, waiting for transfers between devices: 0.01 us -> 3.83 us  [local(): gots.append(lax.all_to_all(after(lamb, [gots[0]]), ('gx', 'gy'), 0, 0))]
    ppermute x8, starting transfers between devices: 15.7 us -> 19 us  [send(): lax.ppermute(value, axis, [(i, i + step) for i in range(count) if 0 <= i...]
  transfers between devices with their start and end apart: 35 -> 35, of which waited for: 11 -> 16; matrix products, arithmetic and copies ran while one was open for 9% -> 10% of each run, Pallas kernels for 28% -> 27%
where the time goes in v3:
time: 285 us; the launch traced here: 283 us
  Pallas kernels  93.8 us (33%)
  starting transfers between devices  80.4 us (28%)
  waiting for transfers between devices  67.1 us (24%)
  other arithmetic  21.5 us (8%)
  local copies, waits for them, and re-layouts  20.2 us (7%)
    pallas_call x3, Pallas kernels, flow(): pl.pallas_call(body, grid=(groups,), in_specs=[pl.BlockSpec(memory_space=...  28.3 us
    pallas_call x4, Pallas kernels, sweep(): pl.pallas_call(body, grid=(3,), in_specs=[pl.BlockSpec((full_y, 1), lambd...  26.3 us
    ppermute x2, waiting for transfers between devices, local(): brought = [lax.ppermute(value, 'sec', [(0, 3)]) for value in tiles]  21.6 us
    ppermute x8, starting transfers between devices, send(): lax.ppermute(value, axis, [(i, i + step) for i in range(count) if 0 <= i...  19 us
    unnamed x65, local copies, waits for them, and re-layouts  15.5 us
    ppermute x4, waiting for transfers between devices, placed(): lax.ppermute(fars[n], 'sec', [(0, 1), (3, 2)] if first else [(0, 1)])  14.3 us
    pallas_call x4, Pallas kernels, place(): pl.pallas_call(body, grid=(1,), in_specs=[pl.BlockSpec(memory_space=pltpu...  14.3 us
    ppermute x4, starting transfers between devices, placed(): lax.ppermute(fars[n], 'sec', [(0, 1), (3, 2)] if first else [(0, 1)])  14.1 us
  transfers between devices with their start and end apart: 35, of which 16 were waited for; matrix products, arithmetic and copies ran while one was open for 10% of the time, Pallas kernels for 27%

profile of v3, /device:TPU:0, one launch (start us, length us, event | category | flops | bytes accessed | tf_op | source)
XLA Modules:
  0.0 283.4 jit_solution(7053349853830270733)
XLA Ops:
  2.5 3.0 %tile_edges.1 = (f32[64,128]{1,0:T(8,128)}, f32[64,128]{1,0:T(8,128)}, f32[3,32,128]{2,1,0:T(8,128)}, f32[3,32,128]{2,1,0:T(8,128)}) custom-call(f32[3,128,2048]{2,1,0:T(8,128)} %bitcast.21, f32[3,128,2048]{2,1,0:T(8,128)} %bitcast.22, f32[3,128,2048]{2,1,0:T(8,128)} %bitcast.23, f32[3,128,2048]{2,1,0:T(8,128)} %bitcast.24), custom_call_target="tpu_custom_call" | custom-call | tf_op jit(solution)/shard_map/tile_edges/pallas_call | solution.py:56
  6.8 3.0 %collective-permute-start.2 = (f32[3,32,128]{2,1,0:T(8,128)}, f32[3,32,128]{2,1,0:T(8,128)S(1)}, u32[]{:S(2)}, u32[]{:S(2)}) collective-permute-start(f32[3,32,128]{2,1,0:T(8,128)} %get-tuple-element.30), channel_id=1, source_target_pairs={{0,1},{1,2},{2,3},{4,5},{5,6},{6,7},{8,9},{9,10},{10,11},{12,13},{... | collective-permute-start | bytes 147464 | tf_op jit(solution)/shard_map/ppermute | solution.py:219
  11.1 4.9 %collective-permute-start = (f32[64,128]{1,0:T(8,128)}, f32[64,128]{1,0:T(8,128)S(1)}, u32[]{:S(2)}, u32[]{:S(2)}) collective-permute-start(f32[64,128]{1,0:T(8,128)} %get-tuple-element.29), channel_id=1, source_target_pairs={{0,4},{1,5},{2,6},{3,7},{8,12},{9,13},{10,14},{11,15},{16,20},{17,... | collective-permute-start | bytes 98312 | tf_op jit(solution)/shard_map/ppermute | solution.py:219
  16.0 5.4 %to_planes.1.refs_1_ = f32[32,3,64,128]{3,2,1,0:T(8,128)} custom-call(f32[3,128,2048]{2,1,0:T(8,128)} %bitcast.25, f32[64,128]{1,0:T(8,128)} %get-tuple-element.28.refs_0_), custom_call_target="tpu_custom_call" | custom-call | tf_op jit(solution)/shard_map/to_planes/pallas_call | solution.py:89
  23.9 7.1 %flow.3.refs_6_ = f32[8,2,2,3,64,128]{5,4,3,2,1,0:T(8,128)} custom-call(s32[1]{0:T(128)} %bitcast.refs_0_.flag_ref, f32[32,3,64,128]{3,2,1,0:T(8,128)} %to_planes.1.refs_1_, f32[64,128]{1,0:T(8,128)} %after.29.refs_2_, f32[64,128]{1,0:T(8,128)} %after.30.refs_3_, f32[3,32,128]{2,1,0:T(8,128)} %after.31.refs_4_, f32[3,32,128]{2,1,0:T(8,128)} %after.32.refs_5_), custom_call_target="tpu_custom_call" | custom-call | tf_op jit(solution)/shard_map/flow/pallas_call | solution.py:197
  31.0 3.9 %all-to-all-start = ((f32[8,2,2,3,64,128]{5,4,3,2,1,0:T(8,128)}), f32[8,2,2,3,64,128]{5,4,3,2,1,0:T(8,128)S(1)}, u32[]{:S(2)}, u32[]{:S(2)}) async-start(f32[8,2,2,3,64,128]{5,4,3,2,1,0:T(8,128)} %flow.3.refs_6_), calls=%async_computation | async-start | bytes 6291456 | tf_op jit(solution)/shard_map/all_to_all | solution.py:552
  35.6 1.9 pad_add_fusion.2.refs_7_.refs_0_
  38.7 12.6 %flow.4 = (f32[32,3,64,128]{3,2,1,0:T(8,128)}, f32[64,128]{1,0:T(8,128)}, f32[64,128]{1,0:T(8,128)}, f32[3,32,128]{2,1,0:T(8,128)}, f32[3,32,128]{2,1,0:T(8,128)}) custom-call(s32[1]{0:T(128)} %bitcast.refs_0_.flag_ref, f32[32,3,64,128]{3,2,1,0:T(8,128)} %to_planes.1.refs_1_, f32[64,128]{1,0:T(8,128)} %after.29.refs_2_, f32[64,128]{1,0:T(8,128)} %after.30.refs_3_, ...), custom_call_target="tpu_custom_call" | custom-call | tf_op jit(solution)/shard_map/flow/pallas_call | solution.py:197
  51.3 3.3 %collective-permute-start.6 = (f32[3,32,128]{2,1,0:T(8,128)}, f32[3,32,128]{2,1,0:T(8,128)S(1)}, u32[]{:S(2)}, u32[]{:S(2)}) collective-permute-start(f32[3,32,128]{2,1,0:T(8,128)} %get-tuple-element.35), channel_id=1, source_target_pairs={{0,1},{1,2},{2,3},{4,5},{5,6},{6,7},{8,9},{9,10},{10,11},{12,13},{... | collective-permute-start | bytes 147464 | tf_op jit(solution)/shard_map/ppermute | solution.py:219
  55.9 2.7 collective-permute-start.4
  61.7 3.2 %collective-permute-done.5.refs_3_ = f32[64,128]{1,0:T(8,128)S(1)} collective-permute-done((f32[64,128]{1,0:T(8,128)}, f32[64,128]{1,0:T(8,128)S(1)}, u32[]{:S(2)}, u32[]{:S(2)}) %collective-permute-start.5) | collective-permute-done | bytes 32800 | tf_op jit(solution)/shard_map/ppermute | solution.py:219
  65.5 8.6 %flow.5 = (f32[8,2,2,3,64,128]{5,4,3,2,1,0:T(8,128)}, f32[32,3,64,128]{3,2,1,0:T(8,128)}) custom-call(s32[1]{0:T(128)} %bitcast.refs_0_.flag_ref, f32[32,3,64,128]{3,2,1,0:T(8,128)} %get-tuple-element.32.refs_1_, f32[64,128]{1,0:T(8,128)} %copy-done.28, f32[64,128]{1,0:T(8,128)} %copy-done.29, f32[3,32,128]{2,1,0:T(8,128)} %copy-done.26, ...), custom_call_target="tpu_custom_call" | custom-call | tf_op jit(solution)/shard_map/flow/pallas_call | solution.py:197
  75.9 10.4 %all-to-all-start.1 = ((f32[8,2,2,3,64,128]{5,4,3,2,1,0:T(8,128)}), f32[8,2,2,3,64,128]{5,4,3,2,1,0:T(8,128)S(1)}, u32[]{:S(2)}, u32[]{:S(2)}) async-start(f32[8,2,2,3,64,128]{5,4,3,2,1,0:T(8,128)} %after.34), calls=%async_computation.1 | async-start | bytes 6291456 | tf_op jit(solution)/shard_map/all_to_all | solution.py:558
  86.2 3.7 %place.4 = (f32[3,256,256]{2,1,0:T(8,128)}, f32[3,256,256]{2,1,0:T(8,128)}) custom-call(s32[4]{0:T(128)} %pad_add_fusion.2.refs_7_.refs_0_, f32[3,3]{1,0:T(4,128)} %select_bitcast_fusion.refs_8_.refs_1_, f32[8,2,2,3,64,128]{5,4,3,2,1,0:T(8,128)} %after.33.refs_2_.refs_1_), custom_call_target="tpu_custom_call" | custom-call | tf_op jit(solution)/shard_map/place/pallas_call | solution.py:303
  90.0 5.2 %collective-permute-start.9 = (f32[3,256,256]{2,1,0:T(8,128)}, f32[3,256,256]{2,1,0:T(8,128)}, u32[]{:S(2)}, u32[]{:S(2)}) collective-permute-start(f32[3,256,256]{2,1,0:T(8,128)} %get-tuple-element.39.refs_3_), channel_id=1, source_target_pairs={{0,8},{24,16},{1,9},{25,17},{2,10},{26,18},{3,11},{27,19},{4,12},{... | collective-permute-start | bytes 2359304 | tf_op jit(solution)/shard_map/ppermute | solution.py:570
  95.1 3.7 %place.5 = (f32[3,256,256]{2,1,0:T(8,128)}, f32[3,256,256]{2,1,0:T(8,128)}) custom-call(s32[4]{0:T(128)} %pad_add_fusion.2.refs_7_.refs_0_, f32[3,3]{1,0:T(4,128)} %select_bitcast_fusion.refs_8_.refs_1_, f32[8,2,2,3,64,128]{5,4,3,2,1,0:T(8,128)} %after.33.refs_2_.refs_1_, f32[3,256,256]{2,1,0:T(8,128)} %get-tuple-element.39.refs_3_), custom_call_target="tpu_custom_call" | custom-call | tf_op jit(solution)/shard_map/place/pallas_call | solution.py:303
  98.8 2.2 collective-permute-start.8
  101.0 11.2 %collective-permute-done.9.refs_0_ = f32[3,256,256]{2,1,0:T(8,128)} collective-permute-done((f32[3,256,256]{2,1,0:T(8,128)}, f32[3,256,256]{2,1,0:T(8,128)}, u32[]{:S(2)}, u32[]{:S(2)}) %collective-permute-start.9) | collective-permute-done | bytes 786464 | tf_op jit(solution)/shard_map/ppermute | solution.py:570
  112.2 2.4 add.65.refs_3_
  116.1 2.1 copy.59.refs_0_
  118.2 2.1 constant_dynamic-slice_fusion.refs_0_
  120.3 3.8 %all-to-all-done.1.refs_2_.refs_1_ = f32[8,2,2,3,64,128]{5,4,3,2,1,0:T(8,128)S(1)} async-done(((f32[8,2,2,3,64,128]{5,4,3,2,1,0:T(8,128)}), f32[8,2,2,3,64,128]{5,4,3,2,1,0:T(8,128)S(1)}, u32[]{:S(2)}, u32[]{:S(2)}) %all-to-all-start.1) | async-done | bytes 3145760 | tf_op jit(solution)/shard_map/all_to_all | solution.py:558
  125.8 3.4 %place.6 = (f32[3,256,256]{2,1,0:T(8,128)}, f32[3,256,256]{2,1,0:T(8,128)}) custom-call(s32[4]{0:T(128)} %pad_add_fusion.2.refs_7_.refs_0_, f32[3,3]{1,0:T(4,128)} %select_bitcast_fusion.refs_8_.refs_1_, f32[8,2,2,3,64,128]{5,4,3,2,1,0:T(8,128)} %copy-done.2, f32[3,256,256]{2,1,0:T(8,128)} %add.65.refs_3_), custom_call_target="tpu_custom_call" | custom-call | tf_op jit(solution)/shard_map/place/pallas_call | solution.py:303
  129.2 4.3 %collective-permute-start.13 = (f32[3,256,256]{2,1,0:T(8,128)}, f32[3,256,256]{2,1,0:T(8,128)S(1)}, u32[]{:S(2)}, u32[]{:S(2)}) collective-permute-start(f32[3,256,256]{2,1,0:T(8,128)} %get-tuple-element.42.refs_1_), channel_id=1, source_target_pairs={{0,8},{1,9},{2,10},{3,11},{4,12},{5,13},{6,14},{7,15}} | collective-permute-start | bytes 2359304 | tf_op jit(solution)/shard_map/ppermute | solution.py:570
  133.6 2.3 add.66.refs_1_
  137.9 2.2 add.67.refs_3_
  143.1 3.4 %place.7 = (f32[3,256,256]{2,1,0:T(8,128)}, f32[3,256,256]{2,1,0:T(8,128)}) custom-call(s32[4]{0:T(128)} %pad_add_fusion.2.refs_7_.refs_0_, f32[3,3]{1,0:T(4,128)} %select_bitcast_fusion.refs_8_.refs_1_, f32[8,2,2,3,64,128]{5,4,3,2,1,0:T(8,128)} %copy-done.2, f32[3,256,256]{2,1,0:T(8,128)} %add.67.refs_3_), custom_call_target="tpu_custom_call" | custom-call | tf_op jit(solution)/shard_map/place/pallas_call | solution.py:303
  146.5 2.9 %collective-permute-done.13.refs_0_ = f32[3,256,256]{2,1,0:T(8,128)S(1)} collective-permute-done((f32[3,256,256]{2,1,0:T(8,128)}, f32[3,256,256]{2,1,0:T(8,128)S(1)}, u32[]{:S(2)}, u32[]{:S(2)}) %collective-permute-start.13) | collective-permute-done | bytes 786464 | tf_op jit(solution)/shard_map/ppermute | solution.py:570
  150.3 2.2 add.68.refs_1_
  154.6 6.0 %collective-permute-done.12.refs_0_ = f32[3,256,256]{2,1,0:T(8,128)S(1)} collective-permute-done((f32[3,256,256]{2,1,0:T(8,128)}, f32[3,256,256]{2,1,0:T(8,128)S(1)}, u32[]{:S(2)}, u32[]{:S(2)}) %collective-permute-start.12) | collective-permute-done | bytes 786464 | tf_op jit(solution)/shard_map/ppermute | solution.py:594
  160.7 2.4 collective-permute-start.24
  168.0 4.9 %x_operators.1 = (bf16[4,3,256,256]{3,2,1,0:T(8,128)(2,1)}, bf16[4,3,256,256]{3,2,1,0:T(8,128)(2,1)}) custom-call(s32[3]{0:T(128)} %pad_add_fusion.3.pos_ref, f32[4,3,128,256]{3,2,1,0:T(8,128)} %mine_ref.1, f32[2,3,128,256]{3,2,1,0:T(8,128)} %after.44.first_ref, f32[2,3,128,256]{3,2,1,0:T(8,128)} %after.45.second_ref), custom_call_target="tpu_custom_call" | custom-call | tf_op jit(solution)/shard_map/x_operators/pallas_call | solution.py:382
  172.9 4.5 %y_operators.1 = (bf16[4,3,256,256]{3,2,1,0:T(8,128)(2,1)}, bf16[4,3,256,256]{3,2,1,0:T(8,128)(2,1)}) custom-call(s32[3]{0:T(128)} %pad_add_fusion.3.pos_ref, f32[4,3,64,256]{3,2,1,0:T(8,128)} %b0_ref.1, f32[4,3,64,256]{3,2,1,0:T(8,128)} %after.46.b1_ref, f32[4,3,64,256]{3,2,1,0:T(8,128)} %after.48.b2_ref, f32[4,3,64,256]{3,2,1,0:T(8,128)} %after.49.b3_ref), custom_call_target="tpu_custom_call" | custom-call | tf_op jit(solution)/shard_map/y_operators/pallas_call | solution.py:382
  177.5 2.4 add.74.refs_1_
  181.6 2.2 add.75.refs_1_
  195.3 6.5 %sweep.4.refs_1_.refs_8_ = f32[3,256,256]{2,1,0:T(8,128)} custom-call(s32[256,1]{1,0:T(8,128)} %select_n.92.refs_0_, s32[1,256]{1,0:T(1,128)} %bitcast.26, bf16[4,3,256,256]{3,2,1,0:T(8,128)(2,1)} %get-tuple-element.45.refs_1_.refs_2_, bf16[4,3,256,256]{3,2,1,0:T(8,128)(2,1)} %get-tuple-element.46.refs_2_.refs_3_, ...), custom_call_target="tpu_custom_call" | custom-call | tf_op jit(solution)/shard_map/sweep/pallas_call | solution.py:478
  204.4 2.9 %collective-permute-done.25.refs_0_ = f32[3,256,256]{2,1,0:T(8,128)S(1)} collective-permute-done((f32[3,256,256]{2,1,0:T(8,128)}, f32[3,256,256]{2,1,0:T(8,128)S(1)}, u32[]{:S(2)}, u32[]{:S(2)}) %collective-permute-start.25) | collective-permute-done | bytes 786464 | tf_op jit(solution)/shard_map/ppermute | solution.py:594
  208.2 6.6 %sweep.5.refs_1_ = f32[8,3,64,128]{3,2,1,0:T(8,128)} custom-call(s32[256,1]{1,0:T(8,128)} %select_n.92.refs_0_, s32[1,256]{1,0:T(1,128)} %bitcast.27, bf16[4,3,256,256]{3,2,1,0:T(8,128)(2,1)} %get-tuple-element.45.refs_1_.refs_2_, bf16[4,3,256,256]{3,2,1,0:T(8,128)(2,1)} %get-tuple-element.46.refs_2_.refs_3_, ...), custom_call_target="tpu_custom_call" | custom-call | tf_op jit(solution)/shard_map/sweep/pallas_call | solution.py:478
  214.9 3.5 %all-to-all-start.2 = ((f32[8,3,64,128]{3,2,1,0:T(8,128)}), f32[8,3,64,128]{3,2,1,0:T(8,128)S(1)}, u32[]{:S(2)}, u32[]{:S(2)}) async-start(f32[8,3,64,128]{3,2,1,0:T(8,128)} %sweep.5.refs_1_), calls=%async_computation.2 | async-start | bytes 1572864 | tf_op jit(solution)/shard_map/all_to_all | solution.py:616
  218.4 6.5 %sweep.6.refs_1_.refs_8_ = f32[3,256,256]{2,1,0:T(8,128)} custom-call(s32[256,1]{1,0:T(8,128)} %select_n.92.refs_0_, s32[1,256]{1,0:T(1,128)} %bitcast.28, bf16[4,3,256,256]{3,2,1,0:T(8,128)(2,1)} %get-tuple-element.45.refs_1_.refs_2_, bf16[4,3,256,256]{3,2,1,0:T(8,128)(2,1)} %get-tuple-element.46.refs_2_.refs_3_, ...), custom_call_target="tpu_custom_call" | custom-call | tf_op jit(solution)/shard_map/sweep/pallas_call | solution.py:478
  226.1 6.6 %sweep.7 = f32[8,3,64,128]{3,2,1,0:T(8,128)} custom-call(s32[256,1]{1,0:T(8,128)} %select_n.92.refs_0_, s32[1,256]{1,0:T(1,128)} %bitcast.29, bf16[4,3,256,256]{3,2,1,0:T(8,128)(2,1)} %get-tuple-element.45.refs_1_.refs_2_, bf16[4,3,256,256]{3,2,1,0:T(8,128)(2,1)} %get-tuple-element.46.refs_2_.refs_3_, ...), custom_call_target="tpu_custom_call" | custom-call | tf_op jit(solution)/shard_map/sweep/pallas_call | solution.py:478
  232.7 3.9 %all-to-all-start.3 = ((f32[8,3,64,128]{3,2,1,0:T(8,128)}), f32[8,3,64,128]{3,2,1,0:T(8,128)S(1)}, u32[]{:S(2)}, u32[]{:S(2)}) async-start(f32[8,3,64,128]{3,2,1,0:T(8,128)} %sweep.7), calls=%async_computation.3 | async-start | bytes 1572864 | tf_op jit(solution)/shard_map/all_to_all | solution.py:616
  236.6 4.4 %collective-permute-start.28 = (f32[8,3,64,128]{3,2,1,0:T(8,128)S(1)}, f32[8,3,64,128]{3,2,1,0:T(8,128)S(1)}, u32[]{:S(2)}, u32[]{:S(2)}) collective-permute-start(f32[8,3,64,128]{3,2,1,0:T(8,128)S(1)} %all-to-all-done.2.refs_2_), channel_id=1, source_target_pairs={{0,24},{1,25},{2,26},{3,27},{4,28},{5,29},{6,30},{7,31}} | collective-permute-start | bytes 2359304 | tf_op jit(solution)/shard_map/ppermute | solution.py:617
  241.0 8.2 %all-to-all-done.3.refs_3_ = f32[8,3,64,128]{3,2,1,0:T(8,128)S(1)} async-done(((f32[8,3,64,128]{3,2,1,0:T(8,128)}), f32[8,3,64,128]{3,2,1,0:T(8,128)S(1)}, u32[]{:S(2)}, u32[]{:S(2)}) %all-to-all-start.3) | async-done | bytes 786464 | tf_op jit(solution)/shard_map/all_to_all | solution.py:616
  249.2 4.4 %collective-permute-start.30 = (f32[8,3,64,128]{3,2,1,0:T(8,128)S(1)}, f32[8,3,64,128]{3,2,1,0:T(8,128)S(1)}, u32[]{:S(2)}, u32[]{:S(2)}) collective-permute-start(f32[8,3,64,128]{3,2,1,0:T(8,128)S(1)} %all-to-all-done.3.refs_3_), channel_id=1, source_target_pairs={{0,24},{1,25},{2,26},{3,27},{4,28},{5,29},{6,30},{7,31}} | collective-permute-start | bytes 2359304 | tf_op jit(solution)/shard_map/ppermute | solution.py:617
  253.6 5.2 %collective-permute-done.28.refs_0_ = f32[8,3,64,128]{3,2,1,0:T(8,128)S(1)} collective-permute-done((f32[8,3,64,128]{3,2,1,0:T(8,128)S(1)}, f32[8,3,64,128]{3,2,1,0:T(8,128)S(1)}, u32[]{:S(2)}, u32[]{:S(2)}) %collective-permute-start.28) | collective-permute-done | bytes 786464 | tf_op jit(solution)/shard_map/ppermute | solution.py:617
  258.8 16.5 %collective-permute-done.30.refs_1_ = f32[8,3,64,128]{3,2,1,0:T(8,128)S(1)} collective-permute-done((f32[8,3,64,128]{3,2,1,0:T(8,128)S(1)}, f32[8,3,64,128]{3,2,1,0:T(8,128)S(1)}, u32[]{:S(2)}, u32[]{:S(2)}) %collective-permute-start.30) | collective-permute-done | bytes 786464 | tf_op jit(solution)/shard_map/ppermute | solution.py:617
  276.2 7.2 %to_output.1 = f32[1,3,128,2048]{3,2,1,0:T(8,128)} custom-call(s32[1]{0:T(128)} %bitcast.refs_0_.flag_ref, f32[32,3,64,128]{3,2,1,0:T(8,128)} %get-tuple-element.37.u_ref, f32[8,3,64,128]{3,2,1,0:T(8,128)} %copy-done.20, f32[8,3,64,128]{3,2,1,0:T(8,128)} %copy-done.21, f32[8,3,64,128]{3,2,1,0:T(8,128)} %copy-done.8, f32[8,3,64,128]{3,2,1,0:T(8,128)} %copy-done.9), custom_call_target="tpu_custom_call" | custom-call | tf_op jit(solution)/shard_map/to_output/pallas_call | solution.py:518
  (159 shorter events, 50.9 us)
Async XLA Ops:
  0.0 34.9 %copy-start = (s32[3,2]{0,1:T(2,128)S(1)}, s32[3,2]{0,1:T(2,128)}, u32[]{:S(2)}) copy-start(s32[3,2]{0,1:T(2,128)} %param.12) | copy-start | bytes 76
  5.5 17.1 %collective-permute-start.3 = (f32[3,32,128]{2,1,0:T(8,128)}, f32[3,32,128]{2,1,0:T(8,128)S(1)}, u32[]{:S(2)}, u32[]{:S(2)}) collective-permute-start(f32[3,32,128]{2,1,0:T(8,128)} %get-tuple-element.31), channel_id=1, source_target_pairs={{1,0},{2,1},{3,2},{5,4},{6,5},{7,6},{9,8},{10,9},{11,10},{13,12},{... | collective-permute-start | bytes 147464 | tf_op jit(solution)/shard_map/ppermute | solution.py:219
  6.8 16.5 %collective-permute-start.2 = (f32[3,32,128]{2,1,0:T(8,128)}, f32[3,32,128]{2,1,0:T(8,128)S(1)}, u32[]{:S(2)}, u32[]{:S(2)}) collective-permute-start(f32[3,32,128]{2,1,0:T(8,128)} %get-tuple-element.30), channel_id=1, source_target_pairs={{0,1},{1,2},{2,3},{4,5},{5,6},{6,7},{8,9},{9,10},{10,11},{12,13},{... | collective-permute-start | bytes 147464 | tf_op jit(solution)/shard_map/ppermute | solution.py:219
  9.8 11.6 %collective-permute-start.1 = (f32[64,128]{1,0:T(8,128)}, f32[64,128]{1,0:T(8,128)S(1)}, u32[]{:S(2)}, u32[]{:S(2)}) collective-permute-start(f32[64,128]{1,0:T(8,128)} %get-tuple-element.28.refs_0_), channel_id=1, source_target_pairs={{4,0},{5,1},{6,2},{7,3},{12,8},{13,9},{14,10},{15,11},{20,16},{21,... | collective-permute-start | bytes 98312 | tf_op jit(solution)/shard_map/ppermute | solution.py:219
  11.1 10.9 %collective-permute-start = (f32[64,128]{1,0:T(8,128)}, f32[64,128]{1,0:T(8,128)S(1)}, u32[]{:S(2)}, u32[]{:S(2)}) collective-permute-start(f32[64,128]{1,0:T(8,128)} %get-tuple-element.29), channel_id=1, source_target_pairs={{0,4},{1,5},{2,6},{3,7},{8,12},{9,13},{10,14},{11,15},{16,20},{17,... | collective-permute-start | bytes 98312 | tf_op jit(solution)/shard_map/ppermute | solution.py:219
  31.0 43.2 %all-to-all-start = ((f32[8,2,2,3,64,128]{5,4,3,2,1,0:T(8,128)}), f32[8,2,2,3,64,128]{5,4,3,2,1,0:T(8,128)S(1)}, u32[]{:S(2)}, u32[]{:S(2)}) async-start(f32[8,2,2,3,64,128]{5,4,3,2,1,0:T(8,128)} %flow.3.refs_6_), calls=%async_computation | async-start | bytes 6291456 | tf_op jit(solution)/shard_map/all_to_all | solution.py:552
  51.3 13.6 %collective-permute-start.6 = (f32[3,32,128]{2,1,0:T(8,128)}, f32[3,32,128]{2,1,0:T(8,128)S(1)}, u32[]{:S(2)}, u32[]{:S(2)}) collective-permute-start(f32[3,32,128]{2,1,0:T(8,128)} %get-tuple-element.35), channel_id=1, source_target_pairs={{0,1},{1,2},{2,3},{4,5},{5,6},{6,7},{8,9},{9,10},{10,11},{12,13},{... | collective-permute-start | bytes 147464 | tf_op jit(solution)/shard_map/ppermute | solution.py:219
  54.6 10.3 %collective-permute-start.7 = (f32[3,32,128]{2,1,0:T(8,128)}, f32[3,32,128]{2,1,0:T(8,128)S(1)}, u32[]{:S(2)}, u32[]{:S(2)}) collective-permute-start(f32[3,32,128]{2,1,0:T(8,128)} %get-tuple-element.36), channel_id=1, source_target_pairs={{1,0},{2,1},{3,2},{5,4},{6,5},{7,6},{9,8},{10,9},{11,10},{13,12},{... | collective-permute-start | bytes 147464 | tf_op jit(solution)/shard_map/ppermute | solution.py:219
  55.9 5.8 %collective-permute-start.4 = (f32[64,128]{1,0:T(8,128)}, f32[64,128]{1,0:T(8,128)S(1)}, u32[]{:S(2)}, u32[]{:S(2)}) collective-permute-start(f32[64,128]{1,0:T(8,128)} %get-tuple-element.33), channel_id=1, source_target_pairs={{0,4},{1,5},{2,6},{3,7},{8,12},{9,13},{10,14},{11,15},{16,20},{17,... | collective-permute-start | bytes 98312 | tf_op jit(solution)/shard_map/ppermute | solution.py:219
  58.6 6.3 %collective-permute-start.5 = (f32[64,128]{1,0:T(8,128)}, f32[64,128]{1,0:T(8,128)S(1)}, u32[]{:S(2)}, u32[]{:S(2)}) collective-permute-start(f32[64,128]{1,0:T(8,128)} %get-tuple-element.34), channel_id=1, source_target_pairs={{4,0},{5,1},{6,2},{7,3},{12,8},{13,9},{14,10},{15,11},{20,16},{21,... | collective-permute-start | bytes 98312 | tf_op jit(solution)/shard_map/ppermute | solution.py:219
  75.9 48.3 %all-to-all-start.1 = ((f32[8,2,2,3,64,128]{5,4,3,2,1,0:T(8,128)}), f32[8,2,2,3,64,128]{5,4,3,2,1,0:T(8,128)S(1)}, u32[]{:S(2)}, u32[]{:S(2)}) async-start(f32[8,2,2,3,64,128]{5,4,3,2,1,0:T(8,128)} %after.34), calls=%async_computation.1 | async-start | bytes 6291456 | tf_op jit(solution)/shard_map/all_to_all | solution.py:558
  90.0 22.2 %collective-permute-start.9 = (f32[3,256,256]{2,1,0:T(8,128)}, f32[3,256,256]{2,1,0:T(8,128)}, u32[]{:S(2)}, u32[]{:S(2)}) collective-permute-start(f32[3,256,256]{2,1,0:T(8,128)} %get-tuple-element.39.refs_3_), channel_id=1, source_target_pairs={{0,8},{24,16},{1,9},{25,17},{2,10},{26,18},{3,11},{27,19},{4,12},{... | collective-permute-start | bytes 2359304 | tf_op jit(solution)/shard_map/ppermute | solution.py:570
  98.8 34.8 %collective-permute-start.8 = (f32[3,256,256]{2,1,0:T(8,128)}, f32[3,256,256]{2,1,0:T(8,128)}, u32[]{:S(2)}, u32[]{:S(2)}) collective-permute-start(f32[3,256,256]{2,1,0:T(8,128)} %get-tuple-element.41.refs_1_), channel_id=1, source_target_pairs={{0,8},{24,16},{1,9},{25,17},{2,10},{26,18},{3,11},{27,19},{4,12},{... | collective-permute-start | bytes 2359304 | tf_op jit(solution)/shard_map/ppermute | solution.py:570
  114.5 23.4 %collective-permute-start.11 = (f32[3,256,256]{2,1,0:T(8,128)}, f32[3,256,256]{2,1,0:T(8,128)}, u32[]{:S(2)}, u32[]{:S(2)}) collective-permute-start(f32[3,256,256]{2,1,0:T(8,128)} %add.65.refs_3_), channel_id=1, source_target_pairs={{8,16},{16,8},{9,17},{17,9},{10,18},{18,10},{11,19},{19,11},{12,20... | collective-permute-start | bytes 2359304 | tf_op jit(solution)/shard_map/ppermute | solution.py:589
  129.2 20.2 %collective-permute-start.13 = (f32[3,256,256]{2,1,0:T(8,128)}, f32[3,256,256]{2,1,0:T(8,128)S(1)}, u32[]{:S(2)}, u32[]{:S(2)}) collective-permute-start(f32[3,256,256]{2,1,0:T(8,128)} %get-tuple-element.42.refs_1_), channel_id=1, source_target_pairs={{0,8},{1,9},{2,10},{3,11},{4,12},{5,13},{6,14},{7,15}} | collective-permute-start | bytes 2359304 | tf_op jit(solution)/shard_map/ppermute | solution.py:570
  135.9 18.1 %collective-permute-start.18 = (f32[2,3,128,256]{3,2,1,0:T(8,128)}, f32[2,3,128,256]{3,2,1,0:T(8,128)}, u32[]{:S(2)}, u32[]{:S(2)}) collective-permute-start(f32[2,3,128,256]{3,2,1,0:T(8,128)} %after.43), channel_id=1, source_target_pairs={{0,4},{4,0},{1,5},{5,1},{2,6},{6,2},{3,7},{7,3},{8,12},{12,8},{9,1... | collective-permute-start | bytes 2359304 | tf_op jit(solution)/shard_map/ppermute | solution.py:397
  136.7 4.8 %copy-start.16 = (f32[3,256,256]{2,1,0:T(8,128)S(1)}, f32[3,256,256]{2,1,0:T(8,128)}, u32[]{:S(2)}) copy-start(f32[3,256,256]{2,1,0:T(8,128)} %add.66.refs_1_) | copy-start | bytes 2359300
  136.7 17.9 %collective-permute-start.21 = (f32[4,3,64,256]{3,2,1,0:T(8,128)}, f32[4,3,64,256]{3,2,1,0:T(8,128)}, u32[]{:S(2)}, u32[]{:S(2)}) collective-permute-start(f32[4,3,64,256]{3,2,1,0:T(8,128)} %after.47), channel_id=1, source_target_pairs={{0,2},{1,3},{2,0},{3,1},{4,6},{5,7},{6,4},{7,5},{8,10},{9,11},{10,... | collective-permute-start | bytes 2359304 | tf_op jit(solution)/shard_map/ppermute | solution.py:398
  140.1 10.2 %copy-start.17 = (f32[3,256,256]{2,1,0:T(8,128)S(1)}, f32[3,256,256]{2,1,0:T(8,128)}, u32[]{:S(2)}) copy-start(f32[3,256,256]{2,1,0:T(8,128)} %get-tuple-element.42.refs_1_) | copy-start | bytes 2359300
  140.1 20.6 %collective-permute-start.12 = (f32[3,256,256]{2,1,0:T(8,128)}, f32[3,256,256]{2,1,0:T(8,128)S(1)}, u32[]{:S(2)}, u32[]{:S(2)}) collective-permute-start(f32[3,256,256]{2,1,0:T(8,128)} %add.67.refs_3_), channel_id=1, source_target_pairs={{8,0},{16,24},{9,1},{17,25},{10,2},{18,26},{11,3},{19,27},{12,4},{... | collective-permute-start | bytes 2359304 | tf_op jit(solution)/shard_map/ppermute | solution.py:594
  141.5 21.6 %collective-permute-start.10 = (f32[3,256,256]{2,1,0:T(8,128)S(1)}, f32[3,256,256]{2,1,0:T(8,128)}, u32[]{:S(2)}, u32[]{:S(2)}) collective-permute-start(f32[3,256,256]{2,1,0:T(8,128)S(1)} %copy-done.16), channel_id=1, source_target_pairs={{8,16},{16,8},{9,17},{17,9},{10,18},{18,10},{11,19},{19,11},{12,20... | collective-permute-start | bytes 2359304 | tf_op jit(solution)/shard_map/ppermute | solution.py:589
  149.4 17.3 %collective-permute-start.20 = (f32[4,3,64,256]{3,2,1,0:T(8,128)}, f32[4,3,64,256]{3,2,1,0:T(8,128)}, u32[]{:S(2)}, u32[]{:S(2)}) collective-permute-start(f32[4,3,64,256]{3,2,1,0:T(8,128)} %b0_ref.1), channel_id=1, source_target_pairs={{0,1},{1,0},{2,3},{3,2},{4,5},{5,4},{6,7},{7,6},{8,9},{9,8},{10,11... | collective-permute-start | bytes 2359304 | tf_op jit(solution)/shard_map/ppermute | solution.py:404
  152.5 10.7 %copy-start.7 = (f32[3,256,256]{2,1,0:T(8,128)S(1)}, f32[3,256,256]{2,1,0:T(8,128)}, u32[]{:S(2)}) copy-start(f32[3,256,256]{2,1,0:T(8,128)} %add.68.refs_1_) | copy-start | bytes 2359300
  154.1 11.3 %copy-start.10 = (f32[3,256,256]{2,1,0:T(8,128)S(1)}, f32[3,256,256]{2,1,0:T(8,128)}, u32[]{:S(2)}) copy-start(f32[3,256,256]{2,1,0:T(8,128)} %get-tuple-element.40.refs_6_) | copy-start | bytes 2359300
  154.1 14.0 %collective-permute-start.19 = (f32[2,3,128,256]{3,2,1,0:T(8,128)}, f32[2,3,128,256]{3,2,1,0:T(8,128)}, u32[]{:S(2)}, u32[]{:S(2)}) collective-permute-start(f32[2,3,128,256]{3,2,1,0:T(8,128)} %after.44.first_ref), channel_id=1, source_target_pairs={{0,1},{1,0},{2,3},{3,2},{4,5},{5,4},{6,7},{7,6},{8,9},{9,8},{10,11... | collective-permute-start | bytes 2359304 | tf_op jit(solution)/shard_map/ppermute | solution.py:404
  154.6 18.3 %collective-permute-start.22 = (f32[4,3,64,256]{3,2,1,0:T(8,128)}, f32[4,3,64,256]{3,2,1,0:T(8,128)}, u32[]{:S(2)}, u32[]{:S(2)}) collective-permute-start(f32[4,3,64,256]{3,2,1,0:T(8,128)} %after.48.b2_ref), channel_id=1, source_target_pairs={{0,1},{1,0},{2,3},{3,2},{4,5},{5,4},{6,7},{7,6},{8,9},{9,8},{10,11... | collective-permute-start | bytes 2359304 | tf_op jit(solution)/shard_map/ppermute | solution.py:404
  160.7 4.7 %copy-start.6 = (f32[3,256,256]{2,1,0:T(8,128)}, f32[3,256,256]{2,1,0:T(8,128)S(1)}, u32[]{:S(2)}) copy-start(f32[3,256,256]{2,1,0:T(8,128)S(1)} %collective-permute-done.12.refs_0_) | copy-start | bytes 2359300
  160.7 16.8 %collective-permute-start.24 = (f32[3,256,256]{2,1,0:T(8,128)}, f32[3,256,256]{2,1,0:T(8,128)}, u32[]{:S(2)}, u32[]{:S(2)}) collective-permute-start(f32[3,256,256]{2,1,0:T(8,128)} %get-tuple-element.44.refs_1_), channel_id=1, source_target_pairs={{0,8},{1,9},{2,10},{3,11},{4,12},{5,13},{6,14},{7,15}} | collective-permute-start | bytes 2359304 | tf_op jit(solution)/shard_map/ppermute | solution.py:570
  163.1 18.4 %collective-permute-start.23 = (f32[3,256,256]{2,1,0:T(8,128)S(1)}, f32[3,256,256]{2,1,0:T(8,128)}, u32[]{:S(2)}, u32[]{:S(2)}) collective-permute-start(f32[3,256,256]{2,1,0:T(8,128)S(1)} %copy-done.7), channel_id=1, source_target_pairs={{8,16},{16,8},{9,17},{17,9},{10,18},{18,10},{11,19},{19,11},{12,20... | collective-permute-start | bytes 2359304 | tf_op jit(solution)/shard_map/ppermute | solution.py:589
  166.7 27.7 %collective-permute-start.27 = (f32[3,256,256]{2,1,0:T(8,128)S(1)}, f32[3,256,256]{2,1,0:T(8,128)S(1)}, u32[]{:S(2)}, u32[]{:S(2)}) collective-permute-start(f32[3,256,256]{2,1,0:T(8,128)S(1)} %add.69.refs_1_), channel_id=1, source_target_pairs={{8,0},{16,24},{9,1},{17,25},{10,2},{18,26},{11,3},{19,27},{12,4},{... | collective-permute-start | bytes 2359304 | tf_op jit(solution)/shard_map/ppermute | solution.py:594
  177.5 4.1 %copy-start.12 = (f32[3,256,256]{2,1,0:T(8,128)S(1)}, f32[3,256,256]{2,1,0:T(8,128)}, u32[]{:S(2)}) copy-start(f32[3,256,256]{2,1,0:T(8,128)} %get-tuple-element.49.refs_6_) | copy-start | bytes 2359300
  179.9 21.9 %collective-permute-start.26 = (f32[3,256,256]{2,1,0:T(8,128)}, f32[3,256,256]{2,1,0:T(8,128)}, u32[]{:S(2)}, u32[]{:S(2)}) collective-permute-start(f32[3,256,256]{2,1,0:T(8,128)} %add.74.refs_1_), channel_id=1, source_target_pairs={{8,16},{16,8},{9,17},{17,9},{10,18},{18,10},{11,19},{19,11},{12,20... | collective-permute-start | bytes 2359304 | tf_op jit(solution)/shard_map/ppermute | solution.py:589
  181.5 4.4 %collective-permute-start.14 = (s32[64]{0:T(128)}, s32[64]{0:T(128)S(1)}, u32[]{:S(2)}, u32[]{:S(2)}) collective-permute-start(s32[64]{0:T(128)} %after.41), channel_id=1, source_target_pairs={{0,1},{1,0},{2,3},{3,2},{4,5},{5,4},{6,7},{7,6},{8,9},{9,8},{10,11... | collective-permute-start | bytes 776 | tf_op jit(solution)/shard_map/ppermute | solution.py:425
  183.8 23.5 %collective-permute-start.25 = (f32[3,256,256]{2,1,0:T(8,128)}, f32[3,256,256]{2,1,0:T(8,128)S(1)}, u32[]{:S(2)}, u32[]{:S(2)}) collective-permute-start(f32[3,256,256]{2,1,0:T(8,128)} %add.75.refs_1_), channel_id=1, source_target_pairs={{8,0},{16,24},{9,1},{17,25},{10,2},{18,26},{11,3},{19,27},{12,4},{... | collective-permute-start | bytes 2359304 | tf_op jit(solution)/shard_map/ppermute | solution.py:594
  185.3 3.6 %collective-permute-start.15 = (s32[64]{0:T(128)S(1)}, s32[64]{0:T(128)S(1)}, u32[]{:S(2)}, u32[]{:S(2)}) collective-permute-start(s32[64]{0:T(128)S(1)} %copy-done.30), channel_id=1, source_target_pairs={{0,2},{1,3},{2,0},{3,1},{4,6},{5,7},{6,4},{7,5},{8,10},{9,11},{10,... | collective-permute-start | bytes 776 | tf_op jit(solution)/shard_map/ppermute | solution.py:425
  185.9 4.1 %collective-permute-start.16 = (s32[64]{0:T(128)S(1)}, s32[64]{0:T(128)S(1)}, u32[]{:S(2)}, u32[]{:S(2)}) collective-permute-start(s32[64]{0:T(128)S(1)} %copy-done.30), channel_id=1, source_target_pairs={{0,3},{1,2},{2,1},{3,0},{4,7},{5,6},{6,5},{7,4},{8,11},{9,10},{10,... | collective-permute-start | bytes 776 | tf_op jit(solution)/shard_map/ppermute | solution.py:425
  188.9 3.6 %collective-permute-start.17 = (s32[128]{0:T(128)}, s32[128]{0:T(128)S(1)}, u32[]{:S(2)}, u32[]{:S(2)}) collective-permute-start(s32[128]{0:T(128)} %after.42), channel_id=1, source_target_pairs={{0,4},{4,0},{1,5},{5,1},{2,6},{6,2},{3,7},{7,3},{8,12},{12,8},{9,1... | collective-permute-start | bytes 1544 | tf_op jit(solution)/shard_map/ppermute | solution.py:425
  195.3 6.6 %copy-start.13 = (f32[3,256,256]{2,1,0:T(8,128)S(1)}, f32[3,256,256]{2,1,0:T(8,128)}, u32[]{:S(2)}) copy-start(f32[3,256,256]{2,1,0:T(8,128)} %get-tuple-element.50.refs_6_) | copy-start | bytes 2359300
  203.1 4.2 %copy-start.19 = (f32[3,256,256]{2,1,0:T(8,128)}, f32[3,256,256]{2,1,0:T(8,128)S(1)}, u32[]{:S(2)}) copy-start(f32[3,256,256]{2,1,0:T(8,128)S(1)} %add.76.refs_1_) | copy-start | bytes 2359300
  203.1 22.0 %collective-permute-start.29 = (f32[3,256,256]{2,1,0:T(8,128)S(1)}, f32[3,256,256]{2,1,0:T(8,128)S(1)}, u32[]{:S(2)}, u32[]{:S(2)}) collective-permute-start(f32[3,256,256]{2,1,0:T(8,128)S(1)} %add.76.refs_1_), channel_id=1, source_target_pairs={{8,0},{16,24},{9,1},{17,25},{10,2},{18,26},{11,3},{19,27},{12,4},{... | collective-permute-start | bytes 2359304 | tf_op jit(solution)/shard_map/ppermute | solution.py:594
  214.9 17.8 %all-to-all-start.2 = ((f32[8,3,64,128]{3,2,1,0:T(8,128)}), f32[8,3,64,128]{3,2,1,0:T(8,128)S(1)}, u32[]{:S(2)}, u32[]{:S(2)}) async-start(f32[8,3,64,128]{3,2,1,0:T(8,128)} %sweep.5.refs_1_), calls=%async_computation.2 | async-start | bytes 1572864 | tf_op jit(solution)/shard_map/all_to_all | solution.py:616
  232.7 42.6 %copy-start.8 = (f32[8,3,64,128]{3,2,1,0:T(8,128)}, f32[8,3,64,128]{3,2,1,0:T(8,128)S(1)}, u32[]{:S(2)}) copy-start(f32[8,3,64,128]{3,2,1,0:T(8,128)S(1)} %all-to-all-done.2.refs_2_) | copy-start | bytes 2359300
  232.7 16.5 %all-to-all-start.3 = ((f32[8,3,64,128]{3,2,1,0:T(8,128)}), f32[8,3,64,128]{3,2,1,0:T(8,128)S(1)}, u32[]{:S(2)}, u32[]{:S(2)}) async-start(f32[8,3,64,128]{3,2,1,0:T(8,128)} %sweep.7), calls=%async_computation.3 | async-start | bytes 1572864 | tf_op jit(solution)/shard_map/all_to_all | solution.py:616
  236.6 22.2 %collective-permute-start.28 = (f32[8,3,64,128]{3,2,1,0:T(8,128)S(1)}, f32[8,3,64,128]{3,2,1,0:T(8,128)S(1)}, u32[]{:S(2)}, u32[]{:S(2)}) collective-permute-start(f32[8,3,64,128]{3,2,1,0:T(8,128)S(1)} %all-to-all-done.2.refs_2_), channel_id=1, source_target_pairs={{0,24},{1,25},{2,26},{3,27},{4,28},{5,29},{6,30},{7,31}} | collective-permute-start | bytes 2359304 | tf_op jit(solution)/shard_map/ppermute | solution.py:617
  249.2 26.1 %copy-start.9 = (f32[8,3,64,128]{3,2,1,0:T(8,128)}, f32[8,3,64,128]{3,2,1,0:T(8,128)S(1)}, u32[]{:S(2)}) copy-start(f32[8,3,64,128]{3,2,1,0:T(8,128)S(1)} %all-to-all-done.3.refs_3_) | copy-start | bytes 2359300
  249.2 26.1 %collective-permute-start.30 = (f32[8,3,64,128]{3,2,1,0:T(8,128)S(1)}, f32[8,3,64,128]{3,2,1,0:T(8,128)S(1)}, u32[]{:S(2)}, u32[]{:S(2)}) collective-permute-start(f32[8,3,64,128]{3,2,1,0:T(8,128)S(1)} %all-to-all-done.3.refs_3_), channel_id=1, source_target_pairs={{0,24},{1,25},{2,26},{3,27},{4,28},{5,29},{6,30},{7,31}} | collective-permute-start | bytes 2359304 | tf_op jit(solution)/shard_map/ppermute | solution.py:617
  258.8 16.5 %copy-start.20 = (f32[8,3,64,128]{3,2,1,0:T(8,128)}, f32[8,3,64,128]{3,2,1,0:T(8,128)S(1)}, u32[]{:S(2)}) copy-start(f32[8,3,64,128]{3,2,1,0:T(8,128)S(1)} %collective-permute-done.28.refs_0_) | copy-start | bytes 2359300
  275.3 8.1 %copy-start.1 = (s32[3,2]{0,1:T(2,128)S(1)}, s32[3,2]{0,1:T(2,128)}, u32[]{:S(2)}) copy-start(s32[3,2]{0,1:T(2,128)} %param.12) | copy-start | bytes 76
  (18 other events, 22.5 us)

commit v4 on v3

--- a/solution.py
+++ b/solution.py
@@ -394,9 +394,10 @@
     core = lax.rem(lax.axis_index("gy"), 2)
     half = NCLASS // 2
     piece = lax.dynamic_slice_in_dim(x_ops, core * half, half, 0)
-    got_x = lax.ppermute(after(piece, earlier), "gx", [(0, 1), (1, 0)])
-    got_y = lax.ppermute(after(y_ops, earlier), "gy", [(i, i ^ 2) for i in range(4)])
-    return got_x, got_y
+    sent = [after(piece, earlier), after(y_ops, earlier)]
+    got_x = lax.ppermute(sent[0], "gx", [(0, 1), (1, 0)])
+    got_y = lax.ppermute(sent[1], "gy", [(i, i ^ 2) for i in range(4)])
+    return [got_x, got_y], sent
 
 
 def paired_ops(y_ops, got_x, got_y):
@@ -556,23 +557,21 @@
     lamb, planes = flow(flag, planes, halo, (), groups, ("lamb", "next"))
     gots[0] = after(gots[0], [lamb])
     gots.append(lax.all_to_all(after(lamb, [gots[0]]), ("gx", "gy"), 0, 0))
-    fetched = list(fetched_ops(x_ops, y_ops, [gots[1]]))
+    fetched, taken = fetched_ops(x_ops, y_ops, [planes])
 
     total = STEPS * CHUNKS
     fars, nears, firsts, seconds, thirds, ends = ([None] * total for _ in range(6))
-    lines, beside, parts = [], [], []
-    token = []
+    lines = gathered_classes(x_line_class, y_line_class)
+    beside, parts = [], []
+    token = list(lines)
 
     def placed(n):
         first = n < CHUNKS
         got = gots[n // CHUNKS]
-        fars[n], nears[n] = place(ints, matrix, got, n % CHUNKS, token, gx, gy, first)
+        waits = token + taken if n == CHUNKS else token
+        fars[n], nears[n] = place(ints, matrix, got, n % CHUNKS, waits, gx, gy, first)
         firsts[n] = lax.ppermute(fars[n], "sec", [(0, 1), (3, 2)] if first else [(0, 1)])
         return [fars[n]]
-
-    def classes(n):
-        lines.extend(gathered_classes(after(x_line_class, token), after(y_line_class, token)))
-        return token
 
     def paired(n):
         fetched[:] = [after(value, token) for value in fetched]
@@ -607,9 +606,9 @@
 
     order = (
         (placed, 0), (placed, 1), (first_hop, 0), (placed, 2), (first_hop, 1), (second_hop, 0),
-        (placed, 3), (first_hop, 2), (paired, 0), (arrived, 0), (second_hop, 1), (classes, 0),
-        (prepared, 0), (first_hop, 3), (second_hop, 2), (arrived, 1), (swept, 0),
-        (second_hop, 3), (swept, 2), (swept, 1), (swept, 3),
+        (placed, 3), (first_hop, 2), (second_hop, 1), (arrived, 0), (paired, 0), (first_hop, 3),
+        (second_hop, 2), (arrived, 1), (prepared, 0), (swept, 0), (second_hop, 3),
+        (swept, 2), (swept, 1), (swept, 3),
     )
     for work, n in order:
         token = work(n)

time: 285 us -> 279 us (0.979)
  waiting for transfers between devices: 67.1 us -> 57.9 us
  starting transfers between devices: 80.4 us -> 88.9 us
  local copies, waits for them, and re-layouts: 20.2 us -> 15.9 us
    ppermute x4, starting transfers between devices: 3.06 us -> 14.8 us  [rows(): lax.ppermute(value, axis, [(i, i ^ step) for i in range(count)])]
    all_to_all x1, starting transfers between devices: 10.4 us -> 3.65 us  [local(): gots.append(lax.all_to_all(after(lamb, [gots[0]]), ('gx', 'gy'), 0, 0))]
    ppermute x4, starting transfers between devices: 14.1 us -> 19.2 us  [placed(): lax.ppermute(fars[n], 'sec', [(0, 1), (3, 2)] if first else [(0, 1)])]
    ppermute x8, waiting for transfers between devices: 5.04 us -> 0.02 us  [send(): lax.ppermute(value, axis, [(i, i + step) for i in range(count) if 0 <= i...]
    unnamed x65, local copies, waits for them, and re-layouts: 15.5 us -> 11.3 us
    ppermute x4, waiting for transfers between devices: 14.3 us -> 18.1 us  [placed(): lax.ppermute(fars[n], 'sec', [(0, 1), (3, 2)] if first else [(0, 1)])]
    ppermute x2, starting transfers between devices: 8.82 us -> 5.04 us  [local(): brought = [lax.ppermute(value, 'sec', [(0, 3)]) for value in tiles]]
    all_to_all x1, waiting for transfers between devices: 3.83 us -> 0.95 us  [local(): gots.append(lax.all_to_all(after(lamb, [gots[0]]), ('gx', 'gy'), 0, 0))]
  transfers between devices with their start and end apart: 35 -> 35, of which waited for: 16 -> 8; matrix products, arithmetic and copies ran while one was open for 10% -> 10% of each run, Pallas kernels for 27% -> 28%
where the time goes in v4:
time: 279 us; the launch traced here: 277 us
  Pallas kernels  93.9 us (34%)
  starting transfers between devices  88.9 us (32%)
  waiting for transfers between devices  57.9 us (21%)
  other arithmetic  19.9 us (7%)
  local copies, waits for them, and re-layouts  15.9 us (6%)
    pallas_call x3, Pallas kernels, flow(): pl.pallas_call(body, grid=(groups,), in_specs=[pl.BlockSpec(memory_space=...  28.4 us
    pallas_call x4, Pallas kernels, sweep(): pl.pallas_call(body, grid=(3,), in_specs=[pl.BlockSpec((full_y, 1), lambd...  26.3 us
    ppermute x2, waiting for transfers between devices, local(): brought = [lax.ppermute(value, 'sec', [(0, 3)]) for value in tiles]  21.8 us
    ppermute x4, starting transfers between devices, placed(): lax.ppermute(fars[n], 'sec', [(0, 1), (3, 2)] if first else [(0, 1)])  19.2 us
    ppermute x8, starting transfers between devices, send(): lax.ppermute(value, axis, [(i, i + step) for i in range(count) if 0 <= i...  19 us
    ppermute x4, waiting for transfers between devices, placed(): lax.ppermute(fars[n], 'sec', [(0, 1), (3, 2)] if first else [(0, 1)])  18.1 us
    ppermute x4, starting transfers between devices, rows(): lax.ppermute(value, axis, [(i, i ^ step) for i in range(count)])  14.8 us
    pallas_call x4, Pallas kernels, place(): pl.pallas_call(body, grid=(1,), in_specs=[pl.BlockSpec(memory_space=pltpu...  14.2 us
  transfers between devices with their start and end apart: 35, of which 8 were waited for; matrix products, arithmetic and copies ran while one was open for 10% of the time, Pallas kernels for 28%

profile of v4, /device:TPU:0, one launch (start us, length us, event | category | flops | bytes accessed | tf_op | source)
XLA Modules:
  0.0 276.9 jit_solution(407409852007304484)
XLA Ops:
  0.0 3.0 %tile_edges.1 = (f32[64,128]{1,0:T(8,128)}, f32[64,128]{1,0:T(8,128)}, f32[3,32,128]{2,1,0:T(8,128)}, f32[3,32,128]{2,1,0:T(8,128)}) custom-call(f32[3,128,2048]{2,1,0:T(8,128)} %bitcast.21, f32[3,128,2048]{2,1,0:T(8,128)} %bitcast.22, f32[3,128,2048]{2,1,0:T(8,128)} %bitcast.23, f32[3,128,2048]{2,1,0:T(8,128)} %bitcast.24), custom_call_target="tpu_custom_call" | custom-call | tf_op jit(solution)/shard_map/tile_edges/pallas_call | solution.py:56
  4.3 3.0 %collective-permute-start.2 = (f32[3,32,128]{2,1,0:T(8,128)}, f32[3,32,128]{2,1,0:T(8,128)S(1)}, u32[]{:S(2)}, u32[]{:S(2)}) collective-permute-start(f32[3,32,128]{2,1,0:T(8,128)} %get-tuple-element.30), channel_id=1, source_target_pairs={{0,1},{1,2},{2,3},{4,5},{5,6},{6,7},{8,9},{9,10},{10,11},{12,13},{... | collective-permute-start | bytes 147464 | tf_op jit(solution)/shard_map/ppermute | solution.py:219
  8.7 4.9 %collective-permute-start = (f32[64,128]{1,0:T(8,128)}, f32[64,128]{1,0:T(8,128)S(1)}, u32[]{:S(2)}, u32[]{:S(2)}) collective-permute-start(f32[64,128]{1,0:T(8,128)} %get-tuple-element.29), channel_id=1, source_target_pairs={{0,4},{1,5},{2,6},{3,7},{8,12},{9,13},{10,14},{11,15},{16,20},{17,... | collective-permute-start | bytes 98312 | tf_op jit(solution)/shard_map/ppermute | solution.py:219
  13.5 5.4 %to_planes.1.refs_1_ = f32[32,3,64,128]{3,2,1,0:T(8,128)} custom-call(f32[3,128,2048]{2,1,0:T(8,128)} %bitcast.25, f32[64,128]{1,0:T(8,128)} %get-tuple-element.28.refs_0_), custom_call_target="tpu_custom_call" | custom-call | tf_op jit(solution)/shard_map/to_planes/pallas_call | solution.py:89
  21.4 7.1 %flow.3.refs_6_ = f32[8,2,2,3,64,128]{5,4,3,2,1,0:T(8,128)} custom-call(s32[1]{0:T(128)} %bitcast.refs_0_.flag_ref, f32[32,3,64,128]{3,2,1,0:T(8,128)} %to_planes.1.refs_1_, f32[64,128]{1,0:T(8,128)} %after.27.refs_2_, f32[64,128]{1,0:T(8,128)} %after.28.refs_3_, f32[3,32,128]{2,1,0:T(8,128)} %after.29.refs_4_, f32[3,32,128]{2,1,0:T(8,128)} %after.30.refs_5_), custom_call_target="tpu_custom_call" | custom-call | tf_op jit(solution)/shard_map/flow/pallas_call | solution.py:197
  28.5 3.9 %all-to-all-start = ((f32[8,2,2,3,64,128]{5,4,3,2,1,0:T(8,128)}), f32[8,2,2,3,64,128]{5,4,3,2,1,0:T(8,128)S(1)}, u32[]{:S(2)}, u32[]{:S(2)}) async-start(f32[8,2,2,3,64,128]{5,4,3,2,1,0:T(8,128)} %flow.3.refs_6_), calls=%async_computation | async-start | bytes 6291456 | tf_op jit(solution)/shard_map/all_to_all | solution.py:553
  33.1 1.9 pad_add_fusion.2.refs_7_.refs_0_
  36.1 12.6 %flow.4 = (f32[32,3,64,128]{3,2,1,0:T(8,128)}, f32[64,128]{1,0:T(8,128)}, f32[64,128]{1,0:T(8,128)}, f32[3,32,128]{2,1,0:T(8,128)}, f32[3,32,128]{2,1,0:T(8,128)}) custom-call(s32[1]{0:T(128)} %bitcast.refs_0_.flag_ref, f32[32,3,64,128]{3,2,1,0:T(8,128)} %to_planes.1.refs_1_, f32[64,128]{1,0:T(8,128)} %after.27.refs_2_, f32[64,128]{1,0:T(8,128)} %after.28.refs_3_, ...), custom_call_target="tpu_custom_call" | custom-call | tf_op jit(solution)/shard_map/flow/pallas_call | solution.py:197
  48.8 3.3 %collective-permute-start.6 = (f32[3,32,128]{2,1,0:T(8,128)}, f32[3,32,128]{2,1,0:T(8,128)S(1)}, u32[]{:S(2)}, u32[]{:S(2)}) collective-permute-start(f32[3,32,128]{2,1,0:T(8,128)} %get-tuple-element.35), channel_id=1, source_target_pairs={{0,1},{1,2},{2,3},{4,5},{5,6},{6,7},{8,9},{9,10},{10,11},{12,13},{... | collective-permute-start | bytes 147464 | tf_op jit(solution)/shard_map/ppermute | solution.py:219
  53.4 2.7 collective-permute-start.4
  57.4 1.8 collective-permute-start.8
  59.2 10.1 %collective-permute-start.10 = (s32[64]{0:T(128)S(1)}, s32[64]{0:T(128)S(1)}, u32[]{:S(2)}, u32[]{:S(2)}) collective-permute-start(s32[64]{0:T(128)S(1)} %copy-done.31), channel_id=1, source_target_pairs={{0,3},{1,2},{2,1},{3,0},{4,7},{5,6},{6,5},{7,4},{8,11},{9,10},{10,... | collective-permute-start | bytes 776 | tf_op jit(solution)/shard_map/ppermute | solution.py:426
  69.3 2.2 collective-permute-start.9
  72.8 8.6 %flow.5 = (f32[8,2,2,3,64,128]{5,4,3,2,1,0:T(8,128)}, f32[32,3,64,128]{3,2,1,0:T(8,128)}) custom-call(s32[1]{0:T(128)} %bitcast.refs_0_.flag_ref, f32[32,3,64,128]{3,2,1,0:T(8,128)} %get-tuple-element.32.refs_1_, f32[64,128]{1,0:T(8,128)} %copy-done.28, f32[64,128]{1,0:T(8,128)} %copy-done.29, f32[3,32,128]{2,1,0:T(8,128)} %copy-done.26, ...), custom_call_target="tpu_custom_call" | custom-call | tf_op jit(solution)/shard_map/flow/pallas_call | solution.py:197
  83.2 3.7 %all-to-all-start.1 = ((f32[8,2,2,3,64,128]{5,4,3,2,1,0:T(8,128)}), f32[8,2,2,3,64,128]{5,4,3,2,1,0:T(8,128)S(1)}, u32[]{:S(2)}, u32[]{:S(2)}) async-start(f32[8,2,2,3,64,128]{5,4,3,2,1,0:T(8,128)} %after.34), calls=%async_computation.1 | async-start | bytes 6291456 | tf_op jit(solution)/shard_map/all_to_all | solution.py:559
  89.6 3.6 %place.4 = (f32[3,256,256]{2,1,0:T(8,128)}, f32[3,256,256]{2,1,0:T(8,128)}) custom-call(s32[4]{0:T(128)} %pad_add_fusion.2.refs_7_.refs_0_, f32[3,3]{1,0:T(4,128)} %select_bitcast_fusion.refs_8_.refs_1_, f32[8,2,2,3,64,128]{5,4,3,2,1,0:T(8,128)} %after.32.refs_2_.refs_1_, s32[256,1]{1,0:T(8,128)} %select_n.92.refs_3_.refs_0_, s32[1,256]{1,0:T(1,128)} %bitcast.26), custom_call_target="tpu_custom_call" | custom-call | tf_op jit(solution)/shard_map/place/pallas_call | solution.py:303
  93.2 5.1 %collective-permute-start.13 = (f32[3,256,256]{2,1,0:T(8,128)}, f32[3,256,256]{2,1,0:T(8,128)}, u32[]{:S(2)}, u32[]{:S(2)}) collective-permute-start(f32[3,256,256]{2,1,0:T(8,128)} %get-tuple-element.40.refs_3_), channel_id=1, source_target_pairs={{0,8},{24,16},{1,9},{25,17},{2,10},{26,18},{3,11},{27,19},{4,12},{... | collective-permute-start | bytes 2359304 | tf_op jit(solution)/shard_map/ppermute | solution.py:573
  98.3 3.7 %place.5 = (f32[3,256,256]{2,1,0:T(8,128)}, f32[3,256,256]{2,1,0:T(8,128)}) custom-call(s32[4]{0:T(128)} %pad_add_fusion.2.refs_7_.refs_0_, f32[3,3]{1,0:T(4,128)} %select_bitcast_fusion.refs_8_.refs_1_, f32[8,2,2,3,64,128]{5,4,3,2,1,0:T(8,128)} %after.32.refs_2_.refs_1_, f32[3,256,256]{2,1,0:T(8,128)} %get-tuple-element.40.refs_3_), custom_call_target="tpu_custom_call" | custom-call | tf_op jit(solution)/shard_map/place/pallas_call | solution.py:303
  102.0 2.2 collective-permute-start.15
  104.2 11.4 %collective-permute-done.13.refs_0_ = f32[3,256,256]{2,1,0:T(8,128)} collective-permute-done((f32[3,256,256]{2,1,0:T(8,128)}, f32[3,256,256]{2,1,0:T(8,128)}, u32[]{:S(2)}, u32[]{:S(2)}) %collective-permute-start.13) | collective-permute-done | bytes 786464 | tf_op jit(solution)/shard_map/ppermute | solution.py:573
  115.6 2.4 add.69.refs_3_
  119.5 2.1 copy.48.refs_0_
  121.6 2.1 constant_dynamic-slice_fusion.refs_0_
  126.3 3.4 %place.6 = (f32[3,256,256]{2,1,0:T(8,128)}, f32[3,256,256]{2,1,0:T(8,128)}) custom-call(s32[4]{0:T(128)} %pad_add_fusion.2.refs_7_.refs_0_, f32[3,3]{1,0:T(4,128)} %select_bitcast_fusion.refs_8_.refs_1_, f32[8,2,2,3,64,128]{5,4,3,2,1,0:T(8,128)} %copy-done.3, f32[3,256,256]{2,1,0:T(8,128)} %add.69.refs_3_, f32[2,3,128,256]{3,2,1,0:T(8,128)} %after.31.refs_4_, ...), custom_call_target="tpu_custom_call" | custom-call | tf_op jit(solution)/shard_map/place/pallas_call | solution.py:303
  129.8 6.5 %collective-permute-start.18 = (f32[3,256,256]{2,1,0:T(8,128)}, f32[3,256,256]{2,1,0:T(8,128)}, u32[]{:S(2)}, u32[]{:S(2)}) collective-permute-start(f32[3,256,256]{2,1,0:T(8,128)} %get-tuple-element.42.refs_1_), channel_id=1, source_target_pairs={{0,8},{1,9},{2,10},{3,11},{4,12},{5,13},{6,14},{7,15}} | collective-permute-start | bytes 2359304 | tf_op jit(solution)/shard_map/ppermute | solution.py:573
  136.2 2.5 add.70.refs_1_
  140.3 2.2 add.71.refs_3_
  143.8 2.0 collective-permute-start.12
  147.2 3.4 %place.7 = (f32[3,256,256]{2,1,0:T(8,128)}, f32[3,256,256]{2,1,0:T(8,128)}) custom-call(s32[4]{0:T(128)} %pad_add_fusion.2.refs_7_.refs_0_, f32[3,3]{1,0:T(4,128)} %select_bitcast_fusion.refs_8_.refs_1_, f32[8,2,2,3,64,128]{5,4,3,2,1,0:T(8,128)} %copy-done.3, f32[3,256,256]{2,1,0:T(8,128)} %add.71.refs_3_), custom_call_target="tpu_custom_call" | custom-call | tf_op jit(solution)/shard_map/place/pallas_call | solution.py:303
  151.3 5.5 %collective-permute-start.22 = (f32[3,256,256]{2,1,0:T(8,128)}, f32[3,256,256]{2,1,0:T(8,128)}, u32[]{:S(2)}, u32[]{:S(2)}) collective-permute-start(f32[3,256,256]{2,1,0:T(8,128)} %get-tuple-element.44.refs_1_), channel_id=1, source_target_pairs={{0,8},{1,9},{2,10},{3,11},{4,12},{5,13},{6,14},{7,15}} | collective-permute-start | bytes 2359304 | tf_op jit(solution)/shard_map/ppermute | solution.py:573
  156.7 2.3 add.72.refs_1_
  160.7 2.2 add.73.refs_1_
  164.8 6.1 %collective-permute-done.22.refs_0_ = f32[3,256,256]{2,1,0:T(8,128)} collective-permute-done((f32[3,256,256]{2,1,0:T(8,128)}, f32[3,256,256]{2,1,0:T(8,128)}, u32[]{:S(2)}, u32[]{:S(2)}) %collective-permute-start.22) | collective-permute-done | bytes 786464 | tf_op jit(solution)/shard_map/ppermute | solution.py:573
  175.1 6.8 %collective-permute-done.20.refs_0_ = f32[3,256,256]{2,1,0:T(8,128)S(1)} collective-permute-done((f32[3,256,256]{2,1,0:T(8,128)}, f32[3,256,256]{2,1,0:T(8,128)S(1)}, u32[]{:S(2)}, u32[]{:S(2)}) %collective-permute-start.20) | collective-permute-done | bytes 786464 | tf_op jit(solution)/shard_map/ppermute | solution.py:593
  184.0 4.9 %x_operators.1 = (bf16[4,3,256,256]{3,2,1,0:T(8,128)(2,1)}, bf16[4,3,256,256]{3,2,1,0:T(8,128)(2,1)}) custom-call(s32[3]{0:T(128)} %pad_add_fusion.3.pos_ref, f32[4,3,128,256]{3,2,1,0:T(8,128)} %mine_ref.1, f32[2,3,128,256]{3,2,1,0:T(8,128)} %after.41.first_ref, f32[2,3,128,256]{3,2,1,0:T(8,128)} %after.45.second_ref), custom_call_target="tpu_custom_call" | custom-call | tf_op jit(solution)/shard_map/x_operators/pallas_call | solution.py:382
  188.9 4.5 %y_operators.1 = (bf16[4,3,256,256]{3,2,1,0:T(8,128)(2,1)}, bf16[4,3,256,256]{3,2,1,0:T(8,128)(2,1)}) custom-call(s32[3]{0:T(128)} %pad_add_fusion.3.pos_ref, f32[4,3,64,256]{3,2,1,0:T(8,128)} %b0_ref.1, f32[4,3,64,256]{3,2,1,0:T(8,128)} %after.46.b1_ref, f32[4,3,64,256]{3,2,1,0:T(8,128)} %after.47.b2_ref, f32[4,3,64,256]{3,2,1,0:T(8,128)} %after.48.b3_ref), custom_call_target="tpu_custom_call" | custom-call | tf_op jit(solution)/shard_map/y_operators/pallas_call | solution.py:382
  193.4 6.5 %sweep.4.refs_1_.refs_8_ = f32[3,256,256]{2,1,0:T(8,128)} custom-call(s32[256,1]{1,0:T(8,128)} %select_n.92.refs_3_.refs_0_, s32[1,256]{1,0:T(1,128)} %bitcast.27, bf16[4,3,256,256]{3,2,1,0:T(8,128)(2,1)} %get-tuple-element.46.refs_1_.refs_2_, bf16[4,3,256,256]{3,2,1,0:T(8,128)(2,1)} %get-tuple-element.47.refs_2_.refs_3_, ...), custom_call_target="tpu_custom_call" | custom-call | tf_op jit(solution)/shard_map/sweep/pallas_call | solution.py:479
  203.5 6.6 %sweep.5.refs_1_ = f32[8,3,64,128]{3,2,1,0:T(8,128)} custom-call(s32[256,1]{1,0:T(8,128)} %select_n.92.refs_3_.refs_0_, s32[1,256]{1,0:T(1,128)} %bitcast.28, bf16[4,3,256,256]{3,2,1,0:T(8,128)(2,1)} %get-tuple-element.46.refs_1_.refs_2_, bf16[4,3,256,256]{3,2,1,0:T(8,128)(2,1)} %get-tuple-element.47.refs_2_.refs_3_, ...), custom_call_target="tpu_custom_call" | custom-call | tf_op jit(solution)/shard_map/sweep/pallas_call | solution.py:479
  210.2 3.5 %all-to-all-start.2 = ((f32[8,3,64,128]{3,2,1,0:T(8,128)}), f32[8,3,64,128]{3,2,1,0:T(8,128)S(1)}, u32[]{:S(2)}, u32[]{:S(2)}) async-start(f32[8,3,64,128]{3,2,1,0:T(8,128)} %sweep.5.refs_1_), calls=%async_computation.2 | async-start | bytes 1572864 | tf_op jit(solution)/shard_map/all_to_all | solution.py:615
  213.7 6.5 %sweep.6.refs_1_.refs_8_ = f32[3,256,256]{2,1,0:T(8,128)} custom-call(s32[256,1]{1,0:T(8,128)} %select_n.92.refs_3_.refs_0_, s32[1,256]{1,0:T(1,128)} %bitcast.29, bf16[4,3,256,256]{3,2,1,0:T(8,128)(2,1)} %get-tuple-element.46.refs_1_.refs_2_, bf16[4,3,256,256]{3,2,1,0:T(8,128)(2,1)} %get-tuple-element.47.refs_2_.refs_3_, ...), custom_call_target="tpu_custom_call" | custom-call | tf_op jit(solution)/shard_map/sweep/pallas_call | solution.py:479
  221.1 6.6 %sweep.7 = f32[8,3,64,128]{3,2,1,0:T(8,128)} custom-call(s32[256,1]{1,0:T(8,128)} %select_n.92.refs_3_.refs_0_, s32[1,256]{1,0:T(1,128)} %bitcast.30, bf16[4,3,256,256]{3,2,1,0:T(8,128)(2,1)} %get-tuple-element.46.refs_1_.refs_2_, bf16[4,3,256,256]{3,2,1,0:T(8,128)(2,1)} %get-tuple-element.47.refs_2_.refs_3_, ...), custom_call_target="tpu_custom_call" | custom-call | tf_op jit(solution)/shard_map/sweep/pallas_call | solution.py:479
  227.8 4.1 %all-to-all-start.3 = ((f32[8,3,64,128]{3,2,1,0:T(8,128)}), f32[8,3,64,128]{3,2,1,0:T(8,128)S(1)}, u32[]{:S(2)}, u32[]{:S(2)}) async-start(f32[8,3,64,128]{3,2,1,0:T(8,128)} %sweep.7), calls=%async_computation.3 | async-start | bytes 1572864 | tf_op jit(solution)/shard_map/all_to_all | solution.py:615
  231.9 2.5 collective-permute-start.28
  234.5 10.1 %all-to-all-done.3.refs_3_ = f32[8,3,64,128]{3,2,1,0:T(8,128)S(1)} async-done(((f32[8,3,64,128]{3,2,1,0:T(8,128)}), f32[8,3,64,128]{3,2,1,0:T(8,128)S(1)}, u32[]{:S(2)}, u32[]{:S(2)}) %all-to-all-start.3) | async-done | bytes 786464 | tf_op jit(solution)/shard_map/all_to_all | solution.py:615
  244.5 2.5 collective-permute-start.30
  247.1 5.2 %collective-permute-done.28.refs_0_ = f32[8,3,64,128]{3,2,1,0:T(8,128)S(1)} collective-permute-done((f32[8,3,64,128]{3,2,1,0:T(8,128)S(1)}, f32[8,3,64,128]{3,2,1,0:T(8,128)S(1)}, u32[]{:S(2)}, u32[]{:S(2)}) %collective-permute-start.28) | collective-permute-done | bytes 786464 | tf_op jit(solution)/shard_map/ppermute | solution.py:616
  252.2 16.6 %collective-permute-done.30.refs_1_ = f32[8,3,64,128]{3,2,1,0:T(8,128)S(1)} collective-permute-done((f32[8,3,64,128]{3,2,1,0:T(8,128)S(1)}, f32[8,3,64,128]{3,2,1,0:T(8,128)S(1)}, u32[]{:S(2)}, u32[]{:S(2)}) %collective-permute-start.30) | collective-permute-done | bytes 786464 | tf_op jit(solution)/shard_map/ppermute | solution.py:616
  269.7 7.2 %to_output.1 = f32[1,3,128,2048]{3,2,1,0:T(8,128)} custom-call(s32[1]{0:T(128)} %bitcast.refs_0_.flag_ref, f32[32,3,64,128]{3,2,1,0:T(8,128)} %get-tuple-element.37.refs_1_.u_ref, f32[8,3,64,128]{3,2,1,0:T(8,128)} %copy-done.20, f32[8,3,64,128]{3,2,1,0:T(8,128)} %copy-done.21, f32[8,3,64,128]{3,2,1,0:T(8,128)} %copy-done.8, f32[8,3,64,128]{3,2,1,0:T(8,128)} %copy-done.9), custom_call_target="tpu_custom_call" | custom-call | tf_op jit(solution)/shard_map/to_output/pallas_call | solution.py:519
  (157 shorter events, 39.3 us)
Async XLA Ops:
  0.0 32.4 %copy-start = (s32[3,2]{0,1:T(2,128)S(1)}, s32[3,2]{0,1:T(2,128)}, u32[]{:S(2)}) copy-start(s32[3,2]{0,1:T(2,128)} %param.12) | copy-start | bytes 76
  3.0 17.1 %collective-permute-start.3 = (f32[3,32,128]{2,1,0:T(8,128)}, f32[3,32,128]{2,1,0:T(8,128)S(1)}, u32[]{:S(2)}, u32[]{:S(2)}) collective-permute-start(f32[3,32,128]{2,1,0:T(8,128)} %get-tuple-element.31), channel_id=1, source_target_pairs={{1,0},{2,1},{3,2},{5,4},{6,5},{7,6},{9,8},{10,9},{11,10},{13,12},{... | collective-permute-start | bytes 147464 | tf_op jit(solution)/shard_map/ppermute | solution.py:219
  4.3 16.5 %collective-permute-start.2 = (f32[3,32,128]{2,1,0:T(8,128)}, f32[3,32,128]{2,1,0:T(8,128)S(1)}, u32[]{:S(2)}, u32[]{:S(2)}) collective-permute-start(f32[3,32,128]{2,1,0:T(8,128)} %get-tuple-element.30), channel_id=1, source_target_pairs={{0,1},{1,2},{2,3},{4,5},{5,6},{6,7},{8,9},{9,10},{10,11},{12,13},{... | collective-permute-start | bytes 147464 | tf_op jit(solution)/shard_map/ppermute | solution.py:219
  7.4 11.6 %collective-permute-start.1 = (f32[64,128]{1,0:T(8,128)}, f32[64,128]{1,0:T(8,128)S(1)}, u32[]{:S(2)}, u32[]{:S(2)}) collective-permute-start(f32[64,128]{1,0:T(8,128)} %get-tuple-element.28.refs_0_), channel_id=1, source_target_pairs={{4,0},{5,1},{6,2},{7,3},{12,8},{13,9},{14,10},{15,11},{20,16},{21,... | collective-permute-start | bytes 98312 | tf_op jit(solution)/shard_map/ppermute | solution.py:219
  8.7 10.9 %collective-permute-start = (f32[64,128]{1,0:T(8,128)}, f32[64,128]{1,0:T(8,128)S(1)}, u32[]{:S(2)}, u32[]{:S(2)}) collective-permute-start(f32[64,128]{1,0:T(8,128)} %get-tuple-element.29), channel_id=1, source_target_pairs={{0,4},{1,5},{2,6},{3,7},{8,12},{9,13},{10,14},{11,15},{16,20},{17,... | collective-permute-start | bytes 98312 | tf_op jit(solution)/shard_map/ppermute | solution.py:219
  28.5 52.9 %all-to-all-start = ((f32[8,2,2,3,64,128]{5,4,3,2,1,0:T(8,128)}), f32[8,2,2,3,64,128]{5,4,3,2,1,0:T(8,128)S(1)}, u32[]{:S(2)}, u32[]{:S(2)}) async-start(f32[8,2,2,3,64,128]{5,4,3,2,1,0:T(8,128)} %flow.3.refs_6_), calls=%async_computation | async-start | bytes 6291456 | tf_op jit(solution)/shard_map/all_to_all | solution.py:553
  36.1 21.2 %copy-start.31 = (s32[64]{0:T(128)S(1)}, s32[64]{0:T(128)}, u32[]{:S(2)}) copy-start(s32[64]{0:T(128)} %param.10) | copy-start | bytes 772
  36.1 35.4 %copy-start.30 = (s32[128]{0:T(128)S(1)}, s32[128]{0:T(128)}, u32[]{:S(2)}) copy-start(s32[128]{0:T(128)} %param.11) | copy-start | bytes 1540
  48.8 22.8 %collective-permute-start.6 = (f32[3,32,128]{2,1,0:T(8,128)}, f32[3,32,128]{2,1,0:T(8,128)S(1)}, u32[]{:S(2)}, u32[]{:S(2)}) collective-permute-start(f32[3,32,128]{2,1,0:T(8,128)} %get-tuple-element.35), channel_id=1, source_target_pairs={{0,1},{1,2},{2,3},{4,5},{5,6},{6,7},{8,9},{9,10},{10,11},{12,13},{... | collective-permute-start | bytes 147464 | tf_op jit(solution)/shard_map/ppermute | solution.py:219
  52.1 20.1 %collective-permute-start.7 = (f32[3,32,128]{2,1,0:T(8,128)}, f32[3,32,128]{2,1,0:T(8,128)S(1)}, u32[]{:S(2)}, u32[]{:S(2)}) collective-permute-start(f32[3,32,128]{2,1,0:T(8,128)} %get-tuple-element.36), channel_id=1, source_target_pairs={{1,0},{2,1},{3,2},{5,4},{6,5},{7,6},{9,8},{10,9},{11,10},{13,12},{... | collective-permute-start | bytes 147464 | tf_op jit(solution)/shard_map/ppermute | solution.py:219
  53.4 5.8 %collective-permute-start.4 = (f32[64,128]{1,0:T(8,128)}, f32[64,128]{1,0:T(8,128)S(1)}, u32[]{:S(2)}, u32[]{:S(2)}) collective-permute-start(f32[64,128]{1,0:T(8,128)} %get-tuple-element.33), channel_id=1, source_target_pairs={{0,4},{1,5},{2,6},{3,7},{8,12},{9,13},{10,14},{11,15},{16,20},{17,... | collective-permute-start | bytes 98312 | tf_op jit(solution)/shard_map/ppermute | solution.py:219
  56.1 13.3 %collective-permute-start.5 = (f32[64,128]{1,0:T(8,128)}, f32[64,128]{1,0:T(8,128)S(1)}, u32[]{:S(2)}, u32[]{:S(2)}) collective-permute-start(f32[64,128]{1,0:T(8,128)} %get-tuple-element.34), channel_id=1, source_target_pairs={{4,0},{5,1},{6,2},{7,3},{12,8},{13,9},{14,10},{15,11},{20,16},{21,... | collective-permute-start | bytes 98312 | tf_op jit(solution)/shard_map/ppermute | solution.py:219
  57.4 29.5 %collective-permute-start.8 = (s32[64]{0:T(128)S(1)}, s32[64]{0:T(128)S(1)}, u32[]{:S(2)}, u32[]{:S(2)}) collective-permute-start(s32[64]{0:T(128)S(1)} %copy-done.31), channel_id=1, source_target_pairs={{0,1},{1,0},{2,3},{3,2},{4,5},{5,4},{6,7},{7,6},{8,9},{9,8},{10,11... | collective-permute-start | bytes 776 | tf_op jit(solution)/shard_map/ppermute | solution.py:426
  59.2 13.0 %copy-start.28 = (f32[64,128]{1,0:T(8,128)}, f32[64,128]{1,0:T(8,128)S(1)}, u32[]{:S(2)}) copy-start(f32[64,128]{1,0:T(8,128)S(1)} %collective-permute-done.4.refs_2_) | copy-start | bytes 98308
  59.2 27.7 %collective-permute-start.10 = (s32[64]{0:T(128)S(1)}, s32[64]{0:T(128)S(1)}, u32[]{:S(2)}, u32[]{:S(2)}) collective-permute-start(s32[64]{0:T(128)S(1)} %copy-done.31), channel_id=1, source_target_pairs={{0,3},{1,2},{2,1},{3,0},{4,7},{5,6},{6,5},{7,4},{8,11},{9,10},{10,... | collective-permute-start | bytes 776 | tf_op jit(solution)/shard_map/ppermute | solution.py:426
  69.3 17.6 %collective-permute-start.9 = (s32[64]{0:T(128)S(1)}, s32[64]{0:T(128)S(1)}, u32[]{:S(2)}, u32[]{:S(2)}) collective-permute-start(s32[64]{0:T(128)S(1)} %copy-done.31), channel_id=1, source_target_pairs={{0,2},{1,3},{2,0},{3,1},{4,6},{5,7},{6,4},{7,5},{8,10},{9,11},{10,... | collective-permute-start | bytes 776 | tf_op jit(solution)/shard_map/ppermute | solution.py:426
  71.5 16.9 %collective-permute-start.11 = (s32[128]{0:T(128)S(1)}, s32[128]{0:T(128)S(1)}, u32[]{:S(2)}, u32[]{:S(2)}) collective-permute-start(s32[128]{0:T(128)S(1)} %copy-done.30), channel_id=1, source_target_pairs={{0,4},{4,0},{1,5},{5,1},{2,6},{6,2},{3,7},{7,3},{8,12},{12,8},{9,1... | collective-permute-start | bytes 1544 | tf_op jit(solution)/shard_map/ppermute | solution.py:426
  83.2 41.5 %all-to-all-start.1 = ((f32[8,2,2,3,64,128]{5,4,3,2,1,0:T(8,128)}), f32[8,2,2,3,64,128]{5,4,3,2,1,0:T(8,128)S(1)}, u32[]{:S(2)}, u32[]{:S(2)}) async-start(f32[8,2,2,3,64,128]{5,4,3,2,1,0:T(8,128)} %after.34), calls=%async_computation.1 | async-start | bytes 6291456 | tf_op jit(solution)/shard_map/all_to_all | solution.py:559
  93.2 22.3 %collective-permute-start.13 = (f32[3,256,256]{2,1,0:T(8,128)}, f32[3,256,256]{2,1,0:T(8,128)}, u32[]{:S(2)}, u32[]{:S(2)}) collective-permute-start(f32[3,256,256]{2,1,0:T(8,128)} %get-tuple-element.40.refs_3_), channel_id=1, source_target_pairs={{0,8},{24,16},{1,9},{25,17},{2,10},{26,18},{3,11},{27,19},{4,12},{... | collective-permute-start | bytes 2359304 | tf_op jit(solution)/shard_map/ppermute | solution.py:573
  102.0 34.3 %collective-permute-start.15 = (f32[3,256,256]{2,1,0:T(8,128)}, f32[3,256,256]{2,1,0:T(8,128)}, u32[]{:S(2)}, u32[]{:S(2)}) collective-permute-start(f32[3,256,256]{2,1,0:T(8,128)} %get-tuple-element.41.refs_1_), channel_id=1, source_target_pairs={{0,8},{24,16},{1,9},{25,17},{2,10},{26,18},{3,11},{27,19},{4,12},{... | collective-permute-start | bytes 2359304 | tf_op jit(solution)/shard_map/ppermute | solution.py:573
  117.9 22.3 %collective-permute-start.14 = (f32[3,256,256]{2,1,0:T(8,128)}, f32[3,256,256]{2,1,0:T(8,128)}, u32[]{:S(2)}, u32[]{:S(2)}) collective-permute-start(f32[3,256,256]{2,1,0:T(8,128)} %add.69.refs_3_), channel_id=1, source_target_pairs={{8,16},{16,8},{9,17},{17,9},{10,18},{18,10},{11,19},{19,11},{12,20... | collective-permute-start | bytes 2359304 | tf_op jit(solution)/shard_map/ppermute | solution.py:588
  129.8 10.5 %copy-start.11 = (f32[3,256,256]{2,1,0:T(8,128)S(1)}, f32[3,256,256]{2,1,0:T(8,128)}, u32[]{:S(2)}) copy-start(f32[3,256,256]{2,1,0:T(8,128)} %get-tuple-element.39.refs_6_) | copy-start | bytes 2359300
  129.8 21.5 %collective-permute-start.18 = (f32[3,256,256]{2,1,0:T(8,128)}, f32[3,256,256]{2,1,0:T(8,128)}, u32[]{:S(2)}, u32[]{:S(2)}) collective-permute-start(f32[3,256,256]{2,1,0:T(8,128)} %get-tuple-element.42.refs_1_), channel_id=1, source_target_pairs={{0,8},{1,9},{2,10},{3,11},{4,12},{5,13},{6,14},{7,15}} | collective-permute-start | bytes 2359304 | tf_op jit(solution)/shard_map/ppermute | solution.py:573
  136.2 9.5 %copy-start.6 = (f32[4,3,64,256]{3,2,1,0:T(8,128)S(1)}, f32[4,3,64,256]{3,2,1,0:T(8,128)}, u32[]{:S(2)}) copy-start(f32[4,3,64,256]{3,2,1,0:T(8,128)} %after.35.refs_5_) | copy-start | bytes 2359300
  138.7 20.4 %collective-permute-start.17 = (f32[3,256,256]{2,1,0:T(8,128)}, f32[3,256,256]{2,1,0:T(8,128)}, u32[]{:S(2)}, u32[]{:S(2)}) collective-permute-start(f32[3,256,256]{2,1,0:T(8,128)} %add.70.refs_1_), channel_id=1, source_target_pairs={{8,16},{16,8},{9,17},{17,9},{10,18},{18,10},{11,19},{19,11},{12,20... | collective-permute-start | bytes 2359304 | tf_op jit(solution)/shard_map/ppermute | solution.py:588
  142.5 20.4 %collective-permute-start.16 = (f32[3,256,256]{2,1,0:T(8,128)}, f32[3,256,256]{2,1,0:T(8,128)S(1)}, u32[]{:S(2)}, u32[]{:S(2)}) collective-permute-start(f32[3,256,256]{2,1,0:T(8,128)} %add.71.refs_3_), channel_id=1, source_target_pairs={{8,0},{16,24},{9,1},{17,25},{10,2},{18,26},{11,3},{19,27},{12,4},{... | collective-permute-start | bytes 2359304 | tf_op jit(solution)/shard_map/ppermute | solution.py:593
  143.8 20.4 %collective-permute-start.12 = (f32[2,3,128,256]{3,2,1,0:T(8,128)S(1)}, f32[2,3,128,256]{3,2,1,0:T(8,128)}, u32[]{:S(2)}, u32[]{:S(2)}) collective-permute-start(f32[2,3,128,256]{3,2,1,0:T(8,128)S(1)} %copy-done.7), channel_id=1, source_target_pairs={{0,4},{4,0},{1,5},{5,1},{2,6},{6,2},{3,7},{7,3},{8,12},{12,8},{9,1... | collective-permute-start | bytes 2359304 | tf_op jit(solution)/shard_map/ppermute | solution.py:398
  145.7 18.5 %collective-permute-start.24 = (f32[4,3,64,256]{3,2,1,0:T(8,128)S(1)}, f32[4,3,64,256]{3,2,1,0:T(8,128)}, u32[]{:S(2)}, u32[]{:S(2)}) collective-permute-start(f32[4,3,64,256]{3,2,1,0:T(8,128)S(1)} %copy-done.6), channel_id=1, source_target_pairs={{0,2},{1,3},{2,0},{3,1},{4,6},{5,7},{6,4},{7,5},{8,10},{9,11},{10,... | collective-permute-start | bytes 2359304 | tf_op jit(solution)/shard_map/ppermute | solution.py:399
  151.3 9.4 %copy-start.10 = (f32[3,256,256]{2,1,0:T(8,128)S(1)}, f32[3,256,256]{2,1,0:T(8,128)}, u32[]{:S(2)}) copy-start(f32[3,256,256]{2,1,0:T(8,128)} %get-tuple-element.43.refs_6_) | copy-start | bytes 2359300
  151.3 19.6 %collective-permute-start.22 = (f32[3,256,256]{2,1,0:T(8,128)}, f32[3,256,256]{2,1,0:T(8,128)}, u32[]{:S(2)}, u32[]{:S(2)}) collective-permute-start(f32[3,256,256]{2,1,0:T(8,128)} %get-tuple-element.44.refs_1_), channel_id=1, source_target_pairs={{0,8},{1,9},{2,10},{3,11},{4,12},{5,13},{6,14},{7,15}} | collective-permute-start | bytes 2359304 | tf_op jit(solution)/shard_map/ppermute | solution.py:573
  159.1 13.1 %collective-permute-start.21 = (f32[3,256,256]{2,1,0:T(8,128)}, f32[3,256,256]{2,1,0:T(8,128)}, u32[]{:S(2)}, u32[]{:S(2)}) collective-permute-start(f32[3,256,256]{2,1,0:T(8,128)} %add.72.refs_1_), channel_id=1, source_target_pairs={{8,16},{16,8},{9,17},{17,9},{10,18},{18,10},{11,19},{19,11},{12,20... | collective-permute-start | bytes 2359304 | tf_op jit(solution)/shard_map/ppermute | solution.py:588
  162.8 19.1 %collective-permute-start.20 = (f32[3,256,256]{2,1,0:T(8,128)}, f32[3,256,256]{2,1,0:T(8,128)S(1)}, u32[]{:S(2)}, u32[]{:S(2)}) collective-permute-start(f32[3,256,256]{2,1,0:T(8,128)} %add.73.refs_1_), channel_id=1, source_target_pairs={{8,0},{16,24},{9,1},{17,25},{10,2},{18,26},{11,3},{19,27},{12,4},{... | collective-permute-start | bytes 2359304 | tf_op jit(solution)/shard_map/ppermute | solution.py:593
  164.2 19.8 %collective-permute-start.19 = (f32[2,3,128,256]{3,2,1,0:T(8,128)}, f32[2,3,128,256]{3,2,1,0:T(8,128)}, u32[]{:S(2)}, u32[]{:S(2)}) collective-permute-start(f32[2,3,128,256]{3,2,1,0:T(8,128)} %after.41.first_ref), channel_id=1, source_target_pairs={{0,1},{1,0},{2,3},{3,2},{4,5},{5,4},{6,7},{7,6},{8,9},{9,8},{10,11... | collective-permute-start | bytes 2359304 | tf_op jit(solution)/shard_map/ppermute | solution.py:405
  164.3 24.6 %collective-permute-start.23 = (f32[4,3,64,256]{3,2,1,0:T(8,128)}, f32[4,3,64,256]{3,2,1,0:T(8,128)}, u32[]{:S(2)}, u32[]{:S(2)}) collective-permute-start(f32[4,3,64,256]{3,2,1,0:T(8,128)} %b0_ref.1), channel_id=1, source_target_pairs={{0,1},{1,0},{2,3},{3,2},{4,5},{5,4},{6,7},{7,6},{8,9},{9,8},{10,11... | collective-permute-start | bytes 2359304 | tf_op jit(solution)/shard_map/ppermute | solution.py:405
  164.8 9.0 %copy-start.12 = (f32[3,256,256]{2,1,0:T(8,128)S(1)}, f32[3,256,256]{2,1,0:T(8,128)}, u32[]{:S(2)}) copy-start(f32[3,256,256]{2,1,0:T(8,128)} %get-tuple-element.45.refs_6_) | copy-start | bytes 2359300
  170.9 18.0 %collective-permute-start.25 = (f32[4,3,64,256]{3,2,1,0:T(8,128)}, f32[4,3,64,256]{3,2,1,0:T(8,128)}, u32[]{:S(2)}, u32[]{:S(2)}) collective-permute-start(f32[4,3,64,256]{3,2,1,0:T(8,128)} %after.47.b2_ref), channel_id=1, source_target_pairs={{0,1},{1,0},{2,3},{3,2},{4,5},{5,4},{6,7},{7,6},{8,9},{9,8},{10,11... | collective-permute-start | bytes 2359304 | tf_op jit(solution)/shard_map/ppermute | solution.py:405
  172.2 27.8 %collective-permute-start.27 = (f32[3,256,256]{2,1,0:T(8,128)S(1)}, f32[3,256,256]{2,1,0:T(8,128)}, u32[]{:S(2)}, u32[]{:S(2)}) collective-permute-start(f32[3,256,256]{2,1,0:T(8,128)S(1)} %add.74.refs_1_), channel_id=1, source_target_pairs={{8,16},{16,8},{9,17},{17,9},{10,18},{18,10},{11,19},{19,11},{12,20... | collective-permute-start | bytes 2359304 | tf_op jit(solution)/shard_map/ppermute | solution.py:588
  175.1 9.0 %copy-start.18 = (f32[3,256,256]{2,1,0:T(8,128)}, f32[3,256,256]{2,1,0:T(8,128)S(1)}, u32[]{:S(2)}) copy-start(f32[3,256,256]{2,1,0:T(8,128)S(1)} %add.75.refs_1_) | copy-start | bytes 2359300
  181.9 20.7 %collective-permute-start.26 = (f32[3,256,256]{2,1,0:T(8,128)S(1)}, f32[3,256,256]{2,1,0:T(8,128)S(1)}, u32[]{:S(2)}, u32[]{:S(2)}) collective-permute-start(f32[3,256,256]{2,1,0:T(8,128)S(1)} %add.75.refs_1_), channel_id=1, source_target_pairs={{8,0},{16,24},{9,1},{17,25},{10,2},{18,26},{11,3},{19,27},{12,4},{... | collective-permute-start | bytes 2359304 | tf_op jit(solution)/shard_map/ppermute | solution.py:593
  201.3 18.9 %collective-permute-start.29 = (f32[3,256,256]{2,1,0:T(8,128)S(1)}, f32[3,256,256]{2,1,0:T(8,128)S(1)}, u32[]{:S(2)}, u32[]{:S(2)}) collective-permute-start(f32[3,256,256]{2,1,0:T(8,128)S(1)} %add.76.refs_1_), channel_id=1, source_target_pairs={{8,0},{16,24},{9,1},{17,25},{10,2},{18,26},{11,3},{19,27},{12,4},{... | collective-permute-start | bytes 2359304 | tf_op jit(solution)/shard_map/ppermute | solution.py:593
  210.2 17.6 %all-to-all-start.2 = ((f32[8,3,64,128]{3,2,1,0:T(8,128)}), f32[8,3,64,128]{3,2,1,0:T(8,128)S(1)}, u32[]{:S(2)}, u32[]{:S(2)}) async-start(f32[8,3,64,128]{3,2,1,0:T(8,128)} %sweep.5.refs_1_), calls=%async_computation.2 | async-start | bytes 1572864 | tf_op jit(solution)/shard_map/all_to_all | solution.py:615
  227.8 41.0 %copy-start.8 = (f32[8,3,64,128]{3,2,1,0:T(8,128)}, f32[8,3,64,128]{3,2,1,0:T(8,128)S(1)}, u32[]{:S(2)}) copy-start(f32[8,3,64,128]{3,2,1,0:T(8,128)S(1)} %all-to-all-done.2.refs_2_) | copy-start | bytes 2359300
  227.8 16.7 %all-to-all-start.3 = ((f32[8,3,64,128]{3,2,1,0:T(8,128)}), f32[8,3,64,128]{3,2,1,0:T(8,128)S(1)}, u32[]{:S(2)}, u32[]{:S(2)}) async-start(f32[8,3,64,128]{3,2,1,0:T(8,128)} %sweep.7), calls=%async_computation.3 | async-start | bytes 1572864 | tf_op jit(solution)/shard_map/all_to_all | solution.py:615
  231.9 45.0 %copy-start.1 = (s32[3,2]{0,1:T(2,128)S(1)}, s32[3,2]{0,1:T(2,128)}, u32[]{:S(2)}) copy-start(s32[3,2]{0,1:T(2,128)} %param.12) | copy-start | bytes 76
  231.9 20.3 %collective-permute-start.28 = (f32[8,3,64,128]{3,2,1,0:T(8,128)S(1)}, f32[8,3,64,128]{3,2,1,0:T(8,128)S(1)}, u32[]{:S(2)}, u32[]{:S(2)}) collective-permute-start(f32[8,3,64,128]{3,2,1,0:T(8,128)S(1)} %all-to-all-done.2.refs_2_), channel_id=1, source_target_pairs={{0,24},{1,25},{2,26},{3,27},{4,28},{5,29},{6,30},{7,31}} | collective-permute-start | bytes 2359304 | tf_op jit(solution)/shard_map/ppermute | solution.py:616
  244.5 24.3 %copy-start.9 = (f32[8,3,64,128]{3,2,1,0:T(8,128)}, f32[8,3,64,128]{3,2,1,0:T(8,128)S(1)}, u32[]{:S(2)}) copy-start(f32[8,3,64,128]{3,2,1,0:T(8,128)S(1)} %all-to-all-done.3.refs_3_) | copy-start | bytes 2359300
  244.5 24.3 %collective-permute-start.30 = (f32[8,3,64,128]{3,2,1,0:T(8,128)S(1)}, f32[8,3,64,128]{3,2,1,0:T(8,128)S(1)}, u32[]{:S(2)}, u32[]{:S(2)}) collective-permute-start(f32[8,3,64,128]{3,2,1,0:T(8,128)S(1)} %all-to-all-done.3.refs_3_), channel_id=1, source_target_pairs={{0,24},{1,25},{2,26},{3,27},{4,28},{5,29},{6,30},{7,31}} | collective-permute-start | bytes 2359304 | tf_op jit(solution)/shard_map/ppermute | solution.py:616
  252.2 16.6 %copy-start.20 = (f32[8,3,64,128]{3,2,1,0:T(8,128)}, f32[8,3,64,128]{3,2,1,0:T(8,128)S(1)}, u32[]{:S(2)}) copy-start(f32[8,3,64,128]{3,2,1,0:T(8,128)S(1)} %collective-permute-done.28.refs_0_) | copy-start | bytes 2359300
  (19 other events, 39.9 us)

commit v5 on v4

--- a/solution.py
+++ b/solution.py
@@ -374,20 +374,31 @@
             low_ref[cls, 0, spot, :] = low
 
 
-def prepare_ops(kernel, pos, blocks, length, name):
+def ops_kernel(pos_ref, *refs):
+    x_ops_kernel(pos_ref, *refs[:3], *refs[7:9])
+    y_ops_kernel(pos_ref, *refs[3:7], *refs[9:])
+
+
+def prepare_ops(pos, x_blocks, y_blocks):
     def spec(block):
         return pl.BlockSpec((block.shape[0], 1) + block.shape[2:], lambda k: (0, k, 0, 0))
 
-    out = jax.ShapeDtypeStruct((NCLASS, 3, length, length), bf16)
-    return pl.pallas_call(
-        kernel,
+    blocks = (*x_blocks, *y_blocks)
+    out = [
+        jax.ShapeDtypeStruct((NCLASS, 3, length, length), bf16)
+        for length in (x_blocks[0].shape[3], y_blocks[0].shape[3])
+        for _ in range(2)
+    ]
+    parts = pl.pallas_call(
+        ops_kernel,
         grid=(3,),
         in_specs=[pl.BlockSpec(memory_space=pltpu.SMEM)] + [spec(b) for b in blocks],
-        out_specs=[spec(out)] * 2,
-        out_shape=[out] * 2,
+        out_specs=[spec(o) for o in out],
+        out_shape=out,
         compiler_params=params(),
-        name=name,
+        name="operators",
     )(pos, *blocks)
+    return parts[:2], parts[2:]
 
 
 def fetched_ops(x_ops, y_ops, earlier):
@@ -410,13 +421,7 @@
     pair_x, pair_y, cross_y = paired
     place_y = lax.axis_index("gy")
     pos = jnp.stack([lax.axis_index("gx"), lax.rem(place_y, 2), place_y]).astype(jnp.int32)
-    x_parts = prepare_ops(
-        x_ops_kernel, pos, (x_ops, got_x, pair_x), x_ops.shape[3], "x_operators"
-    )
-    y_parts = prepare_ops(
-        y_ops_kernel, pos, (y_ops, pair_y, got_y, cross_y), y_ops.shape[3], "y_operators"
-    )
-    return x_parts, y_parts
+    return prepare_ops(pos, (x_ops, got_x, pair_x), (y_ops, pair_y, got_y, cross_y))
 
 
 def gathered_classes(x_line_class, y_line_class):

time: 279 us -> 278 us (level)
    pallas_call x2 -> x1, Pallas kernels: 9.37 us -> 6.84 us  [prepare_ops(): pl.pallas_call(ops_kernel, grid=(3,), in_specs=[pl.BlockSpec(memory_space...]
    unnamed x65 -> x63, local copies, waits for them, and re-layouts: 11.3 us -> 13.1 us
  transfers between devices with their start and end apart: 35 -> 35, of which waited for: 8 -> 8; matrix products, arithmetic and copies ran while one was open for 10% -> 10% of each run, Pallas kernels for 28% -> 27%
where the time goes in v5:
time: 278 us; the launch traced here: 276 us
  Pallas kernels  91.3 us (33%)
  starting transfers between devices  89 us (32%)
  waiting for transfers between devices  55.7 us (20%)
  other arithmetic  22 us (8%)
  local copies, waits for them, and re-layouts  17.8 us (6%)
    pallas_call x3, Pallas kernels, flow(): pl.pallas_call(body, grid=(groups,), in_specs=[pl.BlockSpec(memory_space=...  28.4 us
    pallas_call x4, Pallas kernels, sweep(): pl.pallas_call(body, grid=(3,), in_specs=[pl.BlockSpec((full_y, 1), lambd...  26.3 us
    ppermute x2, waiting for transfers between devices, local(): brought = [lax.ppermute(value, 'sec', [(0, 3)]) for value in tiles]  21.8 us
    ppermute x4, starting transfers between devices, placed(): lax.ppermute(fars[n], 'sec', [(0, 1), (3, 2)] if first else [(0, 1)])  19.3 us
    ppermute x8, starting transfers between devices, send(): lax.ppermute(value, axis, [(i, i + step) for i in range(count) if 0 <= i...  19 us
    ppermute x4, waiting for transfers between devices, placed(): lax.ppermute(fars[n], 'sec', [(0, 1), (3, 2)] if first else [(0, 1)])  18.2 us
    ppermute x4, starting transfers between devices, rows(): lax.ppermute(value, axis, [(i, i ^ step) for i in range(count)])  14.8 us
    pallas_call x4, Pallas kernels, place(): pl.pallas_call(body, grid=(1,), in_specs=[pl.BlockSpec(memory_space=pltpu...  14.2 us
  transfers between devices with their start and end apart: 35, of which 8 were waited for; matrix products, arithmetic and copies ran while one was open for 10% of the time, Pallas kernels for 27%

profile of v5, /device:TPU:0, one launch (start us, length us, event | category | flops | bytes accessed | tf_op | source)
XLA Modules:
  0.0 276.3 jit_solution(417779505557235547)
XLA Ops:
  0.0 3.0 %tile_edges.1 = (f32[64,128]{1,0:T(8,128)}, f32[64,128]{1,0:T(8,128)}, f32[3,32,128]{2,1,0:T(8,128)}, f32[3,32,128]{2,1,0:T(8,128)}) custom-call(f32[3,128,2048]{2,1,0:T(8,128)} %bitcast.21, f32[3,128,2048]{2,1,0:T(8,128)} %bitcast.22, f32[3,128,2048]{2,1,0:T(8,128)} %bitcast.23, f32[3,128,2048]{2,1,0:T(8,128)} %bitcast.24), custom_call_target="tpu_custom_call" | custom-call | tf_op jit(solution)/shard_map/tile_edges/pallas_call | solution.py:56
  4.3 3.0 %collective-permute-start.2 = (f32[3,32,128]{2,1,0:T(8,128)}, f32[3,32,128]{2,1,0:T(8,128)S(1)}, u32[]{:S(2)}, u32[]{:S(2)}) collective-permute-start(f32[3,32,128]{2,1,0:T(8,128)} %get-tuple-element.30), channel_id=1, source_target_pairs={{0,1},{1,2},{2,3},{4,5},{5,6},{6,7},{8,9},{9,10},{10,11},{12,13},{... | collective-permute-start | bytes 147464 | tf_op jit(solution)/shard_map/ppermute | solution.py:219
  8.7 4.9 %collective-permute-start = (f32[64,128]{1,0:T(8,128)}, f32[64,128]{1,0:T(8,128)S(1)}, u32[]{:S(2)}, u32[]{:S(2)}) collective-permute-start(f32[64,128]{1,0:T(8,128)} %get-tuple-element.29), channel_id=1, source_target_pairs={{0,4},{1,5},{2,6},{3,7},{8,12},{9,13},{10,14},{11,15},{16,20},{17,... | collective-permute-start | bytes 98312 | tf_op jit(solution)/shard_map/ppermute | solution.py:219
  13.5 5.4 %to_planes.1.refs_1_ = f32[32,3,64,128]{3,2,1,0:T(8,128)} custom-call(f32[3,128,2048]{2,1,0:T(8,128)} %bitcast.25, f32[64,128]{1,0:T(8,128)} %get-tuple-element.28.refs_0_), custom_call_target="tpu_custom_call" | custom-call | tf_op jit(solution)/shard_map/to_planes/pallas_call | solution.py:89
  21.4 7.2 %flow.3.refs_6_ = f32[8,2,2,3,64,128]{5,4,3,2,1,0:T(8,128)} custom-call(s32[1]{0:T(128)} %bitcast.refs_0_.flag_ref, f32[32,3,64,128]{3,2,1,0:T(8,128)} %to_planes.1.refs_1_, f32[64,128]{1,0:T(8,128)} %after.27.refs_2_, f32[64,128]{1,0:T(8,128)} %after.28.refs_3_, f32[3,32,128]{2,1,0:T(8,128)} %after.29.refs_4_, f32[3,32,128]{2,1,0:T(8,128)} %after.30.refs_5_), custom_call_target="tpu_custom_call" | custom-call | tf_op jit(solution)/shard_map/flow/pallas_call | solution.py:197
  28.6 3.9 %all-to-all-start = ((f32[8,2,2,3,64,128]{5,4,3,2,1,0:T(8,128)}), f32[8,2,2,3,64,128]{5,4,3,2,1,0:T(8,128)S(1)}, u32[]{:S(2)}, u32[]{:S(2)}) async-start(f32[8,2,2,3,64,128]{5,4,3,2,1,0:T(8,128)} %flow.3.refs_6_), calls=%async_computation | async-start | bytes 6291456 | tf_op jit(solution)/shard_map/all_to_all | solution.py:558
  36.2 12.6 %flow.4 = (f32[32,3,64,128]{3,2,1,0:T(8,128)}, f32[64,128]{1,0:T(8,128)}, f32[64,128]{1,0:T(8,128)}, f32[3,32,128]{2,1,0:T(8,128)}, f32[3,32,128]{2,1,0:T(8,128)}) custom-call(s32[1]{0:T(128)} %bitcast.refs_0_.flag_ref, f32[32,3,64,128]{3,2,1,0:T(8,128)} %to_planes.1.refs_1_, f32[64,128]{1,0:T(8,128)} %after.27.refs_2_, f32[64,128]{1,0:T(8,128)} %after.28.refs_3_, ...), custom_call_target="tpu_custom_call" | custom-call | tf_op jit(solution)/shard_map/flow/pallas_call | solution.py:197
  48.9 3.3 %collective-permute-start.6 = (f32[3,32,128]{2,1,0:T(8,128)}, f32[3,32,128]{2,1,0:T(8,128)S(1)}, u32[]{:S(2)}, u32[]{:S(2)}) collective-permute-start(f32[3,32,128]{2,1,0:T(8,128)} %get-tuple-element.35), channel_id=1, source_target_pairs={{0,1},{1,2},{2,3},{4,5},{5,6},{6,7},{8,9},{9,10},{10,11},{12,13},{... | collective-permute-start | bytes 147464 | tf_op jit(solution)/shard_map/ppermute | solution.py:219
  53.5 2.7 collective-permute-start.4
  57.5 1.8 collective-permute-start.8
  59.3 10.1 %collective-permute-start.10 = (s32[64]{0:T(128)S(1)}, s32[64]{0:T(128)S(1)}, u32[]{:S(2)}, u32[]{:S(2)}) collective-permute-start(s32[64]{0:T(128)S(1)} %copy-done.30), channel_id=1, source_target_pairs={{0,3},{1,2},{2,1},{3,0},{4,7},{5,6},{6,5},{7,4},{8,11},{9,10},{10,... | collective-permute-start | bytes 776 | tf_op jit(solution)/shard_map/ppermute | solution.py:431
  69.4 2.2 collective-permute-start.9
  72.9 8.7 %flow.5 = (f32[8,2,2,3,64,128]{5,4,3,2,1,0:T(8,128)}, f32[32,3,64,128]{3,2,1,0:T(8,128)}) custom-call(s32[1]{0:T(128)} %bitcast.refs_0_.flag_ref, f32[32,3,64,128]{3,2,1,0:T(8,128)} %get-tuple-element.32.refs_1_, f32[64,128]{1,0:T(8,128)} %copy-done.27, f32[64,128]{1,0:T(8,128)} %copy-done.28, f32[3,32,128]{2,1,0:T(8,128)} %copy-done.25, ...), custom_call_target="tpu_custom_call" | custom-call | tf_op jit(solution)/shard_map/flow/pallas_call | solution.py:197
  83.2 3.7 %all-to-all-start.1 = ((f32[8,2,2,3,64,128]{5,4,3,2,1,0:T(8,128)}), f32[8,2,2,3,64,128]{5,4,3,2,1,0:T(8,128)S(1)}, u32[]{:S(2)}, u32[]{:S(2)}) async-start(f32[8,2,2,3,64,128]{5,4,3,2,1,0:T(8,128)} %after.34), calls=%async_computation.1 | async-start | bytes 6291456 | tf_op jit(solution)/shard_map/all_to_all | solution.py:564
  89.7 3.7 %place.4 = (f32[3,256,256]{2,1,0:T(8,128)}, f32[3,256,256]{2,1,0:T(8,128)}) custom-call(s32[4]{0:T(128)} %pad_add_fusion.2.refs_7_.refs_0_, f32[3,3]{1,0:T(4,128)} %select_bitcast_fusion.refs_8_.refs_1_, f32[8,2,2,3,64,128]{5,4,3,2,1,0:T(8,128)} %after.32.refs_2_.refs_1_, s32[256,1]{1,0:T(8,128)} %select_n.92.refs_3_.refs_0_, s32[1,256]{1,0:T(1,128)} %bitcast.26), custom_call_target="tpu_custom_call" | custom-call | tf_op jit(solution)/shard_map/place/pallas_call | solution.py:303
  93.4 5.1 %collective-permute-start.13 = (f32[3,256,256]{2,1,0:T(8,128)}, f32[3,256,256]{2,1,0:T(8,128)}, u32[]{:S(2)}, u32[]{:S(2)}) collective-permute-start(f32[3,256,256]{2,1,0:T(8,128)} %get-tuple-element.40.refs_3_), channel_id=1, source_target_pairs={{0,8},{24,16},{1,9},{25,17},{2,10},{26,18},{3,11},{27,19},{4,12},{... | collective-permute-start | bytes 2359304 | tf_op jit(solution)/shard_map/ppermute | solution.py:578
  98.4 3.7 %place.5 = (f32[3,256,256]{2,1,0:T(8,128)}, f32[3,256,256]{2,1,0:T(8,128)}) custom-call(s32[4]{0:T(128)} %pad_add_fusion.2.refs_7_.refs_0_, f32[3,3]{1,0:T(4,128)} %select_bitcast_fusion.refs_8_.refs_1_, f32[8,2,2,3,64,128]{5,4,3,2,1,0:T(8,128)} %after.32.refs_2_.refs_1_, f32[3,256,256]{2,1,0:T(8,128)} %get-tuple-element.40.refs_3_), custom_call_target="tpu_custom_call" | custom-call | tf_op jit(solution)/shard_map/place/pallas_call | solution.py:303
  102.1 2.2 collective-permute-start.15
  104.3 11.4 %collective-permute-done.13.refs_0_ = f32[3,256,256]{2,1,0:T(8,128)} collective-permute-done((f32[3,256,256]{2,1,0:T(8,128)}, f32[3,256,256]{2,1,0:T(8,128)}, u32[]{:S(2)}, u32[]{:S(2)}) %collective-permute-start.13) | collective-permute-done | bytes 786464 | tf_op jit(solution)/shard_map/ppermute | solution.py:578
  115.7 2.4 add.69.refs_3_
  119.6 2.1 copy.48.refs_0_
  121.8 2.1 constant_dynamic-slice_fusion.refs_0_
  126.4 3.4 %place.6 = (f32[3,256,256]{2,1,0:T(8,128)}, f32[3,256,256]{2,1,0:T(8,128)}) custom-call(s32[4]{0:T(128)} %pad_add_fusion.2.refs_7_.refs_0_, f32[3,3]{1,0:T(4,128)} %select_bitcast_fusion.refs_8_.refs_1_, f32[8,2,2,3,64,128]{5,4,3,2,1,0:T(8,128)} %copy-done.3, f32[3,256,256]{2,1,0:T(8,128)} %add.69.refs_3_, f32[2,3,128,256]{3,2,1,0:T(8,128)} %after.31.refs_4_, ...), custom_call_target="tpu_custom_call" | custom-call | tf_op jit(solution)/shard_map/place/pallas_call | solution.py:303
  129.8 6.5 %collective-permute-start.18 = (f32[3,256,256]{2,1,0:T(8,128)}, f32[3,256,256]{2,1,0:T(8,128)}, u32[]{:S(2)}, u32[]{:S(2)}) collective-permute-start(f32[3,256,256]{2,1,0:T(8,128)} %get-tuple-element.42.refs_1_), channel_id=1, source_target_pairs={{0,8},{1,9},{2,10},{3,11},{4,12},{5,13},{6,14},{7,15}} | collective-permute-start | bytes 2359304 | tf_op jit(solution)/shard_map/ppermute | solution.py:578
  136.3 2.5 add.70.refs_1_
  140.4 2.2 add.71.refs_3_
  143.9 2.0 collective-permute-start.12
  147.4 3.4 %place.7 = (f32[3,256,256]{2,1,0:T(8,128)}, f32[3,256,256]{2,1,0:T(8,128)}) custom-call(s32[4]{0:T(128)} %pad_add_fusion.2.refs_7_.refs_0_, f32[3,3]{1,0:T(4,128)} %select_bitcast_fusion.refs_8_.refs_1_, f32[8,2,2,3,64,128]{5,4,3,2,1,0:T(8,128)} %copy-done.3, f32[3,256,256]{2,1,0:T(8,128)} %add.71.refs_3_), custom_call_target="tpu_custom_call" | custom-call | tf_op jit(solution)/shard_map/place/pallas_call | solution.py:303
  151.4 5.5 %collective-permute-start.22 = (f32[3,256,256]{2,1,0:T(8,128)}, f32[3,256,256]{2,1,0:T(8,128)}, u32[]{:S(2)}, u32[]{:S(2)}) collective-permute-start(f32[3,256,256]{2,1,0:T(8,128)} %get-tuple-element.44.refs_1_), channel_id=1, source_target_pairs={{0,8},{1,9},{2,10},{3,11},{4,12},{5,13},{6,14},{7,15}} | collective-permute-start | bytes 2359304 | tf_op jit(solution)/shard_map/ppermute | solution.py:578
  156.9 2.3 add.72.refs_1_
  160.8 2.2 add.73.refs_1_
  164.9 6.1 %collective-permute-done.22.refs_0_ = f32[3,256,256]{2,1,0:T(8,128)} collective-permute-done((f32[3,256,256]{2,1,0:T(8,128)}, f32[3,256,256]{2,1,0:T(8,128)}, u32[]{:S(2)}, u32[]{:S(2)}) %collective-permute-start.22) | collective-permute-done | bytes 786464 | tf_op jit(solution)/shard_map/ppermute | solution.py:578
  171.0 2.4 add.74.refs_1_
  175.0 2.2 add.75.refs_1_
  177.2 4.9 %collective-permute-done.20.refs_0_ = f32[3,256,256]{2,1,0:T(8,128)S(1)} collective-permute-done((f32[3,256,256]{2,1,0:T(8,128)}, f32[3,256,256]{2,1,0:T(8,128)S(1)}, u32[]{:S(2)}, u32[]{:S(2)}) %collective-permute-start.20) | collective-permute-done | bytes 786464 | tf_op jit(solution)/shard_map/ppermute | solution.py:598
  186.0 6.8 %operators.1 = (bf16[4,3,256,256]{3,2,1,0:T(8,128)(2,1)}, bf16[4,3,256,256]{3,2,1,0:T(8,128)(2,1)}, bf16[4,3,256,256]{3,2,1,0:T(8,128)(2,1)}, bf16[4,3,256,256]{3,2,1,0:T(8,128)(2,1)}) custom-call(s32[3]{0:T(128)} %pad_add_fusion.3.pos_ref, f32[4,3,128,256]{3,2,1,0:T(8,128)} %refs_0_.2, f32[2,3,128,256]{3,2,1,0:T(8,128)} %after.41.refs_1_, ...), custom_call_target="tpu_custom_call" | custom-call | tf_op jit(solution)/shard_map/operators/pallas_call | solution.py:392
  192.8 6.5 %sweep.4.refs_1_.refs_8_ = f32[3,256,256]{2,1,0:T(8,128)} custom-call(s32[256,1]{1,0:T(8,128)} %select_n.92.refs_3_.refs_0_, s32[1,256]{1,0:T(1,128)} %bitcast.27, bf16[4,3,256,256]{3,2,1,0:T(8,128)(2,1)} %get-tuple-element.46.refs_1_.refs_2_, bf16[4,3,256,256]{3,2,1,0:T(8,128)(2,1)} %get-tuple-element.47.refs_2_.refs_3_, ...), custom_call_target="tpu_custom_call" | custom-call | tf_op jit(solution)/shard_map/sweep/pallas_call | solution.py:484
  202.9 6.6 %sweep.5.refs_1_ = f32[8,3,64,128]{3,2,1,0:T(8,128)} custom-call(s32[256,1]{1,0:T(8,128)} %select_n.92.refs_3_.refs_0_, s32[1,256]{1,0:T(1,128)} %bitcast.28, bf16[4,3,256,256]{3,2,1,0:T(8,128)(2,1)} %get-tuple-element.46.refs_1_.refs_2_, bf16[4,3,256,256]{3,2,1,0:T(8,128)(2,1)} %get-tuple-element.47.refs_2_.refs_3_, ...), custom_call_target="tpu_custom_call" | custom-call | tf_op jit(solution)/shard_map/sweep/pallas_call | solution.py:484
  209.5 3.5 %all-to-all-start.2 = ((f32[8,3,64,128]{3,2,1,0:T(8,128)}), f32[8,3,64,128]{3,2,1,0:T(8,128)S(1)}, u32[]{:S(2)}, u32[]{:S(2)}) async-start(f32[8,3,64,128]{3,2,1,0:T(8,128)} %sweep.5.refs_1_), calls=%async_computation.2 | async-start | bytes 1572864 | tf_op jit(solution)/shard_map/all_to_all | solution.py:620
  213.1 6.5 %sweep.6.refs_1_.refs_8_ = f32[3,256,256]{2,1,0:T(8,128)} custom-call(s32[256,1]{1,0:T(8,128)} %select_n.92.refs_3_.refs_0_, s32[1,256]{1,0:T(1,128)} %bitcast.29, bf16[4,3,256,256]{3,2,1,0:T(8,128)(2,1)} %get-tuple-element.46.refs_1_.refs_2_, bf16[4,3,256,256]{3,2,1,0:T(8,128)(2,1)} %get-tuple-element.47.refs_2_.refs_3_, ...), custom_call_target="tpu_custom_call" | custom-call | tf_op jit(solution)/shard_map/sweep/pallas_call | solution.py:484
  220.5 6.6 %sweep.7 = f32[8,3,64,128]{3,2,1,0:T(8,128)} custom-call(s32[256,1]{1,0:T(8,128)} %select_n.92.refs_3_.refs_0_, s32[1,256]{1,0:T(1,128)} %bitcast.30, bf16[4,3,256,256]{3,2,1,0:T(8,128)(2,1)} %get-tuple-element.46.refs_1_.refs_2_, bf16[4,3,256,256]{3,2,1,0:T(8,128)(2,1)} %get-tuple-element.47.refs_2_.refs_3_, ...), custom_call_target="tpu_custom_call" | custom-call | tf_op jit(solution)/shard_map/sweep/pallas_call | solution.py:484
  227.1 4.1 %all-to-all-start.3 = ((f32[8,3,64,128]{3,2,1,0:T(8,128)}), f32[8,3,64,128]{3,2,1,0:T(8,128)S(1)}, u32[]{:S(2)}, u32[]{:S(2)}) async-start(f32[8,3,64,128]{3,2,1,0:T(8,128)} %sweep.7), calls=%async_computation.3 | async-start | bytes 1572864 | tf_op jit(solution)/shard_map/all_to_all | solution.py:620
  231.2 2.7 collective-permute-start.28
  233.9 9.9 %all-to-all-done.3.refs_3_ = f32[8,3,64,128]{3,2,1,0:T(8,128)S(1)} async-done(((f32[8,3,64,128]{3,2,1,0:T(8,128)}), f32[8,3,64,128]{3,2,1,0:T(8,128)S(1)}, u32[]{:S(2)}, u32[]{:S(2)}) %all-to-all-start.3) | async-done | bytes 786464 | tf_op jit(solution)/shard_map/all_to_all | solution.py:620
  243.8 2.6 collective-permute-start.30
  246.4 5.3 %collective-permute-done.28.refs_0_ = f32[8,3,64,128]{3,2,1,0:T(8,128)S(1)} collective-permute-done((f32[8,3,64,128]{3,2,1,0:T(8,128)S(1)}, f32[8,3,64,128]{3,2,1,0:T(8,128)S(1)}, u32[]{:S(2)}, u32[]{:S(2)}) %collective-permute-start.28) | collective-permute-done | bytes 786464 | tf_op jit(solution)/shard_map/ppermute | solution.py:621
  251.7 16.5 %collective-permute-done.30.refs_1_ = f32[8,3,64,128]{3,2,1,0:T(8,128)S(1)} collective-permute-done((f32[8,3,64,128]{3,2,1,0:T(8,128)S(1)}, f32[8,3,64,128]{3,2,1,0:T(8,128)S(1)}, u32[]{:S(2)}, u32[]{:S(2)}) %collective-permute-start.30) | collective-permute-done | bytes 786464 | tf_op jit(solution)/shard_map/ppermute | solution.py:621
  269.1 7.2 %to_output.1 = f32[1,3,128,2048]{3,2,1,0:T(8,128)} custom-call(s32[1]{0:T(128)} %bitcast.refs_0_.flag_ref, f32[32,3,64,128]{3,2,1,0:T(8,128)} %get-tuple-element.37.refs_1_.u_ref, f32[8,3,64,128]{3,2,1,0:T(8,128)} %copy-done.19, f32[8,3,64,128]{3,2,1,0:T(8,128)} %copy-done.20, f32[8,3,64,128]{3,2,1,0:T(8,128)} %copy-done.8, f32[8,3,64,128]{3,2,1,0:T(8,128)} %copy-done.9), custom_call_target="tpu_custom_call" | custom-call | tf_op jit(solution)/shard_map/to_output/pallas_call | solution.py:524
  (154 shorter events, 40.2 us)
Async XLA Ops:
  0.0 32.5 %copy-start = (s32[3,2]{0,1:T(2,128)S(1)}, s32[3,2]{0,1:T(2,128)}, u32[]{:S(2)}) copy-start(s32[3,2]{0,1:T(2,128)} %param.12) | copy-start | bytes 76
  3.0 17.1 %collective-permute-start.3 = (f32[3,32,128]{2,1,0:T(8,128)}, f32[3,32,128]{2,1,0:T(8,128)S(1)}, u32[]{:S(2)}, u32[]{:S(2)}) collective-permute-start(f32[3,32,128]{2,1,0:T(8,128)} %get-tuple-element.31), channel_id=1, source_target_pairs={{1,0},{2,1},{3,2},{5,4},{6,5},{7,6},{9,8},{10,9},{11,10},{13,12},{... | collective-permute-start | bytes 147464 | tf_op jit(solution)/shard_map/ppermute | solution.py:219
  4.3 16.5 %collective-permute-start.2 = (f32[3,32,128]{2,1,0:T(8,128)}, f32[3,32,128]{2,1,0:T(8,128)S(1)}, u32[]{:S(2)}, u32[]{:S(2)}) collective-permute-start(f32[3,32,128]{2,1,0:T(8,128)} %get-tuple-element.30), channel_id=1, source_target_pairs={{0,1},{1,2},{2,3},{4,5},{5,6},{6,7},{8,9},{9,10},{10,11},{12,13},{... | collective-permute-start | bytes 147464 | tf_op jit(solution)/shard_map/ppermute | solution.py:219
  7.4 11.6 %collective-permute-start.1 = (f32[64,128]{1,0:T(8,128)}, f32[64,128]{1,0:T(8,128)S(1)}, u32[]{:S(2)}, u32[]{:S(2)}) collective-permute-start(f32[64,128]{1,0:T(8,128)} %get-tuple-element.28.refs_0_), channel_id=1, source_target_pairs={{4,0},{5,1},{6,2},{7,3},{12,8},{13,9},{14,10},{15,11},{20,16},{21,... | collective-permute-start | bytes 98312 | tf_op jit(solution)/shard_map/ppermute | solution.py:219
  8.7 10.9 %collective-permute-start = (f32[64,128]{1,0:T(8,128)}, f32[64,128]{1,0:T(8,128)S(1)}, u32[]{:S(2)}, u32[]{:S(2)}) collective-permute-start(f32[64,128]{1,0:T(8,128)} %get-tuple-element.29), channel_id=1, source_target_pairs={{0,4},{1,5},{2,6},{3,7},{8,12},{9,13},{10,14},{11,15},{16,20},{17,... | collective-permute-start | bytes 98312 | tf_op jit(solution)/shard_map/ppermute | solution.py:219
  28.6 53.0 %all-to-all-start = ((f32[8,2,2,3,64,128]{5,4,3,2,1,0:T(8,128)}), f32[8,2,2,3,64,128]{5,4,3,2,1,0:T(8,128)S(1)}, u32[]{:S(2)}, u32[]{:S(2)}) async-start(f32[8,2,2,3,64,128]{5,4,3,2,1,0:T(8,128)} %flow.3.refs_6_), calls=%async_computation | async-start | bytes 6291456 | tf_op jit(solution)/shard_map/all_to_all | solution.py:558
  36.2 21.2 %copy-start.30 = (s32[64]{0:T(128)S(1)}, s32[64]{0:T(128)}, u32[]{:S(2)}) copy-start(s32[64]{0:T(128)} %param.10) | copy-start | bytes 772
  36.2 35.3 %copy-start.29 = (s32[128]{0:T(128)S(1)}, s32[128]{0:T(128)}, u32[]{:S(2)}) copy-start(s32[128]{0:T(128)} %param.11) | copy-start | bytes 1540
  48.9 22.7 %collective-permute-start.6 = (f32[3,32,128]{2,1,0:T(8,128)}, f32[3,32,128]{2,1,0:T(8,128)S(1)}, u32[]{:S(2)}, u32[]{:S(2)}) collective-permute-start(f32[3,32,128]{2,1,0:T(8,128)} %get-tuple-element.35), channel_id=1, source_target_pairs={{0,1},{1,2},{2,3},{4,5},{5,6},{6,7},{8,9},{9,10},{10,11},{12,13},{... | collective-permute-start | bytes 147464 | tf_op jit(solution)/shard_map/ppermute | solution.py:219
  52.2 20.1 %collective-permute-start.7 = (f32[3,32,128]{2,1,0:T(8,128)}, f32[3,32,128]{2,1,0:T(8,128)S(1)}, u32[]{:S(2)}, u32[]{:S(2)}) collective-permute-start(f32[3,32,128]{2,1,0:T(8,128)} %get-tuple-element.36), channel_id=1, source_target_pairs={{1,0},{2,1},{3,2},{5,4},{6,5},{7,6},{9,8},{10,9},{11,10},{13,12},{... | collective-permute-start | bytes 147464 | tf_op jit(solution)/shard_map/ppermute | solution.py:219
  53.5 5.8 %collective-permute-start.4 = (f32[64,128]{1,0:T(8,128)}, f32[64,128]{1,0:T(8,128)S(1)}, u32[]{:S(2)}, u32[]{:S(2)}) collective-permute-start(f32[64,128]{1,0:T(8,128)} %get-tuple-element.33), channel_id=1, source_target_pairs={{0,4},{1,5},{2,6},{3,7},{8,12},{9,13},{10,14},{11,15},{16,20},{17,... | collective-permute-start | bytes 98312 | tf_op jit(solution)/shard_map/ppermute | solution.py:219
  56.1 13.2 %collective-permute-start.5 = (f32[64,128]{1,0:T(8,128)}, f32[64,128]{1,0:T(8,128)S(1)}, u32[]{:S(2)}, u32[]{:S(2)}) collective-permute-start(f32[64,128]{1,0:T(8,128)} %get-tuple-element.34), channel_id=1, source_target_pairs={{4,0},{5,1},{6,2},{7,3},{12,8},{13,9},{14,10},{15,11},{20,16},{21,... | collective-permute-start | bytes 98312 | tf_op jit(solution)/shard_map/ppermute | solution.py:219
  57.5 29.5 %collective-permute-start.8 = (s32[64]{0:T(128)S(1)}, s32[64]{0:T(128)S(1)}, u32[]{:S(2)}, u32[]{:S(2)}) collective-permute-start(s32[64]{0:T(128)S(1)} %copy-done.30), channel_id=1, source_target_pairs={{0,1},{1,0},{2,3},{3,2},{4,5},{5,4},{6,7},{7,6},{8,9},{9,8},{10,11... | collective-permute-start | bytes 776 | tf_op jit(solution)/shard_map/ppermute | solution.py:431
  59.3 13.0 %copy-start.27 = (f32[64,128]{1,0:T(8,128)}, f32[64,128]{1,0:T(8,128)S(1)}, u32[]{:S(2)}) copy-start(f32[64,128]{1,0:T(8,128)S(1)} %collective-permute-done.4.refs_2_) | copy-start | bytes 98308
  59.3 27.7 %collective-permute-start.10 = (s32[64]{0:T(128)S(1)}, s32[64]{0:T(128)S(1)}, u32[]{:S(2)}, u32[]{:S(2)}) collective-permute-start(s32[64]{0:T(128)S(1)} %copy-done.30), channel_id=1, source_target_pairs={{0,3},{1,2},{2,1},{3,0},{4,7},{5,6},{6,5},{7,4},{8,11},{9,10},{10,... | collective-permute-start | bytes 776 | tf_op jit(solution)/shard_map/ppermute | solution.py:431
  69.4 17.6 %collective-permute-start.9 = (s32[64]{0:T(128)S(1)}, s32[64]{0:T(128)S(1)}, u32[]{:S(2)}, u32[]{:S(2)}) collective-permute-start(s32[64]{0:T(128)S(1)} %copy-done.30), channel_id=1, source_target_pairs={{0,2},{1,3},{2,0},{3,1},{4,6},{5,7},{6,4},{7,5},{8,10},{9,11},{10,... | collective-permute-start | bytes 776 | tf_op jit(solution)/shard_map/ppermute | solution.py:431
  71.6 16.9 %collective-permute-start.11 = (s32[128]{0:T(128)S(1)}, s32[128]{0:T(128)S(1)}, u32[]{:S(2)}, u32[]{:S(2)}) collective-permute-start(s32[128]{0:T(128)S(1)} %copy-done.29), channel_id=1, source_target_pairs={{0,4},{4,0},{1,5},{5,1},{2,6},{6,2},{3,7},{7,3},{8,12},{12,8},{9,1... | collective-permute-start | bytes 1544 | tf_op jit(solution)/shard_map/ppermute | solution.py:431
  83.2 41.5 %all-to-all-start.1 = ((f32[8,2,2,3,64,128]{5,4,3,2,1,0:T(8,128)}), f32[8,2,2,3,64,128]{5,4,3,2,1,0:T(8,128)S(1)}, u32[]{:S(2)}, u32[]{:S(2)}) async-start(f32[8,2,2,3,64,128]{5,4,3,2,1,0:T(8,128)} %after.34), calls=%async_computation.1 | async-start | bytes 6291456 | tf_op jit(solution)/shard_map/all_to_all | solution.py:564
  93.4 22.3 %collective-permute-start.13 = (f32[3,256,256]{2,1,0:T(8,128)}, f32[3,256,256]{2,1,0:T(8,128)}, u32[]{:S(2)}, u32[]{:S(2)}) collective-permute-start(f32[3,256,256]{2,1,0:T(8,128)} %get-tuple-element.40.refs_3_), channel_id=1, source_target_pairs={{0,8},{24,16},{1,9},{25,17},{2,10},{26,18},{3,11},{27,19},{4,12},{... | collective-permute-start | bytes 2359304 | tf_op jit(solution)/shard_map/ppermute | solution.py:578
  102.1 34.2 %collective-permute-start.15 = (f32[3,256,256]{2,1,0:T(8,128)}, f32[3,256,256]{2,1,0:T(8,128)}, u32[]{:S(2)}, u32[]{:S(2)}) collective-permute-start(f32[3,256,256]{2,1,0:T(8,128)} %get-tuple-element.41.refs_1_), channel_id=1, source_target_pairs={{0,8},{24,16},{1,9},{25,17},{2,10},{26,18},{3,11},{27,19},{4,12},{... | collective-permute-start | bytes 2359304 | tf_op jit(solution)/shard_map/ppermute | solution.py:578
  118.1 22.3 %collective-permute-start.14 = (f32[3,256,256]{2,1,0:T(8,128)}, f32[3,256,256]{2,1,0:T(8,128)}, u32[]{:S(2)}, u32[]{:S(2)}) collective-permute-start(f32[3,256,256]{2,1,0:T(8,128)} %add.69.refs_3_), channel_id=1, source_target_pairs={{8,16},{16,8},{9,17},{17,9},{10,18},{18,10},{11,19},{19,11},{12,20... | collective-permute-start | bytes 2359304 | tf_op jit(solution)/shard_map/ppermute | solution.py:593
  129.8 10.6 %copy-start.11 = (f32[3,256,256]{2,1,0:T(8,128)S(1)}, f32[3,256,256]{2,1,0:T(8,128)}, u32[]{:S(2)}) copy-start(f32[3,256,256]{2,1,0:T(8,128)} %get-tuple-element.39.refs_6_) | copy-start | bytes 2359300
  129.8 21.6 %collective-permute-start.18 = (f32[3,256,256]{2,1,0:T(8,128)}, f32[3,256,256]{2,1,0:T(8,128)}, u32[]{:S(2)}, u32[]{:S(2)}) collective-permute-start(f32[3,256,256]{2,1,0:T(8,128)} %get-tuple-element.42.refs_1_), channel_id=1, source_target_pairs={{0,8},{1,9},{2,10},{3,11},{4,12},{5,13},{6,14},{7,15}} | collective-permute-start | bytes 2359304 | tf_op jit(solution)/shard_map/ppermute | solution.py:578
  136.3 7.6 %copy-start.7 = (f32[2,3,128,256]{3,2,1,0:T(8,128)S(1)}, f32[2,3,128,256]{3,2,1,0:T(8,128)}, u32[]{:S(2)}) copy-start(f32[2,3,128,256]{3,2,1,0:T(8,128)} %after.31.refs_4_) | copy-start | bytes 2359300
  136.3 9.6 %copy-start.6 = (f32[4,3,64,256]{3,2,1,0:T(8,128)S(1)}, f32[4,3,64,256]{3,2,1,0:T(8,128)}, u32[]{:S(2)}) copy-start(f32[4,3,64,256]{3,2,1,0:T(8,128)} %after.35.refs_5_) | copy-start | bytes 2359300
  138.9 20.4 %collective-permute-start.17 = (f32[3,256,256]{2,1,0:T(8,128)}, f32[3,256,256]{2,1,0:T(8,128)}, u32[]{:S(2)}, u32[]{:S(2)}) collective-permute-start(f32[3,256,256]{2,1,0:T(8,128)} %add.70.refs_1_), channel_id=1, source_target_pairs={{8,16},{16,8},{9,17},{17,9},{10,18},{18,10},{11,19},{19,11},{12,20... | collective-permute-start | bytes 2359304 | tf_op jit(solution)/shard_map/ppermute | solution.py:593
  142.6 20.4 %collective-permute-start.16 = (f32[3,256,256]{2,1,0:T(8,128)}, f32[3,256,256]{2,1,0:T(8,128)S(1)}, u32[]{:S(2)}, u32[]{:S(2)}) collective-permute-start(f32[3,256,256]{2,1,0:T(8,128)} %add.71.refs_3_), channel_id=1, source_target_pairs={{8,0},{16,24},{9,1},{17,25},{10,2},{18,26},{11,3},{19,27},{12,4},{... | collective-permute-start | bytes 2359304 | tf_op jit(solution)/shard_map/ppermute | solution.py:598
  143.9 20.4 %collective-permute-start.12 = (f32[2,3,128,256]{3,2,1,0:T(8,128)S(1)}, f32[2,3,128,256]{3,2,1,0:T(8,128)}, u32[]{:S(2)}, u32[]{:S(2)}) collective-permute-start(f32[2,3,128,256]{3,2,1,0:T(8,128)S(1)} %copy-done.7), channel_id=1, source_target_pairs={{0,4},{4,0},{1,5},{5,1},{2,6},{6,2},{3,7},{7,3},{8,12},{12,8},{9,1... | collective-permute-start | bytes 2359304 | tf_op jit(solution)/shard_map/ppermute | solution.py:409
  145.9 18.5 %collective-permute-start.24 = (f32[4,3,64,256]{3,2,1,0:T(8,128)S(1)}, f32[4,3,64,256]{3,2,1,0:T(8,128)}, u32[]{:S(2)}, u32[]{:S(2)}) collective-permute-start(f32[4,3,64,256]{3,2,1,0:T(8,128)S(1)} %copy-done.6), channel_id=1, source_target_pairs={{0,2},{1,3},{2,0},{3,1},{4,6},{5,7},{6,4},{7,5},{8,10},{9,11},{10,... | collective-permute-start | bytes 2359304 | tf_op jit(solution)/shard_map/ppermute | solution.py:410
  151.4 9.4 %copy-start.10 = (f32[3,256,256]{2,1,0:T(8,128)S(1)}, f32[3,256,256]{2,1,0:T(8,128)}, u32[]{:S(2)}) copy-start(f32[3,256,256]{2,1,0:T(8,128)} %get-tuple-element.43.refs_6_) | copy-start | bytes 2359300
  151.4 19.6 %collective-permute-start.22 = (f32[3,256,256]{2,1,0:T(8,128)}, f32[3,256,256]{2,1,0:T(8,128)}, u32[]{:S(2)}, u32[]{:S(2)}) collective-permute-start(f32[3,256,256]{2,1,0:T(8,128)} %get-tuple-element.44.refs_1_), channel_id=1, source_target_pairs={{0,8},{1,9},{2,10},{3,11},{4,12},{5,13},{6,14},{7,15}} | collective-permute-start | bytes 2359304 | tf_op jit(solution)/shard_map/ppermute | solution.py:578
  159.3 14.2 %collective-permute-start.21 = (f32[3,256,256]{2,1,0:T(8,128)}, f32[3,256,256]{2,1,0:T(8,128)}, u32[]{:S(2)}, u32[]{:S(2)}) collective-permute-start(f32[3,256,256]{2,1,0:T(8,128)} %add.72.refs_1_), channel_id=1, source_target_pairs={{8,16},{16,8},{9,17},{17,9},{10,18},{18,10},{11,19},{19,11},{12,20... | collective-permute-start | bytes 2359304 | tf_op jit(solution)/shard_map/ppermute | solution.py:593
  163.0 19.1 %collective-permute-start.20 = (f32[3,256,256]{2,1,0:T(8,128)}, f32[3,256,256]{2,1,0:T(8,128)S(1)}, u32[]{:S(2)}, u32[]{:S(2)}) collective-permute-start(f32[3,256,256]{2,1,0:T(8,128)} %add.73.refs_1_), channel_id=1, source_target_pairs={{8,0},{16,24},{9,1},{17,25},{10,2},{18,26},{11,3},{19,27},{12,4},{... | collective-permute-start | bytes 2359304 | tf_op jit(solution)/shard_map/ppermute | solution.py:598
  164.3 19.8 %collective-permute-start.23 = (f32[4,3,64,256]{3,2,1,0:T(8,128)}, f32[4,3,64,256]{3,2,1,0:T(8,128)S(1)}, u32[]{:S(2)}, u32[]{:S(2)}) collective-permute-start(f32[4,3,64,256]{3,2,1,0:T(8,128)} %refs_3_.1), channel_id=1, source_target_pairs={{0,1},{1,0},{2,3},{3,2},{4,5},{5,4},{6,7},{7,6},{8,9},{9,8},{10,11... | collective-permute-start | bytes 2359304 | tf_op jit(solution)/shard_map/ppermute | solution.py:416
  164.4 20.6 %collective-permute-start.19 = (f32[2,3,128,256]{3,2,1,0:T(8,128)}, f32[2,3,128,256]{3,2,1,0:T(8,128)S(1)}, u32[]{:S(2)}, u32[]{:S(2)}) collective-permute-start(f32[2,3,128,256]{3,2,1,0:T(8,128)} %after.41.refs_1_), channel_id=1, source_target_pairs={{0,1},{1,0},{2,3},{3,2},{4,5},{5,4},{6,7},{7,6},{8,9},{9,8},{10,11... | collective-permute-start | bytes 2359304 | tf_op jit(solution)/shard_map/ppermute | solution.py:416
  164.9 10.0 %copy-start.12 = (f32[3,256,256]{2,1,0:T(8,128)S(1)}, f32[3,256,256]{2,1,0:T(8,128)}, u32[]{:S(2)}) copy-start(f32[3,256,256]{2,1,0:T(8,128)} %get-tuple-element.45.refs_6_) | copy-start | bytes 2359300
  171.0 14.9 %collective-permute-start.25 = (f32[4,3,64,256]{3,2,1,0:T(8,128)}, f32[4,3,64,256]{3,2,1,0:T(8,128)}, u32[]{:S(2)}, u32[]{:S(2)}) collective-permute-start(f32[4,3,64,256]{3,2,1,0:T(8,128)} %after.47.refs_5_), channel_id=1, source_target_pairs={{0,1},{1,0},{2,3},{3,2},{4,5},{5,4},{6,7},{7,6},{8,9},{9,8},{10,11... | collective-permute-start | bytes 2359304 | tf_op jit(solution)/shard_map/ppermute | solution.py:416
  173.4 25.9 %collective-permute-start.27 = (f32[3,256,256]{2,1,0:T(8,128)}, f32[3,256,256]{2,1,0:T(8,128)}, u32[]{:S(2)}, u32[]{:S(2)}) collective-permute-start(f32[3,256,256]{2,1,0:T(8,128)} %add.74.refs_1_), channel_id=1, source_target_pairs={{8,16},{16,8},{9,17},{17,9},{10,18},{18,10},{11,19},{19,11},{12,20... | collective-permute-start | bytes 2359304 | tf_op jit(solution)/shard_map/ppermute | solution.py:593
  182.1 19.9 %collective-permute-start.26 = (f32[3,256,256]{2,1,0:T(8,128)}, f32[3,256,256]{2,1,0:T(8,128)S(1)}, u32[]{:S(2)}, u32[]{:S(2)}) collective-permute-start(f32[3,256,256]{2,1,0:T(8,128)} %add.75.refs_1_), channel_id=1, source_target_pairs={{8,0},{16,24},{9,1},{17,25},{10,2},{18,26},{11,3},{19,27},{12,4},{... | collective-permute-start | bytes 2359304 | tf_op jit(solution)/shard_map/ppermute | solution.py:598
  200.7 18.9 %collective-permute-start.29 = (f32[3,256,256]{2,1,0:T(8,128)S(1)}, f32[3,256,256]{2,1,0:T(8,128)S(1)}, u32[]{:S(2)}, u32[]{:S(2)}) collective-permute-start(f32[3,256,256]{2,1,0:T(8,128)S(1)} %add.76.refs_1_), channel_id=1, source_target_pairs={{8,0},{16,24},{9,1},{17,25},{10,2},{18,26},{11,3},{19,27},{12,4},{... | collective-permute-start | bytes 2359304 | tf_op jit(solution)/shard_map/ppermute | solution.py:598
  209.5 17.6 %all-to-all-start.2 = ((f32[8,3,64,128]{3,2,1,0:T(8,128)}), f32[8,3,64,128]{3,2,1,0:T(8,128)S(1)}, u32[]{:S(2)}, u32[]{:S(2)}) async-start(f32[8,3,64,128]{3,2,1,0:T(8,128)} %sweep.5.refs_1_), calls=%async_computation.2 | async-start | bytes 1572864 | tf_op jit(solution)/shard_map/all_to_all | solution.py:620
  227.1 41.1 %copy-start.8 = (f32[8,3,64,128]{3,2,1,0:T(8,128)}, f32[8,3,64,128]{3,2,1,0:T(8,128)S(1)}, u32[]{:S(2)}) copy-start(f32[8,3,64,128]{3,2,1,0:T(8,128)S(1)} %all-to-all-done.2.refs_2_) | copy-start | bytes 2359300
  227.1 16.7 %all-to-all-start.3 = ((f32[8,3,64,128]{3,2,1,0:T(8,128)}), f32[8,3,64,128]{3,2,1,0:T(8,128)S(1)}, u32[]{:S(2)}, u32[]{:S(2)}) async-start(f32[8,3,64,128]{3,2,1,0:T(8,128)} %sweep.7), calls=%async_computation.3 | async-start | bytes 1572864 | tf_op jit(solution)/shard_map/all_to_all | solution.py:620
  231.2 45.0 %copy-start.1 = (s32[3,2]{0,1:T(2,128)S(1)}, s32[3,2]{0,1:T(2,128)}, u32[]{:S(2)}) copy-start(s32[3,2]{0,1:T(2,128)} %param.12) | copy-start | bytes 76
  231.2 20.5 %collective-permute-start.28 = (f32[8,3,64,128]{3,2,1,0:T(8,128)S(1)}, f32[8,3,64,128]{3,2,1,0:T(8,128)S(1)}, u32[]{:S(2)}, u32[]{:S(2)}) collective-permute-start(f32[8,3,64,128]{3,2,1,0:T(8,128)S(1)} %all-to-all-done.2.refs_2_), channel_id=1, source_target_pairs={{0,24},{1,25},{2,26},{3,27},{4,28},{5,29},{6,30},{7,31}} | collective-permute-start | bytes 2359304 | tf_op jit(solution)/shard_map/ppermute | solution.py:621
  243.8 24.3 %copy-start.9 = (f32[8,3,64,128]{3,2,1,0:T(8,128)}, f32[8,3,64,128]{3,2,1,0:T(8,128)S(1)}, u32[]{:S(2)}) copy-start(f32[8,3,64,128]{3,2,1,0:T(8,128)S(1)} %all-to-all-done.3.refs_3_) | copy-start | bytes 2359300
  243.8 24.3 %collective-permute-start.30 = (f32[8,3,64,128]{3,2,1,0:T(8,128)S(1)}, f32[8,3,64,128]{3,2,1,0:T(8,128)S(1)}, u32[]{:S(2)}, u32[]{:S(2)}) collective-permute-start(f32[8,3,64,128]{3,2,1,0:T(8,128)S(1)} %all-to-all-done.3.refs_3_), channel_id=1, source_target_pairs={{0,24},{1,25},{2,26},{3,27},{4,28},{5,29},{6,30},{7,31}} | collective-permute-start | bytes 2359304 | tf_op jit(solution)/shard_map/ppermute | solution.py:621
  251.7 16.5 %copy-start.19 = (f32[8,3,64,128]{3,2,1,0:T(8,128)}, f32[8,3,64,128]{3,2,1,0:T(8,128)S(1)}, u32[]{:S(2)}) copy-start(f32[8,3,64,128]{3,2,1,0:T(8,128)S(1)} %collective-permute-done.28.refs_0_) | copy-start | bytes 2359300
  (18 other events, 25.8 us)

commit v6 on v5

--- a/solution.py
+++ b/solution.py
@@ -508,30 +508,30 @@
     @pl.when(flag_ref[0] == 0)
     def _():
         for z in range(CZ):
-            turned[pl.ds(z, TILE_Y, stride=CZ), :] = u_ref[z, 0]
+            turned[pl.ds(z, TILE_Y // 2, stride=CZ), :] = u_ref[z, 0]
 
     @pl.when(flag_ref[0] > 0)
     def _():
         for z in range(CZ):
             g, i = divmod(z, per)
-            turned[pl.ds(z, TILE_Y, stride=CZ), :] = parts[i][g, 0]
+            turned[pl.ds(z, TILE_Y // 2, stride=CZ), :] = parts[i][g, 0]
 
     out_ref[0, 0] = turned[...].T
 
 
 def to_output(flag, planes, parts):
-    part = pl.BlockSpec(parts[0].shape[:1] + (1, TILE_Y, TILE_X), lambda c: (0, c, 0, 0))
+    part = pl.BlockSpec(parts[0].shape[:1] + (1, TILE_Y // 2, TILE_X), lambda c, h: (0, c, h, 0))
     return pl.pallas_call(
         output_kernel,
-        grid=(3,),
+        grid=(3, 2),
         in_specs=[
             pl.BlockSpec(memory_space=pltpu.SMEM),
-            pl.BlockSpec((CZ, 1, TILE_Y, TILE_X), lambda c: (0, c, 0, 0)),
+            pl.BlockSpec((CZ, 1, TILE_Y // 2, TILE_X), lambda c, h: (0, c, h, 0)),
         ]
         + [part] * (2 * CHUNKS),
-        out_specs=pl.BlockSpec((1, 1, TILE_X, TILE_Y * CZ), lambda c: (0, c, 0, 0)),
+        out_specs=pl.BlockSpec((1, 1, TILE_X, TILE_Y // 2 * CZ), lambda c, h: (0, c, 0, h)),
         out_shape=jax.ShapeDtypeStruct((1, 3, TILE_X, TILE_Y * CZ), f32),
-        scratch_shapes=[pltpu.VMEM((TILE_Y * CZ, TILE_X), f32)],
+        scratch_shapes=[pltpu.VMEM((TILE_Y // 2 * CZ, TILE_X), f32)],
         compiler_params=params(),
         name="to_output",
     )(flag, planes, *parts)

time: 278 us -> 279 us (level)
  no operation moved by 1% of the time
where the time goes in v6:
time: 279 us; the launch traced here: 277 us
  Pallas kernels  92 us (33%)
  starting transfers between devices  89 us (32%)
  waiting for transfers between devices  55.7 us (20%)
  other arithmetic  22 us (8%)
  local copies, waits for them, and re-layouts  17.8 us (6%)
    pallas_call x3, Pallas kernels, flow(): pl.pallas_call(body, grid=(groups,), in_specs=[pl.BlockSpec(memory_space=...  28.4 us
    pallas_call x4, Pallas kernels, sweep(): pl.pallas_call(body, grid=(3,), in_specs=[pl.BlockSpec((full_y, 1), lambd...  26.3 us
    ppermute x2, waiting for transfers between devices, local(): brought = [lax.ppermute(value, 'sec', [(0, 3)]) for value in tiles]  21.8 us
    ppermute x4, starting transfers between devices, placed(): lax.ppermute(fars[n], 'sec', [(0, 1), (3, 2)] if first else [(0, 1)])  19.2 us
    ppermute x8, starting transfers between devices, send(): lax.ppermute(value, axis, [(i, i + step) for i in range(count) if 0 <= i...  19 us
    ppermute x4, waiting for transfers between devices, placed(): lax.ppermute(fars[n], 'sec', [(0, 1), (3, 2)] if first else [(0, 1)])  18.2 us
    ppermute x4, starting transfers between devices, rows(): lax.ppermute(value, axis, [(i, i ^ step) for i in range(count)])  14.8 us
    pallas_call x4, Pallas kernels, place(): pl.pallas_call(body, grid=(1,), in_specs=[pl.BlockSpec(memory_space=pltpu...  14.2 us
  transfers between devices with their start and end apart: 35, of which 8 were waited for; matrix products, arithmetic and copies ran while one was open for 10% of the time, Pallas kernels for 27%

profile of v6, /device:TPU:0, one launch (start us, length us, event | category | flops | bytes accessed | tf_op | source)
XLA Modules:
  0.0 276.9 jit_solution(15129601515580161183)
XLA Ops:
  0.0 3.0 %tile_edges.1 = (f32[64,128]{1,0:T(8,128)}, f32[64,128]{1,0:T(8,128)}, f32[3,32,128]{2,1,0:T(8,128)}, f32[3,32,128]{2,1,0:T(8,128)}) custom-call(f32[3,128,2048]{2,1,0:T(8,128)} %bitcast.21, f32[3,128,2048]{2,1,0:T(8,128)} %bitcast.22, f32[3,128,2048]{2,1,0:T(8,128)} %bitcast.23, f32[3,128,2048]{2,1,0:T(8,128)} %bitcast.24), custom_call_target="tpu_custom_call" | custom-call | tf_op jit(solution)/shard_map/tile_edges/pallas_call | solution.py:56
  4.3 3.0 %collective-permute-start.2 = (f32[3,32,128]{2,1,0:T(8,128)}, f32[3,32,128]{2,1,0:T(8,128)S(1)}, u32[]{:S(2)}, u32[]{:S(2)}) collective-permute-start(f32[3,32,128]{2,1,0:T(8,128)} %get-tuple-element.30), channel_id=1, source_target_pairs={{0,1},{1,2},{2,3},{4,5},{5,6},{6,7},{8,9},{9,10},{10,11},{12,13},{... | collective-permute-start | bytes 147464 | tf_op jit(solution)/shard_map/ppermute | solution.py:219
  8.7 4.9 %collective-permute-start = (f32[64,128]{1,0:T(8,128)}, f32[64,128]{1,0:T(8,128)S(1)}, u32[]{:S(2)}, u32[]{:S(2)}) collective-permute-start(f32[64,128]{1,0:T(8,128)} %get-tuple-element.29), channel_id=1, source_target_pairs={{0,4},{1,5},{2,6},{3,7},{8,12},{9,13},{10,14},{11,15},{16,20},{17,... | collective-permute-start | bytes 98312 | tf_op jit(solution)/shard_map/ppermute | solution.py:219
  13.5 5.4 %to_planes.1.refs_1_ = f32[32,3,64,128]{3,2,1,0:T(8,128)} custom-call(f32[3,128,2048]{2,1,0:T(8,128)} %bitcast.25, f32[64,128]{1,0:T(8,128)} %get-tuple-element.28.refs_0_), custom_call_target="tpu_custom_call" | custom-call | tf_op jit(solution)/shard_map/to_planes/pallas_call | solution.py:89
  21.4 7.2 %flow.3.refs_6_ = f32[8,2,2,3,64,128]{5,4,3,2,1,0:T(8,128)} custom-call(s32[1]{0:T(128)} %bitcast.refs_0_.flag_ref, f32[32,3,64,128]{3,2,1,0:T(8,128)} %to_planes.1.refs_1_, f32[64,128]{1,0:T(8,128)} %after.27.refs_2_, f32[64,128]{1,0:T(8,128)} %after.28.refs_3_, f32[3,32,128]{2,1,0:T(8,128)} %after.29.refs_4_, f32[3,32,128]{2,1,0:T(8,128)} %after.30.refs_5_), custom_call_target="tpu_custom_call" | custom-call | tf_op jit(solution)/shard_map/flow/pallas_call | solution.py:197
  28.6 3.9 %all-to-all-start = ((f32[8,2,2,3,64,128]{5,4,3,2,1,0:T(8,128)}), f32[8,2,2,3,64,128]{5,4,3,2,1,0:T(8,128)S(1)}, u32[]{:S(2)}, u32[]{:S(2)}) async-start(f32[8,2,2,3,64,128]{5,4,3,2,1,0:T(8,128)} %flow.3.refs_6_), calls=%async_computation | async-start | bytes 6291456 | tf_op jit(solution)/shard_map/all_to_all | solution.py:558
  36.2 12.6 %flow.4 = (f32[32,3,64,128]{3,2,1,0:T(8,128)}, f32[64,128]{1,0:T(8,128)}, f32[64,128]{1,0:T(8,128)}, f32[3,32,128]{2,1,0:T(8,128)}, f32[3,32,128]{2,1,0:T(8,128)}) custom-call(s32[1]{0:T(128)} %bitcast.refs_0_.flag_ref, f32[32,3,64,128]{3,2,1,0:T(8,128)} %to_planes.1.refs_1_, f32[64,128]{1,0:T(8,128)} %after.27.refs_2_, f32[64,128]{1,0:T(8,128)} %after.28.refs_3_, ...), custom_call_target="tpu_custom_call" | custom-call | tf_op jit(solution)/shard_map/flow/pallas_call | solution.py:197
  48.9 3.3 %collective-permute-start.6 = (f32[3,32,128]{2,1,0:T(8,128)}, f32[3,32,128]{2,1,0:T(8,128)S(1)}, u32[]{:S(2)}, u32[]{:S(2)}) collective-permute-start(f32[3,32,128]{2,1,0:T(8,128)} %get-tuple-element.35), channel_id=1, source_target_pairs={{0,1},{1,2},{2,3},{4,5},{5,6},{6,7},{8,9},{9,10},{10,11},{12,13},{... | collective-permute-start | bytes 147464 | tf_op jit(solution)/shard_map/ppermute | solution.py:219
  53.5 2.7 collective-permute-start.4
  57.5 1.8 collective-permute-start.8
  59.3 10.1 %collective-permute-start.10 = (s32[64]{0:T(128)S(1)}, s32[64]{0:T(128)S(1)}, u32[]{:S(2)}, u32[]{:S(2)}) collective-permute-start(s32[64]{0:T(128)S(1)} %copy-done.30), channel_id=1, source_target_pairs={{0,3},{1,2},{2,1},{3,0},{4,7},{5,6},{6,5},{7,4},{8,11},{9,10},{10,... | collective-permute-start | bytes 776 | tf_op jit(solution)/shard_map/ppermute | solution.py:431
  69.4 2.2 collective-permute-start.9
  72.9 8.7 %flow.5 = (f32[8,2,2,3,64,128]{5,4,3,2,1,0:T(8,128)}, f32[32,3,64,128]{3,2,1,0:T(8,128)}) custom-call(s32[1]{0:T(128)} %bitcast.refs_0_.flag_ref, f32[32,3,64,128]{3,2,1,0:T(8,128)} %get-tuple-element.32.refs_1_, f32[64,128]{1,0:T(8,128)} %copy-done.27, f32[64,128]{1,0:T(8,128)} %copy-done.28, f32[3,32,128]{2,1,0:T(8,128)} %copy-done.25, ...), custom_call_target="tpu_custom_call" | custom-call | tf_op jit(solution)/shard_map/flow/pallas_call | solution.py:197
  83.2 3.7 %all-to-all-start.1 = ((f32[8,2,2,3,64,128]{5,4,3,2,1,0:T(8,128)}), f32[8,2,2,3,64,128]{5,4,3,2,1,0:T(8,128)S(1)}, u32[]{:S(2)}, u32[]{:S(2)}) async-start(f32[8,2,2,3,64,128]{5,4,3,2,1,0:T(8,128)} %after.34), calls=%async_computation.1 | async-start | bytes 6291456 | tf_op jit(solution)/shard_map/all_to_all | solution.py:564
  89.7 3.7 %place.4 = (f32[3,256,256]{2,1,0:T(8,128)}, f32[3,256,256]{2,1,0:T(8,128)}) custom-call(s32[4]{0:T(128)} %pad_add_fusion.2.refs_7_.refs_0_, f32[3,3]{1,0:T(4,128)} %select_bitcast_fusion.refs_8_.refs_1_, f32[8,2,2,3,64,128]{5,4,3,2,1,0:T(8,128)} %after.32.refs_2_.refs_1_, s32[256,1]{1,0:T(8,128)} %select_n.92.refs_3_.refs_0_, s32[1,256]{1,0:T(1,128)} %bitcast.26), custom_call_target="tpu_custom_call" | custom-call | tf_op jit(solution)/shard_map/place/pallas_call | solution.py:303
  93.4 5.1 %collective-permute-start.13 = (f32[3,256,256]{2,1,0:T(8,128)}, f32[3,256,256]{2,1,0:T(8,128)}, u32[]{:S(2)}, u32[]{:S(2)}) collective-permute-start(f32[3,256,256]{2,1,0:T(8,128)} %get-tuple-element.40.refs_3_), channel_id=1, source_target_pairs={{0,8},{24,16},{1,9},{25,17},{2,10},{26,18},{3,11},{27,19},{4,12},{... | collective-permute-start | bytes 2359304 | tf_op jit(solution)/shard_map/ppermute | solution.py:578
  98.4 3.7 %place.5 = (f32[3,256,256]{2,1,0:T(8,128)}, f32[3,256,256]{2,1,0:T(8,128)}) custom-call(s32[4]{0:T(128)} %pad_add_fusion.2.refs_7_.refs_0_, f32[3,3]{1,0:T(4,128)} %select_bitcast_fusion.refs_8_.refs_1_, f32[8,2,2,3,64,128]{5,4,3,2,1,0:T(8,128)} %after.32.refs_2_.refs_1_, f32[3,256,256]{2,1,0:T(8,128)} %get-tuple-element.40.refs_3_), custom_call_target="tpu_custom_call" | custom-call | tf_op jit(solution)/shard_map/place/pallas_call | solution.py:303
  102.1 2.2 collective-permute-start.15
  104.3 11.4 %collective-permute-done.13.refs_0_ = f32[3,256,256]{2,1,0:T(8,128)} collective-permute-done((f32[3,256,256]{2,1,0:T(8,128)}, f32[3,256,256]{2,1,0:T(8,128)}, u32[]{:S(2)}, u32[]{:S(2)}) %collective-permute-start.13) | collective-permute-done | bytes 786464 | tf_op jit(solution)/shard_map/ppermute | solution.py:578
  115.7 2.4 add.69.refs_3_
  119.6 2.1 copy.48.refs_0_
  121.8 2.1 constant_dynamic-slice_fusion.refs_0_
  126.4 3.4 %place.6 = (f32[3,256,256]{2,1,0:T(8,128)}, f32[3,256,256]{2,1,0:T(8,128)}) custom-call(s32[4]{0:T(128)} %pad_add_fusion.2.refs_7_.refs_0_, f32[3,3]{1,0:T(4,128)} %select_bitcast_fusion.refs_8_.refs_1_, f32[8,2,2,3,64,128]{5,4,3,2,1,0:T(8,128)} %copy-done.3, f32[3,256,256]{2,1,0:T(8,128)} %add.69.refs_3_, f32[2,3,128,256]{3,2,1,0:T(8,128)} %after.31.refs_4_, ...), custom_call_target="tpu_custom_call" | custom-call | tf_op jit(solution)/shard_map/place/pallas_call | solution.py:303
  129.8 6.5 %collective-permute-start.18 = (f32[3,256,256]{2,1,0:T(8,128)}, f32[3,256,256]{2,1,0:T(8,128)}, u32[]{:S(2)}, u32[]{:S(2)}) collective-permute-start(f32[3,256,256]{2,1,0:T(8,128)} %get-tuple-element.42.refs_1_), channel_id=1, source_target_pairs={{0,8},{1,9},{2,10},{3,11},{4,12},{5,13},{6,14},{7,15}} | collective-permute-start | bytes 2359304 | tf_op jit(solution)/shard_map/ppermute | solution.py:578
  136.3 2.5 add.70.refs_1_
  140.4 2.2 add.71.refs_3_
  143.9 2.0 collective-permute-start.12
  147.4 3.4 %place.7 = (f32[3,256,256]{2,1,0:T(8,128)}, f32[3,256,256]{2,1,0:T(8,128)}) custom-call(s32[4]{0:T(128)} %pad_add_fusion.2.refs_7_.refs_0_, f32[3,3]{1,0:T(4,128)} %select_bitcast_fusion.refs_8_.refs_1_, f32[8,2,2,3,64,128]{5,4,3,2,1,0:T(8,128)} %copy-done.3, f32[3,256,256]{2,1,0:T(8,128)} %add.71.refs_3_), custom_call_target="tpu_custom_call" | custom-call | tf_op jit(solution)/shard_map/place/pallas_call | solution.py:303
  151.4 5.5 %collective-permute-start.22 = (f32[3,256,256]{2,1,0:T(8,128)}, f32[3,256,256]{2,1,0:T(8,128)}, u32[]{:S(2)}, u32[]{:S(2)}) collective-permute-start(f32[3,256,256]{2,1,0:T(8,128)} %get-tuple-element.44.refs_1_), channel_id=1, source_target_pairs={{0,8},{1,9},{2,10},{3,11},{4,12},{5,13},{6,14},{7,15}} | collective-permute-start | bytes 2359304 | tf_op jit(solution)/shard_map/ppermute | solution.py:578
  156.9 2.3 add.72.refs_1_
  160.8 2.2 add.73.refs_1_
  164.9 6.1 %collective-permute-done.22.refs_0_ = f32[3,256,256]{2,1,0:T(8,128)} collective-permute-done((f32[3,256,256]{2,1,0:T(8,128)}, f32[3,256,256]{2,1,0:T(8,128)}, u32[]{:S(2)}, u32[]{:S(2)}) %collective-permute-start.22) | collective-permute-done | bytes 786464 | tf_op jit(solution)/shard_map/ppermute | solution.py:578
  171.0 2.4 add.74.refs_1_
  175.0 2.2 add.75.refs_1_
  177.2 4.9 %collective-permute-done.20.refs_0_ = f32[3,256,256]{2,1,0:T(8,128)S(1)} collective-permute-done((f32[3,256,256]{2,1,0:T(8,128)}, f32[3,256,256]{2,1,0:T(8,128)S(1)}, u32[]{:S(2)}, u32[]{:S(2)}) %collective-permute-start.20) | collective-permute-done | bytes 786464 | tf_op jit(solution)/shard_map/ppermute | solution.py:598
  186.0 6.8 %operators.1 = (bf16[4,3,256,256]{3,2,1,0:T(8,128)(2,1)}, bf16[4,3,256,256]{3,2,1,0:T(8,128)(2,1)}, bf16[4,3,256,256]{3,2,1,0:T(8,128)(2,1)}, bf16[4,3,256,256]{3,2,1,0:T(8,128)(2,1)}) custom-call(s32[3]{0:T(128)} %pad_add_fusion.3.pos_ref, f32[4,3,128,256]{3,2,1,0:T(8,128)} %refs_0_.2, f32[2,3,128,256]{3,2,1,0:T(8,128)} %after.41.refs_1_, ...), custom_call_target="tpu_custom_call" | custom-call | tf_op jit(solution)/shard_map/operators/pallas_call | solution.py:392
  192.8 6.5 %sweep.4.refs_1_.refs_8_ = f32[3,256,256]{2,1,0:T(8,128)} custom-call(s32[256,1]{1,0:T(8,128)} %select_n.92.refs_3_.refs_0_, s32[1,256]{1,0:T(1,128)} %bitcast.27, bf16[4,3,256,256]{3,2,1,0:T(8,128)(2,1)} %get-tuple-element.46.refs_1_.refs_2_, bf16[4,3,256,256]{3,2,1,0:T(8,128)(2,1)} %get-tuple-element.47.refs_2_.refs_3_, ...), custom_call_target="tpu_custom_call" | custom-call | tf_op jit(solution)/shard_map/sweep/pallas_call | solution.py:484
  202.9 6.6 %sweep.5.refs_1_ = f32[8,3,64,128]{3,2,1,0:T(8,128)} custom-call(s32[256,1]{1,0:T(8,128)} %select_n.92.refs_3_.refs_0_, s32[1,256]{1,0:T(1,128)} %bitcast.28, bf16[4,3,256,256]{3,2,1,0:T(8,128)(2,1)} %get-tuple-element.46.refs_1_.refs_2_, bf16[4,3,256,256]{3,2,1,0:T(8,128)(2,1)} %get-tuple-element.47.refs_2_.refs_3_, ...), custom_call_target="tpu_custom_call" | custom-call | tf_op jit(solution)/shard_map/sweep/pallas_call | solution.py:484
  209.5 3.5 %all-to-all-start.2 = ((f32[8,3,64,128]{3,2,1,0:T(8,128)}), f32[8,3,64,128]{3,2,1,0:T(8,128)S(1)}, u32[]{:S(2)}, u32[]{:S(2)}) async-start(f32[8,3,64,128]{3,2,1,0:T(8,128)} %sweep.5.refs_1_), calls=%async_computation.2 | async-start | bytes 1572864 | tf_op jit(solution)/shard_map/all_to_all | solution.py:620
  213.1 6.5 %sweep.6.refs_1_.refs_8_ = f32[3,256,256]{2,1,0:T(8,128)} custom-call(s32[256,1]{1,0:T(8,128)} %select_n.92.refs_3_.refs_0_, s32[1,256]{1,0:T(1,128)} %bitcast.29, bf16[4,3,256,256]{3,2,1,0:T(8,128)(2,1)} %get-tuple-element.46.refs_1_.refs_2_, bf16[4,3,256,256]{3,2,1,0:T(8,128)(2,1)} %get-tuple-element.47.refs_2_.refs_3_, ...), custom_call_target="tpu_custom_call" | custom-call | tf_op jit(solution)/shard_map/sweep/pallas_call | solution.py:484
  220.5 6.6 %sweep.7 = f32[8,3,64,128]{3,2,1,0:T(8,128)} custom-call(s32[256,1]{1,0:T(8,128)} %select_n.92.refs_3_.refs_0_, s32[1,256]{1,0:T(1,128)} %bitcast.30, bf16[4,3,256,256]{3,2,1,0:T(8,128)(2,1)} %get-tuple-element.46.refs_1_.refs_2_, bf16[4,3,256,256]{3,2,1,0:T(8,128)(2,1)} %get-tuple-element.47.refs_2_.refs_3_, ...), custom_call_target="tpu_custom_call" | custom-call | tf_op jit(solution)/shard_map/sweep/pallas_call | solution.py:484
  227.1 4.1 %all-to-all-start.3 = ((f32[8,3,64,128]{3,2,1,0:T(8,128)}), f32[8,3,64,128]{3,2,1,0:T(8,128)S(1)}, u32[]{:S(2)}, u32[]{:S(2)}) async-start(f32[8,3,64,128]{3,2,1,0:T(8,128)} %sweep.7), calls=%async_computation.3 | async-start | bytes 1572864 | tf_op jit(solution)/shard_map/all_to_all | solution.py:620
  231.2 2.7 collective-permute-start.28
  233.9 9.9 %all-to-all-done.3.refs_3_ = f32[8,3,64,128]{3,2,1,0:T(8,128)S(1)} async-done(((f32[8,3,64,128]{3,2,1,0:T(8,128)}), f32[8,3,64,128]{3,2,1,0:T(8,128)S(1)}, u32[]{:S(2)}, u32[]{:S(2)}) %all-to-all-start.3) | async-done | bytes 786464 | tf_op jit(solution)/shard_map/all_to_all | solution.py:620
  243.8 2.6 collective-permute-start.30
  246.4 5.3 %collective-permute-done.28.refs_0_ = f32[8,3,64,128]{3,2,1,0:T(8,128)S(1)} collective-permute-done((f32[8,3,64,128]{3,2,1,0:T(8,128)S(1)}, f32[8,3,64,128]{3,2,1,0:T(8,128)S(1)}, u32[]{:S(2)}, u32[]{:S(2)}) %collective-permute-start.28) | collective-permute-done | bytes 786464 | tf_op jit(solution)/shard_map/ppermute | solution.py:621
  251.7 16.5 %collective-permute-done.30.refs_1_ = f32[8,3,64,128]{3,2,1,0:T(8,128)S(1)} collective-permute-done((f32[8,3,64,128]{3,2,1,0:T(8,128)S(1)}, f32[8,3,64,128]{3,2,1,0:T(8,128)S(1)}, u32[]{:S(2)}, u32[]{:S(2)}) %collective-permute-start.30) | collective-permute-done | bytes 786464 | tf_op jit(solution)/shard_map/ppermute | solution.py:621
  269.1 7.8 %to_output.1 = f32[1,3,128,2048]{3,2,1,0:T(8,128)} custom-call(s32[1]{0:T(128)} %bitcast.refs_0_.flag_ref, f32[32,3,64,128]{3,2,1,0:T(8,128)} %get-tuple-element.37.refs_1_.u_ref, f32[8,3,64,128]{3,2,1,0:T(8,128)} %copy-done.19, f32[8,3,64,128]{3,2,1,0:T(8,128)} %copy-done.20, f32[8,3,64,128]{3,2,1,0:T(8,128)} %copy-done.8, f32[8,3,64,128]{3,2,1,0:T(8,128)} %copy-done.9), custom_call_target="tpu_custom_call" | custom-call | tf_op jit(solution)/shard_map/to_output/pallas_call | solution.py:524
  (154 shorter events, 40.2 us)
Async XLA Ops:
  0.0 32.5 %copy-start = (s32[3,2]{0,1:T(2,128)S(1)}, s32[3,2]{0,1:T(2,128)}, u32[]{:S(2)}) copy-start(s32[3,2]{0,1:T(2,128)} %param.12) | copy-start | bytes 76
  3.0 17.1 %collective-permute-start.3 = (f32[3,32,128]{2,1,0:T(8,128)}, f32[3,32,128]{2,1,0:T(8,128)S(1)}, u32[]{:S(2)}, u32[]{:S(2)}) collective-permute-start(f32[3,32,128]{2,1,0:T(8,128)} %get-tuple-element.31), channel_id=1, source_target_pairs={{1,0},{2,1},{3,2},{5,4},{6,5},{7,6},{9,8},{10,9},{11,10},{13,12},{... | collective-permute-start | bytes 147464 | tf_op jit(solution)/shard_map/ppermute | solution.py:219
  4.3 16.5 %collective-permute-start.2 = (f32[3,32,128]{2,1,0:T(8,128)}, f32[3,32,128]{2,1,0:T(8,128)S(1)}, u32[]{:S(2)}, u32[]{:S(2)}) collective-permute-start(f32[3,32,128]{2,1,0:T(8,128)} %get-tuple-element.30), channel_id=1, source_target_pairs={{0,1},{1,2},{2,3},{4,5},{5,6},{6,7},{8,9},{9,10},{10,11},{12,13},{... | collective-permute-start | bytes 147464 | tf_op jit(solution)/shard_map/ppermute | solution.py:219
  7.4 11.6 %collective-permute-start.1 = (f32[64,128]{1,0:T(8,128)}, f32[64,128]{1,0:T(8,128)S(1)}, u32[]{:S(2)}, u32[]{:S(2)}) collective-permute-start(f32[64,128]{1,0:T(8,128)} %get-tuple-element.28.refs_0_), channel_id=1, source_target_pairs={{4,0},{5,1},{6,2},{7,3},{12,8},{13,9},{14,10},{15,11},{20,16},{21,... | collective-permute-start | bytes 98312 | tf_op jit(solution)/shard_map/ppermute | solution.py:219
  8.7 10.9 %collective-permute-start = (f32[64,128]{1,0:T(8,128)}, f32[64,128]{1,0:T(8,128)S(1)}, u32[]{:S(2)}, u32[]{:S(2)}) collective-permute-start(f32[64,128]{1,0:T(8,128)} %get-tuple-element.29), channel_id=1, source_target_pairs={{0,4},{1,5},{2,6},{3,7},{8,12},{9,13},{10,14},{11,15},{16,20},{17,... | collective-permute-start | bytes 98312 | tf_op jit(solution)/shard_map/ppermute | solution.py:219
  28.6 53.0 %all-to-all-start = ((f32[8,2,2,3,64,128]{5,4,3,2,1,0:T(8,128)}), f32[8,2,2,3,64,128]{5,4,3,2,1,0:T(8,128)S(1)}, u32[]{:S(2)}, u32[]{:S(2)}) async-start(f32[8,2,2,3,64,128]{5,4,3,2,1,0:T(8,128)} %flow.3.refs_6_), calls=%async_computation | async-start | bytes 6291456 | tf_op jit(solution)/shard_map/all_to_all | solution.py:558
  36.2 21.2 %copy-start.30 = (s32[64]{0:T(128)S(1)}, s32[64]{0:T(128)}, u32[]{:S(2)}) copy-start(s32[64]{0:T(128)} %param.10) | copy-start | bytes 772
  36.2 35.3 %copy-start.29 = (s32[128]{0:T(128)S(1)}, s32[128]{0:T(128)}, u32[]{:S(2)}) copy-start(s32[128]{0:T(128)} %param.11) | copy-start | bytes 1540
  48.9 22.7 %collective-permute-start.6 = (f32[3,32,128]{2,1,0:T(8,128)}, f32[3,32,128]{2,1,0:T(8,128)S(1)}, u32[]{:S(2)}, u32[]{:S(2)}) collective-permute-start(f32[3,32,128]{2,1,0:T(8,128)} %get-tuple-element.35), channel_id=1, source_target_pairs={{0,1},{1,2},{2,3},{4,5},{5,6},{6,7},{8,9},{9,10},{10,11},{12,13},{... | collective-permute-start | bytes 147464 | tf_op jit(solution)/shard_map/ppermute | solution.py:219
  52.2 20.1 %collective-permute-start.7 = (f32[3,32,128]{2,1,0:T(8,128)}, f32[3,32,128]{2,1,0:T(8,128)S(1)}, u32[]{:S(2)}, u32[]{:S(2)}) collective-permute-start(f32[3,32,128]{2,1,0:T(8,128)} %get-tuple-element.36), channel_id=1, source_target_pairs={{1,0},{2,1},{3,2},{5,4},{6,5},{7,6},{9,8},{10,9},{11,10},{13,12},{... | collective-permute-start | bytes 147464 | tf_op jit(solution)/shard_map/ppermute | solution.py:219
  53.5 5.8 %collective-permute-start.4 = (f32[64,128]{1,0:T(8,128)}, f32[64,128]{1,0:T(8,128)S(1)}, u32[]{:S(2)}, u32[]{:S(2)}) collective-permute-start(f32[64,128]{1,0:T(8,128)} %get-tuple-element.33), channel_id=1, source_target_pairs={{0,4},{1,5},{2,6},{3,7},{8,12},{9,13},{10,14},{11,15},{16,20},{17,... | collective-permute-start | bytes 98312 | tf_op jit(solution)/shard_map/ppermute | solution.py:219
  56.1 13.2 %collective-permute-start.5 = (f32[64,128]{1,0:T(8,128)}, f32[64,128]{1,0:T(8,128)S(1)}, u32[]{:S(2)}, u32[]{:S(2)}) collective-permute-start(f32[64,128]{1,0:T(8,128)} %get-tuple-element.34), channel_id=1, source_target_pairs={{4,0},{5,1},{6,2},{7,3},{12,8},{13,9},{14,10},{15,11},{20,16},{21,... | collective-permute-start | bytes 98312 | tf_op jit(solution)/shard_map/ppermute | solution.py:219
  57.5 29.5 %collective-permute-start.8 = (s32[64]{0:T(128)S(1)}, s32[64]{0:T(128)S(1)}, u32[]{:S(2)}, u32[]{:S(2)}) collective-permute-start(s32[64]{0:T(128)S(1)} %copy-done.30), channel_id=1, source_target_pairs={{0,1},{1,0},{2,3},{3,2},{4,5},{5,4},{6,7},{7,6},{8,9},{9,8},{10,11... | collective-permute-start | bytes 776 | tf_op jit(solution)/shard_map/ppermute | solution.py:431
  59.3 13.0 %copy-start.27 = (f32[64,128]{1,0:T(8,128)}, f32[64,128]{1,0:T(8,128)S(1)}, u32[]{:S(2)}) copy-start(f32[64,128]{1,0:T(8,128)S(1)} %collective-permute-done.4.refs_2_) | copy-start | bytes 98308
  59.3 27.7 %collective-permute-start.10 = (s32[64]{0:T(128)S(1)}, s32[64]{0:T(128)S(1)}, u32[]{:S(2)}, u32[]{:S(2)}) collective-permute-start(s32[64]{0:T(128)S(1)} %copy-done.30), channel_id=1, source_target_pairs={{0,3},{1,2},{2,1},{3,0},{4,7},{5,6},{6,5},{7,4},{8,11},{9,10},{10,... | collective-permute-start | bytes 776 | tf_op jit(solution)/shard_map/ppermute | solution.py:431
  69.4 17.6 %collective-permute-start.9 = (s32[64]{0:T(128)S(1)}, s32[64]{0:T(128)S(1)}, u32[]{:S(2)}, u32[]{:S(2)}) collective-permute-start(s32[64]{0:T(128)S(1)} %copy-done.30), channel_id=1, source_target_pairs={{0,2},{1,3},{2,0},{3,1},{4,6},{5,7},{6,4},{7,5},{8,10},{9,11},{10,... | collective-permute-start | bytes 776 | tf_op jit(solution)/shard_map/ppermute | solution.py:431
  71.6 16.9 %collective-permute-start.11 = (s32[128]{0:T(128)S(1)}, s32[128]{0:T(128)S(1)}, u32[]{:S(2)}, u32[]{:S(2)}) collective-permute-start(s32[128]{0:T(128)S(1)} %copy-done.29), channel_id=1, source_target_pairs={{0,4},{4,0},{1,5},{5,1},{2,6},{6,2},{3,7},{7,3},{8,12},{12,8},{9,1... | collective-permute-start | bytes 1544 | tf_op jit(solution)/shard_map/ppermute | solution.py:431
  83.2 41.5 %all-to-all-start.1 = ((f32[8,2,2,3,64,128]{5,4,3,2,1,0:T(8,128)}), f32[8,2,2,3,64,128]{5,4,3,2,1,0:T(8,128)S(1)}, u32[]{:S(2)}, u32[]{:S(2)}) async-start(f32[8,2,2,3,64,128]{5,4,3,2,1,0:T(8,128)} %after.34), calls=%async_computation.1 | async-start | bytes 6291456 | tf_op jit(solution)/shard_map/all_to_all | solution.py:564
  93.4 22.3 %collective-permute-start.13 = (f32[3,256,256]{2,1,0:T(8,128)}, f32[3,256,256]{2,1,0:T(8,128)}, u32[]{:S(2)}, u32[]{:S(2)}) collective-permute-start(f32[3,256,256]{2,1,0:T(8,128)} %get-tuple-element.40.refs_3_), channel_id=1, source_target_pairs={{0,8},{24,16},{1,9},{25,17},{2,10},{26,18},{3,11},{27,19},{4,12},{... | collective-permute-start | bytes 2359304 | tf_op jit(solution)/shard_map/ppermute | solution.py:578
  102.1 34.2 %collective-permute-start.15 = (f32[3,256,256]{2,1,0:T(8,128)}, f32[3,256,256]{2,1,0:T(8,128)}, u32[]{:S(2)}, u32[]{:S(2)}) collective-permute-start(f32[3,256,256]{2,1,0:T(8,128)} %get-tuple-element.41.refs_1_), channel_id=1, source_target_pairs={{0,8},{24,16},{1,9},{25,17},{2,10},{26,18},{3,11},{27,19},{4,12},{... | collective-permute-start | bytes 2359304 | tf_op jit(solution)/shard_map/ppermute | solution.py:578
  118.1 22.3 %collective-permute-start.14 = (f32[3,256,256]{2,1,0:T(8,128)}, f32[3,256,256]{2,1,0:T(8,128)}, u32[]{:S(2)}, u32[]{:S(2)}) collective-permute-start(f32[3,256,256]{2,1,0:T(8,128)} %add.69.refs_3_), channel_id=1, source_target_pairs={{8,16},{16,8},{9,17},{17,9},{10,18},{18,10},{11,19},{19,11},{12,20... | collective-permute-start | bytes 2359304 | tf_op jit(solution)/shard_map/ppermute | solution.py:593
  129.8 10.6 %copy-start.11 = (f32[3,256,256]{2,1,0:T(8,128)S(1)}, f32[3,256,256]{2,1,0:T(8,128)}, u32[]{:S(2)}) copy-start(f32[3,256,256]{2,1,0:T(8,128)} %get-tuple-element.39.refs_6_) | copy-start | bytes 2359300
  129.8 21.6 %collective-permute-start.18 = (f32[3,256,256]{2,1,0:T(8,128)}, f32[3,256,256]{2,1,0:T(8,128)}, u32[]{:S(2)}, u32[]{:S(2)}) collective-permute-start(f32[3,256,256]{2,1,0:T(8,128)} %get-tuple-element.42.refs_1_), channel_id=1, source_target_pairs={{0,8},{1,9},{2,10},{3,11},{4,12},{5,13},{6,14},{7,15}} | collective-permute-start | bytes 2359304 | tf_op jit(solution)/shard_map/ppermute | solution.py:578
  136.3 7.6 %copy-start.7 = (f32[2,3,128,256]{3,2,1,0:T(8,128)S(1)}, f32[2,3,128,256]{3,2,1,0:T(8,128)}, u32[]{:S(2)}) copy-start(f32[2,3,128,256]{3,2,1,0:T(8,128)} %after.31.refs_4_) | copy-start | bytes 2359300
  136.3 9.6 %copy-start.6 = (f32[4,3,64,256]{3,2,1,0:T(8,128)S(1)}, f32[4,3,64,256]{3,2,1,0:T(8,128)}, u32[]{:S(2)}) copy-start(f32[4,3,64,256]{3,2,1,0:T(8,128)} %after.35.refs_5_) | copy-start | bytes 2359300
  138.9 20.4 %collective-permute-start.17 = (f32[3,256,256]{2,1,0:T(8,128)}, f32[3,256,256]{2,1,0:T(8,128)}, u32[]{:S(2)}, u32[]{:S(2)}) collective-permute-start(f32[3,256,256]{2,1,0:T(8,128)} %add.70.refs_1_), channel_id=1, source_target_pairs={{8,16},{16,8},{9,17},{17,9},{10,18},{18,10},{11,19},{19,11},{12,20... | collective-permute-start | bytes 2359304 | tf_op jit(solution)/shard_map/ppermute | solution.py:593
  142.6 20.4 %collective-permute-start.16 = (f32[3,256,256]{2,1,0:T(8,128)}, f32[3,256,256]{2,1,0:T(8,128)S(1)}, u32[]{:S(2)}, u32[]{:S(2)}) collective-permute-start(f32[3,256,256]{2,1,0:T(8,128)} %add.71.refs_3_), channel_id=1, source_target_pairs={{8,0},{16,24},{9,1},{17,25},{10,2},{18,26},{11,3},{19,27},{12,4},{... | collective-permute-start | bytes 2359304 | tf_op jit(solution)/shard_map/ppermute | solution.py:598
  143.9 20.4 %collective-permute-start.12 = (f32[2,3,128,256]{3,2,1,0:T(8,128)S(1)}, f32[2,3,128,256]{3,2,1,0:T(8,128)}, u32[]{:S(2)}, u32[]{:S(2)}) collective-permute-start(f32[2,3,128,256]{3,2,1,0:T(8,128)S(1)} %copy-done.7), channel_id=1, source_target_pairs={{0,4},{4,0},{1,5},{5,1},{2,6},{6,2},{3,7},{7,3},{8,12},{12,8},{9,1... | collective-permute-start | bytes 2359304 | tf_op jit(solution)/shard_map/ppermute | solution.py:409
  145.9 18.5 %collective-permute-start.24 = (f32[4,3,64,256]{3,2,1,0:T(8,128)S(1)}, f32[4,3,64,256]{3,2,1,0:T(8,128)}, u32[]{:S(2)}, u32[]{:S(2)}) collective-permute-start(f32[4,3,64,256]{3,2,1,0:T(8,128)S(1)} %copy-done.6), channel_id=1, source_target_pairs={{0,2},{1,3},{2,0},{3,1},{4,6},{5,7},{6,4},{7,5},{8,10},{9,11},{10,... | collective-permute-start | bytes 2359304 | tf_op jit(solution)/shard_map/ppermute | solution.py:410
  151.4 9.4 %copy-start.10 = (f32[3,256,256]{2,1,0:T(8,128)S(1)}, f32[3,256,256]{2,1,0:T(8,128)}, u32[]{:S(2)}) copy-start(f32[3,256,256]{2,1,0:T(8,128)} %get-tuple-element.43.refs_6_) | copy-start | bytes 2359300
  151.4 19.6 %collective-permute-start.22 = (f32[3,256,256]{2,1,0:T(8,128)}, f32[3,256,256]{2,1,0:T(8,128)}, u32[]{:S(2)}, u32[]{:S(2)}) collective-permute-start(f32[3,256,256]{2,1,0:T(8,128)} %get-tuple-element.44.refs_1_), channel_id=1, source_target_pairs={{0,8},{1,9},{2,10},{3,11},{4,12},{5,13},{6,14},{7,15}} | collective-permute-start | bytes 2359304 | tf_op jit(solution)/shard_map/ppermute | solution.py:578
  159.3 14.2 %collective-permute-start.21 = (f32[3,256,256]{2,1,0:T(8,128)}, f32[3,256,256]{2,1,0:T(8,128)}, u32[]{:S(2)}, u32[]{:S(2)}) collective-permute-start(f32[3,256,256]{2,1,0:T(8,128)} %add.72.refs_1_), channel_id=1, source_target_pairs={{8,16},{16,8},{9,17},{17,9},{10,18},{18,10},{11,19},{19,11},{12,20... | collective-permute-start | bytes 2359304 | tf_op jit(solution)/shard_map/ppermute | solution.py:593
  163.0 19.1 %collective-permute-start.20 = (f32[3,256,256]{2,1,0:T(8,128)}, f32[3,256,256]{2,1,0:T(8,128)S(1)}, u32[]{:S(2)}, u32[]{:S(2)}) collective-permute-start(f32[3,256,256]{2,1,0:T(8,128)} %add.73.refs_1_), channel_id=1, source_target_pairs={{8,0},{16,24},{9,1},{17,25},{10,2},{18,26},{11,3},{19,27},{12,4},{... | collective-permute-start | bytes 2359304 | tf_op jit(solution)/shard_map/ppermute | solution.py:598
  164.3 19.8 %collective-permute-start.23 = (f32[4,3,64,256]{3,2,1,0:T(8,128)}, f32[4,3,64,256]{3,2,1,0:T(8,128)S(1)}, u32[]{:S(2)}, u32[]{:S(2)}) collective-permute-start(f32[4,3,64,256]{3,2,1,0:T(8,128)} %refs_3_.1), channel_id=1, source_target_pairs={{0,1},{1,0},{2,3},{3,2},{4,5},{5,4},{6,7},{7,6},{8,9},{9,8},{10,11... | collective-permute-start | bytes 2359304 | tf_op jit(solution)/shard_map/ppermute | solution.py:416
  164.4 20.6 %collective-permute-start.19 = (f32[2,3,128,256]{3,2,1,0:T(8,128)}, f32[2,3,128,256]{3,2,1,0:T(8,128)S(1)}, u32[]{:S(2)}, u32[]{:S(2)}) collective-permute-start(f32[2,3,128,256]{3,2,1,0:T(8,128)} %after.41.refs_1_), channel_id=1, source_target_pairs={{0,1},{1,0},{2,3},{3,2},{4,5},{5,4},{6,7},{7,6},{8,9},{9,8},{10,11... | collective-permute-start | bytes 2359304 | tf_op jit(solution)/shard_map/ppermute | solution.py:416
  164.9 10.0 %copy-start.12 = (f32[3,256,256]{2,1,0:T(8,128)S(1)}, f32[3,256,256]{2,1,0:T(8,128)}, u32[]{:S(2)}) copy-start(f32[3,256,256]{2,1,0:T(8,128)} %get-tuple-element.45.refs_6_) | copy-start | bytes 2359300
  171.0 14.9 %collective-permute-start.25 = (f32[4,3,64,256]{3,2,1,0:T(8,128)}, f32[4,3,64,256]{3,2,1,0:T(8,128)}, u32[]{:S(2)}, u32[]{:S(2)}) collective-permute-start(f32[4,3,64,256]{3,2,1,0:T(8,128)} %after.47.refs_5_), channel_id=1, source_target_pairs={{0,1},{1,0},{2,3},{3,2},{4,5},{5,4},{6,7},{7,6},{8,9},{9,8},{10,11... | collective-permute-start | bytes 2359304 | tf_op jit(solution)/shard_map/ppermute | solution.py:416
  173.4 25.9 %collective-permute-start.27 = (f32[3,256,256]{2,1,0:T(8,128)}, f32[3,256,256]{2,1,0:T(8,128)}, u32[]{:S(2)}, u32[]{:S(2)}) collective-permute-start(f32[3,256,256]{2,1,0:T(8,128)} %add.74.refs_1_), channel_id=1, source_target_pairs={{8,16},{16,8},{9,17},{17,9},{10,18},{18,10},{11,19},{19,11},{12,20... | collective-permute-start | bytes 2359304 | tf_op jit(solution)/shard_map/ppermute | solution.py:593
  182.1 19.9 %collective-permute-start.26 = (f32[3,256,256]{2,1,0:T(8,128)}, f32[3,256,256]{2,1,0:T(8,128)S(1)}, u32[]{:S(2)}, u32[]{:S(2)}) collective-permute-start(f32[3,256,256]{2,1,0:T(8,128)} %add.75.refs_1_), channel_id=1, source_target_pairs={{8,0},{16,24},{9,1},{17,25},{10,2},{18,26},{11,3},{19,27},{12,4},{... | collective-permute-start | bytes 2359304 | tf_op jit(solution)/shard_map/ppermute | solution.py:598
  200.7 18.9 %collective-permute-start.29 = (f32[3,256,256]{2,1,0:T(8,128)S(1)}, f32[3,256,256]{2,1,0:T(8,128)S(1)}, u32[]{:S(2)}, u32[]{:S(2)}) collective-permute-start(f32[3,256,256]{2,1,0:T(8,128)S(1)} %add.76.refs_1_), channel_id=1, source_target_pairs={{8,0},{16,24},{9,1},{17,25},{10,2},{18,26},{11,3},{19,27},{12,4},{... | collective-permute-start | bytes 2359304 | tf_op jit(solution)/shard_map/ppermute | solution.py:598
  209.5 17.6 %all-to-all-start.2 = ((f32[8,3,64,128]{3,2,1,0:T(8,128)}), f32[8,3,64,128]{3,2,1,0:T(8,128)S(1)}, u32[]{:S(2)}, u32[]{:S(2)}) async-start(f32[8,3,64,128]{3,2,1,0:T(8,128)} %sweep.5.refs_1_), calls=%async_computation.2 | async-start | bytes 1572864 | tf_op jit(solution)/shard_map/all_to_all | solution.py:620
  227.1 41.1 %copy-start.8 = (f32[8,3,64,128]{3,2,1,0:T(8,128)}, f32[8,3,64,128]{3,2,1,0:T(8,128)S(1)}, u32[]{:S(2)}) copy-start(f32[8,3,64,128]{3,2,1,0:T(8,128)S(1)} %all-to-all-done.2.refs_2_) | copy-start | bytes 2359300
  227.1 16.7 %all-to-all-start.3 = ((f32[8,3,64,128]{3,2,1,0:T(8,128)}), f32[8,3,64,128]{3,2,1,0:T(8,128)S(1)}, u32[]{:S(2)}, u32[]{:S(2)}) async-start(f32[8,3,64,128]{3,2,1,0:T(8,128)} %sweep.7), calls=%async_computation.3 | async-start | bytes 1572864 | tf_op jit(solution)/shard_map/all_to_all | solution.py:620
  231.2 45.6 %copy-start.1 = (s32[3,2]{0,1:T(2,128)S(1)}, s32[3,2]{0,1:T(2,128)}, u32[]{:S(2)}) copy-start(s32[3,2]{0,1:T(2,128)} %param.12) | copy-start | bytes 76
  231.2 20.5 %collective-permute-start.28 = (f32[8,3,64,128]{3,2,1,0:T(8,128)S(1)}, f32[8,3,64,128]{3,2,1,0:T(8,128)S(1)}, u32[]{:S(2)}, u32[]{:S(2)}) collective-permute-start(f32[8,3,64,128]{3,2,1,0:T(8,128)S(1)} %all-to-all-done.2.refs_2_), channel_id=1, source_target_pairs={{0,24},{1,25},{2,26},{3,27},{4,28},{5,29},{6,30},{7,31}} | collective-permute-start | bytes 2359304 | tf_op jit(solution)/shard_map/ppermute | solution.py:621
  243.8 24.3 %copy-start.9 = (f32[8,3,64,128]{3,2,1,0:T(8,128)}, f32[8,3,64,128]{3,2,1,0:T(8,128)S(1)}, u32[]{:S(2)}) copy-start(f32[8,3,64,128]{3,2,1,0:T(8,128)S(1)} %all-to-all-done.3.refs_3_) | copy-start | bytes 2359300
  243.8 24.3 %collective-permute-start.30 = (f32[8,3,64,128]{3,2,1,0:T(8,128)S(1)}, f32[8,3,64,128]{3,2,1,0:T(8,128)S(1)}, u32[]{:S(2)}, u32[]{:S(2)}) collective-permute-start(f32[8,3,64,128]{3,2,1,0:T(8,128)S(1)} %all-to-all-done.3.refs_3_), channel_id=1, source_target_pairs={{0,24},{1,25},{2,26},{3,27},{4,28},{5,29},{6,30},{7,31}} | collective-permute-start | bytes 2359304 | tf_op jit(solution)/shard_map/ppermute | solution.py:621
  251.7 16.5 %copy-start.19 = (f32[8,3,64,128]{3,2,1,0:T(8,128)}, f32[8,3,64,128]{3,2,1,0:T(8,128)S(1)}, u32[]{:S(2)}) copy-start(f32[8,3,64,128]{3,2,1,0:T(8,128)S(1)} %collective-permute-done.28.refs_0_) | copy-start | bytes 2359300
  (18 other events, 25.8 us)
